TPU v7x, 32 devices: a whole 2x2x4 slice. The times are simulated.
32 devices in a mesh: expert: 8 (over z, y), dp: 4 (over x, core).
Axes of the slice: x: 2, y: 2, z: 4, core: 2. Of those that a mesh axis runs over, the one named last changes fastest.
Arguments:
- cotangent: bfloat16 [4, 4096, 2048], P('dp', 'expert'), may hold values from -6 to 6
- routing: int32 [4, 4096, 2], P('dp', 'expert'), may hold values from 0 to 7, all different within a row; in each aligned block of 512 rows (0 to 511, 512 to 1023, ..., all dimensions but the last counted through in order) at most 256 rows name the same one
- route_weight: float32 [4, 4096, 2], P('dp', 'expert'), may hold values from 0.1 to 0.6
- saved_preact: bfloat16 [4, 8, 2048, 1536], P('dp', 'expert'), may hold values from -6 to 6
- weight: bfloat16 [8, 768, 2048], P('expert'), may hold values from -0.21875 to 0.21875
- master: float32 [8, 768, 2048], P('expert', 'dp'), may hold values from -0.21875 to 0.21875
- moment1: float32 [8, 768, 2048], P('expert', 'dp'), may hold values from -18 to 18
- moment2: float32 [8, 768, 2048], P('expert', 'dp'), may hold values from 1 to 100
Outputs:
- grad_preact: bfloat16 [4, 8, 2048, 1536], P('dp', 'expert')
- new_weight: bfloat16 [8, 768, 2048], P('expert')
- new_master: float32 [8, 768, 2048], P('expert', 'dp')
- new_moment1: float32 [8, 768, 2048], P('expert', 'dp')
- new_moment2: float32 [8, 768, 2048], P('expert', 'dp')
Inputs may be any that keep to these rules, and one draw needn't show every extreme that they name: `routing`: each row names 2 different experts; no expert is named by more than 256 of the rows of one device, and in every draw some expert is named by exactly 256 rows of some device.
All inputs are finite; a program needn't handle non-finite values.
Results may differ from a plain program's by a relative error of at most 0.019.
Values may be sent and summed in bfloat16 or wider, within the bound.
No kernel may reach another device: no remote copies, remote signals or barrier semaphores. Data moves between devices by JAX's collectives and lax.ppermute only.
A program may use at most 128 MiB of HBM per device.

v0:
```python
import jax
import jax.numpy as jnp
from jax import lax
from jax.sharding import PartitionSpec as P

beta_first = 0.9
beta_second = 0.95
bias_first = 1.0 - 0.9**10
bias_second = 1.0 - 0.95**10
adam_epsilon = 1e-08
learn_rate = 0.001
decay_rate = 0.1


def body(cotangent, routing, route_weight, saved_preact, weight, master, moment1, moment2):
    n_expert = lax.axis_size("expert")
    tokens = cotangent[0]
    width = tokens.shape[1]
    slots = saved_preact.shape[2]
    hidden_width = weight.shape[1]
    capacity = slots // n_expert
    route_count = routing.shape[2]
    chosen = routing[0].reshape(-1)
    onehot = (chosen[:, None] == jnp.arange(n_expert, dtype=jnp.int32)[None, :]).astype(jnp.int32)
    earlier = jnp.cumsum(onehot, axis=0) - onehot
    position = jnp.sum(earlier * onehot, axis=1)
    target = chosen * capacity + position
    source_token = jnp.arange(chosen.shape[0], dtype=jnp.int32) // route_count
    token_table = jnp.zeros((slots,), jnp.int32).at[target].set(source_token)
    weight_table = jnp.zeros((slots,), jnp.float32).at[target].set(route_weight[0].reshape(-1))
    scaled = (tokens[token_table].astype(jnp.float32) * weight_table[:, None]).astype(jnp.bfloat16)
    arrived = lax.all_to_all(
        scaled.reshape(n_expert, capacity, width), "expert", split_axis=0, concat_axis=0, tiled=True
    )
    arrived = arrived.reshape(slots, width)
    preact = saved_preact[0, 0].astype(jnp.float32)
    gate_value = preact[:, :hidden_width]
    up_value = preact[:, hidden_width:]
    sigmoid_gate = jax.nn.sigmoid(gate_value)
    activated = gate_value * sigmoid_gate
    hidden = (activated * up_value).astype(jnp.bfloat16)
    back = lax.dot_general(
        arrived, weight[0], (((1,), (1,)), ((), ())), preferred_element_type=jnp.float32
    )
    grad_gate = back * up_value * sigmoid_gate * (1.0 + gate_value * (1.0 - sigmoid_gate))
    grad_up = back * activated
    grad_preact = jnp.concatenate([grad_gate, grad_up], axis=1).astype(jnp.bfloat16)[None, None]
    gradient = lax.psum_scatter(
        lax.dot_general(
            hidden, arrived, (((0,), (0,)), ((), ())), preferred_element_type=jnp.float32
        ).astype(jnp.bfloat16),
        "dp",
        scatter_dimension=0,
        tiled=True,
    ).astype(jnp.float32)
    moment_one = beta_first * moment1[0] + (1.0 - beta_first) * gradient
    moment_two = beta_second * moment2[0] + (1.0 - beta_second) * gradient * gradient
    step_size = (
        moment_one / bias_first / (jnp.sqrt(moment_two / bias_second) + adam_epsilon)
        + decay_rate * master[0]
    )
    master_next = master[0] - learn_rate * step_size
    weight_next = lax.all_gather(master_next.astype(jnp.bfloat16), "dp", axis=0, tiled=True)
    return (grad_preact, weight_next[None], master_next[None], moment_one[None], moment_two[None])


def solution(mesh):
    placed = (
        P("dp", "expert", None),
        P("dp", "expert", None),
        P("dp", "expert", None),
        P("dp", "expert", None, None),
        P("expert", None, None),
        P("expert", "dp", None),
        P("expert", "dp", None),
        P("expert", "dp", None),
    )
    return jax.shard_map(
        body,
        mesh=mesh,
        in_specs=placed,
        out_specs=(
            P("dp", "expert", None, None),
            P("expert", None, None),
            P("expert", "dp", None),
            P("expert", "dp", None),
            P("expert", "dp", None),
        ),
        check_vma=False,
    )
```

profile of v0, /device:TPU:0, one launch (start us, length us, event | category | flops | bytes accessed | tf_op | source)
XLA Modules:
  0.0 335.3 jit_solution(5394975862379355985)
XLA Ops:
  7.2 0.8 broadcast_multiply_fusion
  8.0 0.9 copy.16
  9.0 0.2 eq.29
  9.5 0.2 mul.92
  9.7 2.3 reduce-window.6
  11.9 0.3 slice_reduce_fusion
  12.5 4.3 %scatter_custom_fusion = s32[2048]{0:T(1024)S(1)} fusion(s32[1024]{0:T(1024)S(1)} %bitcast.77, s32[1024]{0:T(1024)S(1)} %add_select_fusion, s32[]{:T(128)} %constant.16.clone.1), kind=kCustom, calls=%fused_computation.47 | custom fusion | bytes 8196 | tf_op jit(solution)/shard_map/scatter | solution.py:29
  16.8 0.8 copy.18
  17.8 4.3 %scatter_custom_fusion.1 = f32[2048]{0:T(1024)S(1)} fusion(s32[1024]{0:T(1024)S(1)} %bitcast.78, f32[1024]{0:T(1024)S(1)} %reshape.129, f32[]{:T(128)} %constant.41.clone.1), kind=kCustom, calls=%fused_computation.45 | custom fusion | bytes 8196 | tf_op jit(solution)/shard_map/scatter | solution.py:30
  22.2 18.2 %gather_fusion = bf16[2048,2048]{1,0:T(8,128)(2,1)} fusion(bf16[512,2048]{1,0:T(8,128)(2,1)} %bitcast.71, s32[2048]{0:T(1024)S(1)} %fusion.17), kind=kCustom, calls=%fused_computation | custom fusion | bytes 16785408 | tf_op jit(solution)/shard_map/gather | solution.py:31
  40.4 8.1 %fusion = bf16[8,256,2048]{2,1,0:T(8,128)(2,1)} fusion(bf16[8,256,2048]{2,1,0:T(8,128)(2,1)} %bitcast.72, f32[8,256]{1,0:T(8,128)S(1)} %mul.94), kind=kLoop, calls=%fused_computation.4 | loop fusion | flops 12582912 | bytes 16785408 | tf_op jit(solution)/shard_map/convert_element_type | solution.py:31
  48.5 7.3 %all-to-all-start = ((bf16[8,256,2048]{2,1,0:T(8,128)(2,1)}), bf16[8,256,2048]{2,1,0:T(8,128)(2,1)}, u32[]{:S(2)}, u32[]{:S(2)}) async-start(bf16[8,256,2048]{2,1,0:T(8,128)(2,1)} %fusion), calls=%async_computation | async-start | bytes 16777216 | tf_op jit(solution)/shard_map/all_to_all | solution.py:32
  55.8 8.6 %copy.19 = bf16[1,1,2048,1536]{2,3,1,0:T(8,128)(2,1)} copy(bf16[1,1,2048,1536]{3,2,1,0:T(8,128)(2,1)} %param.11) | data formatting | bytes 12582912 | tf_op args[3]
  64.4 8.9 %bitcast_convert_fusion = f32[2048,1536]{0,1:T(8,128)} fusion(bf16[1,1,2048,1536]{2,3,1,0:T(8,128)(2,1)} %copy.19), kind=kLoop, calls=%fused_computation.6 | loop fusion | flops 3145728 | bytes 18874368 | tf_op jit(solution)/shard_map/convert_element_type | solution.py:36
  73.3 165.6 %all-to-all-done = bf16[8,256,2048]{2,1,0:T(8,128)(2,1)} async-done(((bf16[8,256,2048]{2,1,0:T(8,128)(2,1)}), bf16[8,256,2048]{2,1,0:T(8,128)(2,1)}, u32[]{:S(2)}, u32[]{:S(2)}) %all-to-all-start) | async-done | bytes 8388640 | tf_op jit(solution)/shard_map/all_to_all | solution.py:32
  238.9 13.4 %convolution_convert_fusion = bf16[768,2048]{1,0:T(8,128)(2,1)} fusion(bf16[2048,2048]{1,0:T(8,128)(2,1)} %bitcast.5, f32[2048,1536]{0,1:T(8,128)} %bitcast_convert_fusion), kind=kOutput, calls=%fused_computation.12 | convolution fusion | flops 6453460992 | bytes 24117248 | tf_op jit(solution)/shard_map/dot_general | solution.py:49
  252.3 0.2 all-gather.2.cloned.1.call-start
  252.5 36.9 %reduce-scatter.2.cloned.1.call-done = bf16[192,2048]{1,0:T(8,128)(2,1)} async-done(((bf16[768,2048]{1,0:T(8,128)(2,1)}), bf16[192,2048]{1,0:T(8,128)(2,1)}) %reduce-scatter.2.cloned.1.call-update) | async-done | bytes 786448 | tf_op jit(solution)/shard_map/reduce_scatter | solution.py:48
  289.4 6.3 %fusion.26 = (bf16[192,2048]{1,0:T(8,128)(2,1)}, f32[192,2048]{1,0:T(8,128)}, f32[1,192,2048]{2,1,0:T(8,128)}, f32[1,192,2048]{2,1,0:T(8,128)}) fusion(f32[1,192,2048]{2,1,0:T(8,128)} %param.15, bf16[192,2048]{1,0:T(8,128)(2,1)} %reduce-scatter.2.cloned.1.call-done, f32[1,192,2048]{2,1,0:T(8,128)} %param.14, f32[1,192,2048]{2,1,0:T(8,128)} %param.13), kind=kLoop, calls=%fused_computation.52 | loop fusion | flops 6684672 | bytes 11010048 | tf_op jit(solution)/shard_map/convert_element_type | solution.py:63
  295.8 13.7 %fusion.5 = (bf16[1,1,2048,768]{2,3,1,0:T(8,128)(2,1)S(1)}, bf16[1,1,2048,768]{2,3,1,0:T(8,128)(2,1)S(1)}) fusion(f32[2048,1536]{0,1:T(8,128)} %bitcast_convert_fusion, bf16[2048,2048]{1,0:T(8,128)(2,1)} %bitcast.5, bf16[1,768,2048]{2,1,0:T(8,128)(2,1)S(1)} %copy-done), kind=kOutput, calls=%fused_computation.16 | convolution fusion | flops 6462898176 | bytes 30408704 | tf_op jit(solution)/shard_map/dot_general | solution.py:42
  309.5 3.8 %pad_maximum_fusion = bf16[1,1,2048,1536]{2,3,1,0:T(8,128)(2,1)} fusion(bf16[1,1,2048,768]{2,3,1,0:T(8,128)(2,1)S(1)} %get-tuple-element.18, bf16[1,1,2048,768]{2,3,1,0:T(8,128)(2,1)S(1)} %get-tuple-element.17), kind=kLoop, calls=%fused_computation.5 | loop fusion | flops 12582912 | bytes 12582912 | tf_op jit(solution)/shard_map/concatenate | solution.py:47
  313.3 8.6 %copy.20 = bf16[1,1,2048,1536]{3,2,1,0:T(8,128)(2,1)} copy(bf16[1,1,2048,1536]{2,3,1,0:T(8,128)(2,1)} %pad_maximum_fusion) | data formatting | bytes 12582912
  321.9 2.6 all-gather.2.cloned.1.call-done
  324.5 4.0 %copy.24 = bf16[1,768,2048]{2,1,0:T(8,128)(2,1)} copy(bf16[1,768,2048]{2,1,0:T(8,128)(2,1)} %bitcast.73) | data formatting | bytes 6291456
  (16 shorter events, 0.9 us)
Async XLA Ops:
  7.2 288.6 %copy-start = (bf16[1,768,2048]{2,1,0:T(8,128)(2,1)S(1)}, bf16[1,768,2048]{2,1,0:T(8,128)(2,1)}, u32[]{:S(2)}) copy-start(bf16[1,768,2048]{2,1,0:T(8,128)(2,1)} %param.12) | copy-start | bytes 9437188
  48.5 190.4 %all-to-all-start = ((bf16[8,256,2048]{2,1,0:T(8,128)(2,1)}), bf16[8,256,2048]{2,1,0:T(8,128)(2,1)}, u32[]{:S(2)}, u32[]{:S(2)}) async-start(bf16[8,256,2048]{2,1,0:T(8,128)(2,1)} %fusion), calls=%async_computation | async-start | bytes 16777216 | tf_op jit(solution)/shard_map/all_to_all | solution.py:32
  55.7 233.7 %reduce-scatter.2.cloned.1.call-start = ((), (), s32[]{:S(2)}) async-start(), calls=%async_computation.2 | async-start | bytes 3932160 | tf_op jit(solution)/shard_map/reduce_scatter | solution.py:48
  252.3 72.2 %all-gather.2.cloned.1.call-start = ((), (), s32[]{:S(2)}) async-start(), calls=%async_computation.3 | async-start | bytes 3932160 | tf_op jit(solution)/shard_map/all_gather | solution.py:63
Sparse Core Ops, SparseCore 0:
  252.4 36.9 reduce-scatter.1
  295.9 28.5 all-gather.1
where the time goes:
time: 336 us; the launch traced here: 335 us
  waiting for transfers between devices  205 us (61%)
  local copies, waits for them, and re-layouts  50.9 us (15%)
  other arithmetic  30.4 us (9%)
  matrix products  27 us (8%)
  between operations  14.2 us (4%)
  starting transfers between devices  7.54 us (2%)
    all_to_all x1, waiting for transfers between devices, body(): lax.all_to_all(scaled.reshape(n_expert, capacity, width), 'expert', split...  166 us
    reduce_scatter x1, waiting for transfers between devices, body(): lax.psum_scatter(lax.dot_general(hidden, arrived, (((0,), (0,)), ((), ())...  36.9 us
    unnamed x7, local copies, waits for them, and re-layouts  23 us
    gather x1, local copies, waits for them, and re-layouts, body(): tokens[token_table].astype(jnp.float32) * weight_table[:, None]  18.2 us
    dot_general x1, matrix products, body(): lax.dot_general(arrived, weight[0], (((1,), (1,)), ((), ())), preferred_e...  13.7 us
    dot_general x1, matrix products, body(): lax.dot_general(hidden, arrived, (((0,), (0,)), ((), ())), preferred_elem...  13.4 us
    convert_element_type x1, other arithmetic, body(): preact = saved_preact[0, 0].astype(jnp.float32)  8.87 us
    convert_element_type x1, other arithmetic, body(): (tokens[token_table].astype(jnp.float32) * weight_table[:, None]).astype(...  8.08 us
  transfers between devices with their start and end apart: 3, of which 3 were waited for; matrix products, arithmetic and copies ran while one was open for 13% of the time, Pallas kernels for 0%

commit v1 on v0

--- a/solution.py
+++ b/solution.py
@@ -1,6 +1,10 @@
+import functools
+
 import jax
 import jax.numpy as jnp
 from jax import lax
+from jax.experimental import pallas as pl
+from jax.experimental.pallas import tpu as pltpu
 from jax.sharding import PartitionSpec as P
 
 beta_first = 0.9
@@ -10,6 +14,331 @@
 adam_epsilon = 1e-08
 learn_rate = 0.001
 decay_rate = 0.1
+
+VMEM_LIMIT = 40 * 1024 * 1024
+ANY = pl.BlockSpec(memory_space=pl.ANY)
+
+
+def params():
+    return pltpu.CompilerParams(vmem_limit_bytes=VMEM_LIMIT)
+
+
+def call(kernel, name, grid, scalars, ins, specs, outs, out_specs, scratch=(), aliases=None, flops=0, moved=0):
+    shift = len(scalars)
+    return pl.pallas_call(
+        kernel,
+        name=name,
+        grid_spec=pltpu.PrefetchScalarGridSpec(
+            num_scalar_prefetch=shift,
+            grid=grid,
+            in_specs=specs,
+            out_specs=out_specs,
+            scratch_shapes=list(scratch),
+        ),
+        out_shape=outs,
+        input_output_aliases={shift + a: b for a, b in (aliases or {}).items()},
+        compiler_params=params(),
+        cost_estimate=pl.CostEstimate(flops=flops, bytes_accessed=moved, transcendentals=0),
+    )(*scalars, *ins)
+
+
+def shape(dims, dtype):
+    return jax.ShapeDtypeStruct(dims, dtype)
+
+
+def hidden_kernel(order, groups, preact, out, turned):
+    width = preact.shape[-1] // 2
+    gate = preact[0, 0, :, :width].astype(jnp.float32)
+    up = preact[0, 0, :, width:].astype(jnp.float32)
+    value = gate * jax.nn.sigmoid(gate) * up
+    turned[...] = value.T.astype(jnp.bfloat16)
+    rows = width // 4
+    for g in range(4):
+        start = pl.multiple_of(groups[g] * rows, 16)
+        out[g * rows : (g + 1) * rows, :] = turned[pl.ds(start, rows), :]
+
+
+def table_kernel(sources, experts, info, picks, scales):
+    capacity = picks.shape[1] // 2
+    tokens = info.shape[2]
+    first, second = info[0, 0:1, :], info[0, 1:2, :]
+    weight_one, weight_two = info[0, 2:3, :], info[0, 3:4, :]
+    before = lax.broadcasted_iota(jnp.int32, (tokens, tokens), 0)
+    after = lax.broadcasted_iota(jnp.int32, (tokens, tokens), 1)
+    earlier = (before < after).astype(jnp.float32).astype(jnp.bfloat16)
+    for k in range(2):
+        expert = experts[k].astype(jnp.float32)
+        is_first = first == expert
+        named = jnp.logical_or(is_first, second == expert)
+        flag = jnp.where(named, 1.0, 0.0)
+        position = jnp.dot(
+            jnp.broadcast_to(flag, (16, tokens)).astype(jnp.bfloat16), earlier, preferred_element_type=jnp.float32
+        )[0:1, :]
+        place = jnp.where(named, position, -1.0).astype(jnp.int32)
+        slot = lax.broadcasted_iota(jnp.int32, (capacity, tokens), 0)
+        hit = slot == place
+        value = jnp.where(is_first, weight_one, weight_two)
+        picks[0, k * capacity : (k + 1) * capacity, :] = jnp.where(hit, 1.0, 0.0).astype(jnp.bfloat16)
+        scales[0, k * capacity : (k + 1) * capacity, :] = jnp.sum(jnp.where(hit, value, 0.0), axis=1, keepdims=True)
+
+
+def pick_kernel(middle, picks, scales, near, far, mine, other):
+    capacity = mine.shape[0]
+    rows = near[...] if far is None else jnp.where(middle[0] == 1, near[...], far[...])
+    value = jnp.dot(picks[0], rows, preferred_element_type=jnp.float32) * scales[0]
+    mine[...] = value[:capacity].astype(jnp.bfloat16)
+    other[...] = value[capacity:].astype(jnp.bfloat16)
+
+
+def pick_one(middle, picks, scales, near, mine, other):
+    pick_kernel(middle, picks, scales, near, None, mine, other)
+
+
+def product_kernel(*refs):
+    turned, pieces, (send, keep) = refs[0], refs[1:-2], refs[-2:]
+    half = send.shape[0]
+    rows = jnp.concatenate([p[...] for p in pieces], axis=0)
+    send[...] = jnp.dot(turned[:half, :], rows, preferred_element_type=jnp.float32).astype(jnp.bfloat16)
+    keep[...] = jnp.dot(turned[half:, :], rows, preferred_element_type=jnp.float32).astype(jnp.bfloat16)
+
+
+def back_kernel(count, order, *refs):
+    mine, got = refs[:count], refs[count : 2 * count]
+    weight, preact, out = refs[2 * count], refs[2 * count + 1], refs[-1]
+    width = weight.shape[1]
+    one = jnp.concatenate([p[...] for p in mine], axis=1)
+    two = jnp.concatenate([p[...] for p in got], axis=1)
+    rows = jnp.where(pl.program_id(0) == 0, one, two)
+    back = lax.dot_general(rows, weight[0], (((1,), (1,)), ((), ())), preferred_element_type=jnp.float32)
+    gate = preact[0, 0, :, :width].astype(jnp.float32)
+    up = preact[0, 0, :, width:].astype(jnp.float32)
+    sig = jax.nn.sigmoid(gate)
+    out[0, 0, :, :width] = (back * up * sig * (1.0 + gate * (1.0 - sig))).astype(jnp.bfloat16)
+    out[0, 0, :, width:] = (back * (gate * sig)).astype(jnp.bfloat16)
+
+
+def adam_kernel(kept, near, far, master, moment1, moment2, *refs):
+    out_master, out_one, out_two, out_weight = refs[-4:]
+    gradient = (kept[...].astype(jnp.float32) + near[...].astype(jnp.float32)) + far[...].astype(jnp.float32)
+    moment_one = beta_first * moment1[0] + (1.0 - beta_first) * gradient
+    moment_two = beta_second * moment2[0] + (1.0 - beta_second) * gradient * gradient
+    step_size = (
+        moment_one / bias_first / (jnp.sqrt(moment_two / bias_second) + adam_epsilon) + decay_rate * master[0]
+    )
+    master_next = master[0] - learn_rate * step_size
+    out_master[0] = master_next
+    out_one[0] = moment_one
+    out_two[0] = moment_two
+    out_weight[...] = master_next.astype(jnp.bfloat16)
+
+
+def assemble_kernel(places, own, across, sibling, *refs):
+    out = refs[-1]
+    rows = own.shape[0]
+
+    def put(g, value):
+        out[0, pl.ds(pl.multiple_of(places[g] * rows, 16), rows), :] = value
+
+    put(3, own[...])
+    put(2, across[...])
+    put(1, sibling[:rows, :])
+    put(0, sibling[rows:, :])
+
+
+def line_body(cotangent, routing, route_weight, saved_preact, weight, master, moment1, moment2):
+    tokens, width = cotangent.shape[1:]
+    slots, hidden_width = saved_preact.shape[2], weight.shape[1]
+    capacity = slots // 8
+    rows = hidden_width // 4
+    expert = lax.axis_index("expert")
+    replica = lax.axis_index("dp")
+    z, y = expert // 2, expert % 2
+    x, core = replica // 2, replica % 2
+    middle = jnp.where((z == 1) | (z == 2), 1, 0).astype(jnp.int32).reshape(1)
+    lower = z < 2
+    blocks = [z, z ^ 1, jnp.where(lower, 2, 1), jnp.where(lower, 3, 0)]
+    sources = jnp.stack([b * 2 + y for b in blocks]).astype(jnp.int32)
+    order = jnp.stack([b * 2 + s for b in blocks for s in (y, 1 - y)]).astype(jnp.int32)
+    experts = jnp.stack([expert, expert ^ 1]).astype(jnp.int32)
+    groups = jnp.stack([(1 - x) * 2 + 1 - core, x * 2 + 1 - core, (1 - x) * 2 + core, x * 2 + core]).astype(jnp.int32)
+
+    swap_pair = [(e, e ^ 2) for e in range(8)]
+    swap_middle = [(2, 4), (4, 2), (3, 5), (5, 3)]
+    to_end = [(4, 6), (5, 7), (2, 0), (3, 1)]
+    swap_y = [(e, e ^ 1) for e in range(8)]
+    swap_x = [(d, d ^ 2) for d in range(4)]
+    swap_core = [(d, d ^ 1) for d in range(4)]
+
+    own = cotangent[0]
+    info = jnp.concatenate([routing[0].T.astype(jnp.float32), route_weight[0].T], axis=0)
+    info = lax.all_gather(info, "expert")
+    pair = lax.ppermute(own, "expert", swap_pair)
+    middle_one = lax.ppermute(own, "expert", swap_middle)
+
+    turned = call(
+        hidden_kernel,
+        "hidden",
+        (8,),
+        (order, groups),
+        (saved_preact,),
+        [pl.BlockSpec((1, 1, capacity, 2 * hidden_width), lambda i, o, g: (0, 0, o[i], 0))],
+        shape((hidden_width, slots), jnp.bfloat16),
+        pl.BlockSpec((hidden_width, capacity), lambda i, o, g: (0, i)),
+        scratch=[pltpu.VMEM((hidden_width, capacity), jnp.bfloat16)],
+        moved=9 * slots * hidden_width,
+        flops=40 * slots * hidden_width,
+    )
+    picks, scales = call(
+        table_kernel,
+        "tables",
+        (4,),
+        (sources, experts),
+        (info,),
+        [pl.BlockSpec((1, 4, tokens), lambda i, s, e: (s[i], 0, 0))],
+        (shape((4, 2 * capacity, tokens), jnp.bfloat16), shape((4, 2 * capacity, 1), jnp.float32)),
+        (
+            pl.BlockSpec((1, 2 * capacity, tokens), lambda i, s, e: (i, 0, 0)),
+            pl.BlockSpec((1, 2 * capacity, 1), lambda i, s, e: (i, 0, 0)),
+        ),
+        moved=20 * capacity * tokens,
+        flops=40 * capacity * tokens,
+    )
+
+    def pick(block, near, far=None, offset=0, columns=None):
+        columns = width if columns is None else columns
+        tile = min(512, columns)
+        start = offset // tile
+        specs = [
+            pl.BlockSpec((1, 2 * capacity, tokens), lambda i, m: (block, 0, 0)),
+            pl.BlockSpec((1, 2 * capacity, 1), lambda i, m: (block, 0, 0)),
+        ]
+        if far is None:
+            specs += [pl.BlockSpec((tokens, tile), lambda i, m: (0, start + i))]
+            ins = (picks, scales, near)
+        else:
+            specs += [
+                pl.BlockSpec((tokens, tile), lambda i, m: (0, start + i * m[0])),
+                pl.BlockSpec((tokens, tile), lambda i, m: (0, i * (1 - m[0]))),
+            ]
+            ins = (picks, scales, near, far)
+        out = shape((capacity, columns), jnp.bfloat16)
+        mine, other = call(
+            pick_one if far is None else pick_kernel,
+            "pick",
+            (columns // tile,),
+            (middle,),
+            ins,
+            specs,
+            (out, out),
+            (pl.BlockSpec((capacity, tile), lambda i, m: (0, i)),) * 2,
+            flops=4 * capacity * tokens * columns,
+            moved=4 * (tokens + capacity) * columns,
+        )
+        return mine, lax.ppermute(other, "expert", swap_y)
+
+    def back(block, mine, got, previous):
+        specs = [pl.BlockSpec(p.shape, lambda i, o: (0, 0)) for p in (*mine, *got)]
+        specs += [
+            pl.BlockSpec((1, hidden_width, width), lambda i, o: (0, 0, 0)),
+            pl.BlockSpec((1, 1, capacity, 2 * hidden_width), lambda i, o: (0, 0, o[2 * block + i], 0)),
+        ]
+        ins = [*mine, *got, weight, saved_preact]
+        aliases = {}
+        if previous is not None:
+            aliases = {len(ins): 0}
+            ins.append(previous)
+            specs.append(ANY)
+        return call(
+            functools.partial(back_kernel, len(mine)),
+            "back",
+            (2,),
+            (order,),
+            ins,
+            specs,
+            shape(saved_preact.shape, jnp.bfloat16),
+            pl.BlockSpec((1, 1, capacity, 2 * hidden_width), lambda i, o: (0, 0, o[2 * block + i], 0)),
+            aliases=aliases,
+            flops=4 * capacity * hidden_width * width,
+            moved=2 * (hidden_width * width + 6 * capacity * hidden_width + 2 * capacity * width),
+        )
+
+    mine0, got0 = pick(0, own)
+    mine1, got1 = pick(1, pair)
+    middle_two = lax.ppermute(pair, "expert", swap_middle)
+    end_one = lax.ppermute(middle_one, "expert", to_end)
+    grad_preact = back(0, [mine0], [got0], None)
+    grad_preact = back(1, [mine1], [got1], grad_preact)
+    mine2, got2 = pick(2, middle_one, end_one)
+    grad_preact = back(2, [mine2], [got2], grad_preact)
+
+    chunks = [(0, 512), (512, 512), (1024, 512), (1536, 256), (1792, 256)]
+    ends = [lax.ppermute(middle_two[:, o : o + n], "expert", to_end) for o, n in chunks]
+    states = None
+    next_weight = None
+    mines, gots = [], []
+    for (offset, columns), end_two in zip(chunks, ends):
+        mine3, got3 = pick(3, middle_two, end_two, offset, columns)
+        mines.append(mine3)
+        gots.append(got3)
+        column = offset // columns
+        full = pl.BlockSpec((capacity, columns), lambda i, c=column: (0, c))
+        part = pl.BlockSpec((capacity, columns), lambda i: (0, 0))
+        half = shape((2 * rows, columns), jnp.bfloat16)
+        send, keep = call(
+            product_kernel,
+            "product",
+            (1,),
+            (),
+            (turned, mine0, got0, mine1, got1, mine2, got2, mine3, got3),
+            [pl.BlockSpec((hidden_width, slots), lambda i: (0, 0))] + [full] * 6 + [part] * 2,
+            (half, half),
+            (pl.BlockSpec((2 * rows, columns), lambda i: (0, 0)),) * 2,
+            flops=2 * hidden_width * slots * columns,
+            moved=2 * (hidden_width * slots + slots * columns + hidden_width * columns),
+        )
+        near = lax.ppermute(send, "dp", swap_core)
+        across = (keep[:rows].astype(jnp.float32) + near[:rows].astype(jnp.float32)).astype(jnp.bfloat16)
+        far = lax.ppermute(across, "dp", swap_x)
+        state = pl.BlockSpec((1, rows, columns), lambda i, c=column: (0, 0, c))
+        second = pl.BlockSpec((rows, columns), lambda i: (1, 0))
+        whole = pl.BlockSpec((rows, columns), lambda i: (0, 0))
+        out_state = shape(master.shape, jnp.float32)
+        previous = () if states is None else states
+        *states, fresh = call(
+            adam_kernel,
+            "adam",
+            (1,),
+            (),
+            (keep, near, far, master, moment1, moment2, *previous),
+            [second, second, whole, state, state, state] + [ANY] * len(previous),
+            (out_state, out_state, out_state, shape((rows, columns), jnp.bfloat16)),
+            (state, state, state, whole),
+            aliases={6 + k: k for k in range(len(previous))},
+            flops=20 * rows * columns,
+            moved=32 * rows * columns,
+        )
+        crossed = lax.ppermute(fresh, "dp", swap_x)
+        sibling = lax.ppermute(jnp.concatenate([fresh, crossed], axis=0), "dp", swap_core)
+        last = () if next_weight is None else (next_weight,)
+        next_weight = call(
+            assemble_kernel,
+            "assemble",
+            (1,),
+            (groups,),
+            (fresh, crossed, sibling, *last),
+            [
+                pl.BlockSpec((rows, columns), lambda i, g: (0, 0)),
+                pl.BlockSpec((rows, columns), lambda i, g: (0, 0)),
+                pl.BlockSpec((2 * rows, columns), lambda i, g: (0, 0)),
+            ]
+            + [ANY] * len(last),
+            shape((1, hidden_width, width), jnp.bfloat16),
+            pl.BlockSpec((1, hidden_width, columns), lambda i, g, c=column: (0, 0, c)),
+            aliases={3: 0} if last else None,
+            moved=16 * rows * columns,
+        )
+    grad_preact = back(3, mines, gots, grad_preact)
+    return (grad_preact, next_weight, *states)
 
 
 def body(cotangent, routing, route_weight, saved_preact, weight, master, moment1, moment2):
@@ -75,8 +404,9 @@
         P("expert", "dp", None),
         P("expert", "dp", None),
     )
+    line = mesh.shape["expert"] == 8 and mesh.shape["dp"] == 4
     return jax.shard_map(
-        body,
+        line_body if line else body,
         mesh=mesh,
         in_specs=placed,
         out_specs=(

time: 336 us -> 287 us (0.85)
  waiting for transfers between devices: 205 us -> 91.7 us
  Pallas kernels: 0 us -> 72.6 us
  blocking collectives: 0 us -> 71 us
  local copies, waits for them, and re-layouts: 50.9 us -> 12.3 us
  other arithmetic: 30.4 us -> 1.93 us
  starting transfers between devices: 7.54 us -> 35.3 us
  matrix products: 27 us -> 0 us
  between operations: 14.2 us -> 1.27 us
    all_to_all x1 -> x0, waiting for transfers between devices: 166 us -> none  [body(): lax.all_to_all(scaled.reshape(n_expert, capacity, width), 'expert', split...]
    ppermute x0 -> x37, waiting for transfers between devices: none -> 91.7 us  [the longest x1 43.9 us: line_body(): pair = lax.ppermute(own, 'expert', swap_pair)]
    pallas_call x0 -> x29, Pallas kernels: none -> 72.6 us  [call(): pl.pallas_call(kernel, name=name, grid_spec=pltpu.PrefetchScalarGridSpec(...]
    all_gather x0 -> x1, blocking collectives: none -> 71 us  [line_body(): info = lax.all_gather(info, 'expert')]
    reduce_scatter x1 -> x0, waiting for transfers between devices: 36.9 us -> none  [body(): lax.psum_scatter(lax.dot_general(hidden, arrived, (((0,), (0,)), ((), ())...]
    ppermute x0 -> x37, starting transfers between devices: none -> 35.3 us  [the longest x8 6.6 us: pick(): return (mine, lax.ppermute(other, 'expert', swap_y))]
    dot_general x2 -> x0, matrix products: 27 us -> none  [the longest x1 13.7 us: body(): lax.dot_general(arrived, weight[0], (((1,), (1,)), ((), ())), preferred_e...]
    convert_element_type x4 -> x6, other arithmetic: 23.3 us -> 0.9 us  [the longest x1 0.69 us: line_body(): routing[0].T.astype(jnp.float32)]
  transfers between devices with their start and end apart: 3 -> 37, of which waited for: 3 -> 9; matrix products, arithmetic and copies ran while one was open for 13% -> 2% of each run, Pallas kernels for 0% -> 25%
where the time goes in v1:
time: 287 us; the launch traced here: 286 us
  waiting for transfers between devices  91.7 us (32%)
  Pallas kernels  72.6 us (25%)
  blocking collectives  71 us (25%)
  starting transfers between devices  35.3 us (12%)
  local copies, waits for them, and re-layouts  12.3 us (4%)
    pallas_call x29, Pallas kernels, call(): pl.pallas_call(kernel, name=name, grid_spec=pltpu.PrefetchScalarGridSpec(...  72.6 us
    all_gather x1, blocking collectives, line_body(): info = lax.all_gather(info, 'expert')  71 us
    ppermute x1, waiting for transfers between devices, line_body(): pair = lax.ppermute(own, 'expert', swap_pair)  43.9 us
    ppermute x5, waiting for transfers between devices, line_body(): lax.ppermute(middle_two[:, o:o + n], 'expert', to_end)  17.3 us
    ppermute x8, waiting for transfers between devices, pick(): return (mine, lax.ppermute(other, 'expert', swap_y))  16.1 us
    unnamed x72, local copies, waits for them, and re-layouts  7.96 us
    ppermute x5, waiting for transfers between devices, line_body(): far = lax.ppermute(across, 'dp', swap_x)  7.67 us
    ppermute x5, waiting for transfers between devices, line_body(): crossed = lax.ppermute(fresh, 'dp', swap_x)  6.74 us
  transfers between devices with their start and end apart: 37, of which 9 were waited for; matrix products, arithmetic and copies ran while one was open for 2% of the time, Pallas kernels for 25%

profile of v1, /device:TPU:0, one launch (start us, length us, event | category | flops | bytes accessed | tf_op | source)
XLA Modules:
  0.0 286.1 jit_solution(15242084761528663318)
XLA Ops:
  0.6 3.1 %collective-permute-start = (bf16[512,2048]{1,0:T(8,128)(2,1)}, bf16[512,2048]{1,0:T(8,128)(2,1)}, u32[]{:S(2)}, u32[]{:S(2)}) collective-permute-start(bf16[512,2048]{1,0:T(8,128)(2,1)} %bitcast.27), channel_id=1, source_target_pairs={{0,8},{4,12},{8,0},{12,4},{16,24},{20,28},{24,16},{28,20},{1,9},{5... | collective-permute-start | bytes 6291464 | tf_op jit(solution)/shard_map/ppermute | solution.py:175
  5.7 43.9 %collective-permute-done.near = bf16[512,2048]{1,0:T(8,128)(2,1)} collective-permute-done((bf16[512,2048]{1,0:T(8,128)(2,1)}, bf16[512,2048]{1,0:T(8,128)(2,1)}, u32[]{:S(2)}, u32[]{:S(2)}) %collective-permute-start) | collective-permute-done | bytes 2097184 | tf_op jit(solution)/shard_map/ppermute | solution.py:175
  54.4 71.0 %all-gather.1.info = f32[8,4,512]{2,1,0:T(4,128)S(1)} all-gather(f32[1,4,512]{2,1,0:T(4,128)S(1)} %maximum_bitcast_fusion), channel_id=2, replica_groups=mesh['expert'=8,'dp'=4] {'expert'}, dimensions={0}, use_global_device_ids=true | all-gather | bytes 73728 | tf_op jit(solution)/shard_map/all_gather | solution.py:174
  132.6 4.4 %pick.14 = (bf16[256,2048]{1,0:T(8,128)(2,1)S(1)}, bf16[256,2048]{1,0:T(8,128)(2,1)}) custom-call(s32[1]{0:T(128)} %bitcast.8.middle, bf16[4,512,512]{2,1,0:T(8,128)(2,1)S(1)} %get-tuple-element.53.picks, f32[4,512,1]{2,1,0:T(8,128)S(1)} %get-tuple-element.54.scales, bf16[512,2048]{1,0:T(8,128)(2,1)} %collective-permute-done.near), custom_call_target="tpu_custom_call" | custom-call | flops 1073741824 | bytes 6291456 | tf_op jit(solution)/shard_map/pick/pallas_call | solution.py:28
  139.1 2.4 fusion.1
  142.8 4.6 %pick.13 = (bf16[256,2048]{1,0:T(8,128)(2,1)S(1)}, bf16[256,2048]{1,0:T(8,128)(2,1)}) custom-call(s32[1]{0:T(128)} %bitcast.8.middle, bf16[4,512,512]{2,1,0:T(8,128)(2,1)S(1)} %get-tuple-element.53.picks, f32[4,512,1]{2,1,0:T(8,128)S(1)} %get-tuple-element.54.scales, bf16[512,2048]{1,0:T(8,128)(2,1)} %collective-permute-done.12.near, ...), custom_call_target="tpu_custom_call" | custom-call | flops 1073741824 | bytes 6291456 | tf_op jit(solution)/shard_map/pick/pallas_call | solution.py:28
  150.9 7.8 %collective-permute-done.16.refs_1_.refs_2_ = bf16[256,2048]{1,0:T(8,128)(2,1)S(1)} collective-permute-done((bf16[256,2048]{1,0:T(8,128)(2,1)S(1)}, bf16[256,2048]{1,0:T(8,128)(2,1)S(1)}, u32[]{:S(2)}, u32[]{:S(2)}) %collective-permute-start.16) | collective-permute-done | bytes 1048608 | tf_op jit(solution)/shard_map/ppermute | solution.py:237
  161.0 2.7 collective-permute-done.6.far
  171.3 14.5 %collective-permute-done.5.far = bf16[512,256]{1,0:T(8,128)(2,1)} collective-permute-done((bf16[512,256]{1,0:T(8,128)(2,1)}, bf16[512,256]{1,0:T(8,128)(2,1)}, u32[]{:S(2)}, u32[]{:S(2)}) %collective-permute-start.5) | collective-permute-done | bytes 262176 | tf_op jit(solution)/shard_map/ppermute | solution.py:275
  190.4 2.8 copy-done
  193.2 3.4 %hidden.1.refs_0_ = bf16[768,2048]{1,0:T(8,128)(2,1)S(1)} custom-call(s32[8]{0:T(128)S(1)} %stack.66.order, s32[4]{0:T(128)S(1)} %pad_add_fusion.2.groups.places, bf16[1,1,2048,1536]{3,2,1,0:T(8,128)(2,1)S(1)} %copy-done), custom_call_target="tpu_custom_call" | custom-call | flops 62914560 | bytes 14155776 | tf_op jit(solution)/shard_map/hidden/pallas_call | solution.py:28
  201.3 5.2 %collective-permute-done.11.refs_9_.refs_8_ = bf16[256,256]{1,0:T(8,128)(2,1)} collective-permute-done((bf16[256,256]{1,0:T(8,128)(2,1)}, bf16[256,256]{1,0:T(8,128)(2,1)}, u32[]{:S(2)}, u32[]{:S(2)}) %collective-permute-start.11) | collective-permute-done | bytes 131104 | tf_op jit(solution)/shard_map/ppermute | solution.py:237
  206.6 2.7 product.5
  209.3 3.0 %collective-permute-done.10.refs_8_ = bf16[256,256]{1,0:T(8,128)(2,1)S(1)} collective-permute-done((bf16[256,256]{1,0:T(8,128)(2,1)S(1)}, bf16[256,256]{1,0:T(8,128)(2,1)S(1)}, u32[]{:S(2)}, u32[]{:S(2)}) %collective-permute-start.10) | collective-permute-done | bytes 131104 | tf_op jit(solution)/shard_map/ppermute | solution.py:237
  212.4 2.7 product.6
  215.1 3.0 %product.7 = (bf16[384,512]{1,0:T(8,128)(2,1)}, bf16[384,512]{1,0:T(8,128)(2,1)S(1)}) custom-call(bf16[768,2048]{1,0:T(8,128)(2,1)S(1)} %hidden.1.refs_0_, bf16[256,2048]{1,0:T(8,128)(2,1)S(1)} %copy-done.6, bf16[256,2048]{1,0:T(8,128)(2,1)S(1)} %copy-done.9, bf16[256,2048]{1,0:T(8,128)(2,1)S(1)} %copy-done.15, ...), custom_call_target="tpu_custom_call" | custom-call | flops 1610612736 | bytes 6029312 | tf_op jit(solution)/shard_map/product/pallas_call | solution.py:28
  218.6 3.0 %product.8 = (bf16[384,512]{1,0:T(8,128)(2,1)}, bf16[384,512]{1,0:T(8,128)(2,1)S(1)}) custom-call(bf16[768,2048]{1,0:T(8,128)(2,1)S(1)} %hidden.1.refs_0_, bf16[256,2048]{1,0:T(8,128)(2,1)S(1)} %copy-done.6, bf16[256,2048]{1,0:T(8,128)(2,1)S(1)} %copy-done.9, bf16[256,2048]{1,0:T(8,128)(2,1)S(1)} %copy-done.15, ...), custom_call_target="tpu_custom_call" | custom-call | flops 1610612736 | bytes 6029312 | tf_op jit(solution)/shard_map/product/pallas_call | solution.py:28
  221.9 3.0 %product.9 = (bf16[384,512]{1,0:T(8,128)(2,1)S(1)}, bf16[384,512]{1,0:T(8,128)(2,1)S(1)}) custom-call(bf16[768,2048]{1,0:T(8,128)(2,1)S(1)} %hidden.1.refs_0_, bf16[256,2048]{1,0:T(8,128)(2,1)S(1)} %copy-done.7, bf16[256,2048]{1,0:T(8,128)(2,1)S(1)} %copy-done.10, bf16[256,2048]{1,0:T(8,128)(2,1)S(1)} %copy-done.16, ...), custom_call_target="tpu_custom_call" | custom-call | flops 1610612736 | bytes 6029312 | tf_op jit(solution)/shard_map/product/pallas_call | solution.py:28
  232.2 3.8 %back.4.refs_4_ = bf16[1,1,2048,1536]{3,2,1,0:T(8,128)(2,1)} custom-call(s32[8]{0:T(128)S(1)} %stack.66.order, bf16[256,2048]{1,0:T(8,128)(2,1)S(1)} %copy-done.7, bf16[256,2048]{1,0:T(8,128)(2,1)S(1)} %copy-done.10, bf16[1,768,2048]{2,1,0:T(8,128)(2,1)S(1)} %copy-done.1, bf16[1,1,2048,1536]{3,2,1,0:T(8,128)(2,1)S(1)} %bitcast.26), custom_call_target="tpu_custom_call" | custom-call | flops 1610612736 | bytes 7602176 | tf_op jit(solution)/shard_map/back/pallas_call | solution.py:28
  236.0 7.7 %collective-permute-done.26.far = bf16[192,512]{1,0:T(8,128)(2,1)S(1)} collective-permute-done((bf16[192,512]{1,0:T(8,128)(2,1)S(1)}, bf16[192,512]{1,0:T(8,128)(2,1)S(1)}, u32[]{:S(2)}, u32[]{:S(2)}) %collective-permute-start.26) | collective-permute-done | bytes 196640 | tf_op jit(solution)/shard_map/ppermute | solution.py:301
  251.7 5.1 %back.5.refs_4_ = bf16[1,1,2048,1536]{3,2,1,0:T(8,128)(2,1)} custom-call(s32[8]{0:T(128)S(1)} %stack.66.order, bf16[256,2048]{1,0:T(8,128)(2,1)S(1)} %copy-done.16, bf16[256,2048]{1,0:T(8,128)(2,1)} %collective-permute-done.15.refs_1_.refs_4_, bf16[1,768,2048]{2,1,0:T(8,128)(2,1)S(1)} %copy-done.1, ...), custom_call_target="tpu_custom_call", output_to_operand_aliasing={{}: (5, {})} | custom-call | flops 1610612736 | bytes 7602176 | tf_op jit(solution)/shard_map/back/pallas_call | solution.py:28
  261.2 4.7 %collective-permute-done.33.across = bf16[192,512]{1,0:T(8,128)(2,1)S(1)} collective-permute-done((bf16[192,512]{1,0:T(8,128)(2,1)S(1)}, bf16[192,512]{1,0:T(8,128)(2,1)S(1)}, u32[]{:S(2)}, u32[]{:S(2)}) %collective-permute-start.33) | collective-permute-done | bytes 196640 | tf_op jit(solution)/shard_map/ppermute | solution.py:320
  268.8 5.4 %back.6.refs_12_ = bf16[1,1,2048,1536]{3,2,1,0:T(8,128)(2,1)} custom-call(s32[8]{0:T(128)S(1)} %stack.66.order, bf16[256,2048]{1,0:T(8,128)(2,1)S(1)} %copy-done.13, bf16[256,2048]{1,0:T(8,128)(2,1)} %collective-permute-done.14.refs_1_.refs_6_, bf16[1,768,2048]{2,1,0:T(8,128)(2,1)S(1)} %copy-done.1, ...), custom_call_target="tpu_custom_call", output_to_operand_aliasing={{}: (5, {})} | custom-call | flops 1610612736 | bytes 7602176 | tf_op jit(solution)/shard_map/back/pallas_call | solution.py:28
  274.1 4.9 %back.7 = bf16[1,1,2048,1536]{3,2,1,0:T(8,128)(2,1)} custom-call(s32[8]{0:T(128)S(1)} %stack.66.order, bf16[256,512]{1,0:T(8,128)(2,1)S(1)} %copy-done.19, bf16[256,512]{1,0:T(8,128)(2,1)S(1)} %copy-done.21, bf16[256,512]{1,0:T(8,128)(2,1)S(1)} %get-tuple-element.57.refs_2_.refs_7_, ...), custom_call_target="tpu_custom_call", output_to_operand_aliasing={{}: (13, {})} | custom-call | flops 1610612736 | bytes 7602176 | tf_op jit(solution)/shard_map/back/pallas_call | solution.py:28
  (171 shorter events, 69.7 us)
Async XLA Ops:
  0.6 49.0 %collective-permute-start = (bf16[512,2048]{1,0:T(8,128)(2,1)}, bf16[512,2048]{1,0:T(8,128)(2,1)}, u32[]{:S(2)}, u32[]{:S(2)}) collective-permute-start(bf16[512,2048]{1,0:T(8,128)(2,1)} %bitcast.27), channel_id=1, source_target_pairs={{0,8},{4,12},{8,0},{12,4},{16,24},{20,28},{24,16},{28,20},{1,9},{5... | collective-permute-start | bytes 6291464 | tf_op jit(solution)/shard_map/ppermute | solution.py:175
  3.7 47.9 %collective-permute-start.12 = (bf16[512,2048]{1,0:T(8,128)(2,1)}, bf16[512,2048]{1,0:T(8,128)(2,1)}, u32[]{:S(2)}, u32[]{:S(2)}) collective-permute-start(bf16[512,2048]{1,0:T(8,128)(2,1)} %bitcast.28), channel_id=1, source_target_pairs={{8,16},{16,8},{12,20},{20,12},{9,17},{17,9},{13,21},{21,13},{10,18... | collective-permute-start | bytes 6291464 | tf_op jit(solution)/shard_map/ppermute | solution.py:176
  49.7 89.4 %collective-permute-start.1 = (bf16[512,2048]{1,0:T(8,128)(2,1)}, bf16[512,2048]{1,0:T(8,128)(2,1)}, u32[]{:S(2)}, u32[]{:S(2)}) collective-permute-start(bf16[512,2048]{1,0:T(8,128)(2,1)} %collective-permute-done.near), channel_id=1, source_target_pairs={{8,16},{16,8},{12,20},{20,12},{9,17},{17,9},{13,21},{21,13},{10,18... | collective-permute-start | bytes 6291464 | tf_op jit(solution)/shard_map/ppermute | solution.py:267
  51.6 91.2 %collective-permute-start.13 = (bf16[512,2048]{1,0:T(8,128)(2,1)}, bf16[512,2048]{1,0:T(8,128)(2,1)}, u32[]{:S(2)}, u32[]{:S(2)}) collective-permute-start(bf16[512,2048]{1,0:T(8,128)(2,1)} %collective-permute-done.12.near), channel_id=1, source_target_pairs={{16,24},{20,28},{8,0},{12,4},{17,25},{21,29},{9,1},{13,5},{18,26},... | collective-permute-start | bytes 6291464 | tf_op jit(solution)/shard_map/ppermute | solution.py:268
  132.6 26.1 %collective-permute-start.16 = (bf16[256,2048]{1,0:T(8,128)(2,1)S(1)}, bf16[256,2048]{1,0:T(8,128)(2,1)S(1)}, u32[]{:S(2)}, u32[]{:S(2)}) collective-permute-start(bf16[256,2048]{1,0:T(8,128)(2,1)S(1)} %get-tuple-element.70), channel_id=1, source_target_pairs={{0,4},{4,0},{8,12},{12,8},{16,20},{20,16},{24,28},{28,24},{1,5},{5... | collective-permute-start | bytes 3145736 | tf_op jit(solution)/shard_map/ppermute | solution.py:237
  137.0 63.1 %collective-permute-start.15 = (bf16[256,2048]{1,0:T(8,128)(2,1)}, bf16[256,2048]{1,0:T(8,128)(2,1)}, u32[]{:S(2)}, u32[]{:S(2)}) collective-permute-start(bf16[256,2048]{1,0:T(8,128)(2,1)} %get-tuple-element.68), channel_id=1, source_target_pairs={{0,4},{4,0},{8,12},{12,8},{16,20},{20,16},{24,28},{28,24},{1,5},{5... | collective-permute-start | bytes 3145736 | tf_op jit(solution)/shard_map/ppermute | solution.py:237
  141.5 23.5 %collective-permute-start.4 = (bf16[512,512]{1,0:T(8,128)(2,1)S(1)}, bf16[512,512]{1,0:T(8,128)(2,1)S(1)}, u32[]{:S(2)}, u32[]{:S(2)}) collective-permute-start(bf16[512,512]{1,0:T(8,128)(2,1)S(1)} %get-tuple-element.103), channel_id=1, source_target_pairs={{16,24},{20,28},{8,0},{12,4},{17,25},{21,29},{9,1},{13,5},{18,26},... | collective-permute-start | bytes 1572872 | tf_op jit(solution)/shard_map/ppermute | solution.py:275
  147.4 59.1 %collective-permute-start.14 = (bf16[256,2048]{1,0:T(8,128)(2,1)}, bf16[256,2048]{1,0:T(8,128)(2,1)}, u32[]{:S(2)}, u32[]{:S(2)}) collective-permute-start(bf16[256,2048]{1,0:T(8,128)(2,1)} %get-tuple-element.66), channel_id=1, source_target_pairs={{0,4},{4,0},{8,12},{12,8},{16,20},{20,16},{24,28},{28,24},{1,5},{5... | collective-permute-start | bytes 3145736 | tf_op jit(solution)/shard_map/ppermute | solution.py:237
  159.7 27.0 %collective-permute-start.2 = (bf16[512,512]{1,0:T(8,128)(2,1)}, bf16[512,512]{1,0:T(8,128)(2,1)}, u32[]{:S(2)}, u32[]{:S(2)}) collective-permute-start(bf16[512,512]{1,0:T(8,128)(2,1)} %get-tuple-element.105), channel_id=1, source_target_pairs={{16,24},{20,28},{8,0},{12,4},{17,25},{21,29},{9,1},{13,5},{18,26},... | collective-permute-start | bytes 1572872 | tf_op jit(solution)/shard_map/ppermute | solution.py:275
  163.7 25.7 %collective-permute-start.3 = (bf16[512,512]{1,0:T(8,128)(2,1)}, bf16[512,512]{1,0:T(8,128)(2,1)}, u32[]{:S(2)}, u32[]{:S(2)}) collective-permute-start(bf16[512,512]{1,0:T(8,128)(2,1)} %get-tuple-element.104), channel_id=1, source_target_pairs={{16,24},{20,28},{8,0},{12,4},{17,25},{21,29},{9,1},{13,5},{18,26},... | collective-permute-start | bytes 1572872 | tf_op jit(solution)/shard_map/ppermute | solution.py:275
  165.8 20.0 %collective-permute-start.5 = (bf16[512,256]{1,0:T(8,128)(2,1)}, bf16[512,256]{1,0:T(8,128)(2,1)}, u32[]{:S(2)}, u32[]{:S(2)}) collective-permute-start(bf16[512,256]{1,0:T(8,128)(2,1)} %get-tuple-element.102), channel_id=1, source_target_pairs={{16,24},{20,28},{8,0},{12,4},{17,25},{21,29},{9,1},{13,5},{18,26},... | collective-permute-start | bytes 786440 | tf_op jit(solution)/shard_map/ppermute | solution.py:275
  185.9 20.7 %collective-permute-start.11 = (bf16[256,256]{1,0:T(8,128)(2,1)}, bf16[256,256]{1,0:T(8,128)(2,1)}, u32[]{:S(2)}, u32[]{:S(2)}) collective-permute-start(bf16[256,256]{1,0:T(8,128)(2,1)} %get-tuple-element.64), channel_id=1, source_target_pairs={{0,4},{4,0},{8,12},{12,8},{16,20},{20,16},{24,28},{28,24},{1,5},{5... | collective-permute-start | bytes 393224 | tf_op jit(solution)/shard_map/ppermute | solution.py:237
  186.8 28.3 %collective-permute-start.9 = (bf16[256,512]{1,0:T(8,128)(2,1)}, bf16[256,512]{1,0:T(8,128)(2,1)}, u32[]{:S(2)}, u32[]{:S(2)}) collective-permute-start(bf16[256,512]{1,0:T(8,128)(2,1)} %get-tuple-element.62), channel_id=1, source_target_pairs={{0,4},{4,0},{8,12},{12,8},{16,20},{20,16},{24,28},{28,24},{1,5},{5... | collective-permute-start | bytes 786440 | tf_op jit(solution)/shard_map/ppermute | solution.py:237
  189.4 22.9 %collective-permute-start.10 = (bf16[256,256]{1,0:T(8,128)(2,1)S(1)}, bf16[256,256]{1,0:T(8,128)(2,1)S(1)}, u32[]{:S(2)}, u32[]{:S(2)}) collective-permute-start(bf16[256,256]{1,0:T(8,128)(2,1)S(1)} %get-tuple-element.63), channel_id=1, source_target_pairs={{0,4},{4,0},{8,12},{12,8},{16,20},{20,16},{24,28},{28,24},{1,5},{5... | collective-permute-start | bytes 393224 | tf_op jit(solution)/shard_map/ppermute | solution.py:237
  200.1 21.7 %collective-permute-start.7 = (bf16[256,512]{1,0:T(8,128)(2,1)S(1)}, bf16[256,512]{1,0:T(8,128)(2,1)S(1)}, u32[]{:S(2)}, u32[]{:S(2)}) collective-permute-start(bf16[256,512]{1,0:T(8,128)(2,1)S(1)} %get-tuple-element.60), channel_id=1, source_target_pairs={{0,4},{4,0},{8,12},{12,8},{16,20},{20,16},{24,28},{28,24},{1,5},{5... | collective-permute-start | bytes 786440 | tf_op jit(solution)/shard_map/ppermute | solution.py:237
  209.3 16.1 %collective-permute-start.17 = (bf16[384,256]{1,0:T(8,128)(2,1)}, bf16[384,256]{1,0:T(8,128)(2,1)S(1)}, u32[]{:S(2)}, u32[]{:S(2)}) collective-permute-start(bf16[384,256]{1,0:T(8,128)(2,1)} %get-tuple-element.72), channel_id=1, source_target_pairs={{0,1},{1,0},{2,3},{3,2},{4,5},{5,4},{6,7},{7,6},{8,9},{9,8},{10,11... | collective-permute-start | bytes 589832 | tf_op jit(solution)/shard_map/ppermute | solution.py:299
  215.0 14.9 %collective-permute-start.19 = (bf16[384,256]{1,0:T(8,128)(2,1)}, bf16[384,256]{1,0:T(8,128)(2,1)S(1)}, u32[]{:S(2)}, u32[]{:S(2)}) collective-permute-start(bf16[384,256]{1,0:T(8,128)(2,1)} %get-tuple-element.74), channel_id=1, source_target_pairs={{0,1},{1,0},{2,3},{3,2},{4,5},{5,4},{6,7},{7,6},{8,9},{9,8},{10,11... | collective-permute-start | bytes 589832 | tf_op jit(solution)/shard_map/ppermute | solution.py:299
  225.5 23.2 %collective-permute-start.18 = (bf16[192,256]{1,0:T(8,128)(2,1)S(1)}, bf16[192,256]{1,0:T(8,128)(2,1)S(1)}, u32[]{:S(2)}, u32[]{:S(2)}) collective-permute-start(bf16[192,256]{1,0:T(8,128)(2,1)S(1)} %add_convert_fusion.4), channel_id=1, source_target_pairs={{0,2},{1,3},{2,0},{3,1},{4,6},{5,7},{6,4},{7,5},{8,10},{9,11},{10,... | collective-permute-start | bytes 294920 | tf_op jit(solution)/shard_map/ppermute | solution.py:301
  227.1 19.2 %collective-permute-start.22 = (bf16[192,512]{1,0:T(8,128)(2,1)S(1)}, bf16[192,512]{1,0:T(8,128)(2,1)S(1)}, u32[]{:S(2)}, u32[]{:S(2)}) collective-permute-start(bf16[192,512]{1,0:T(8,128)(2,1)S(1)} %add_convert_fusion.2), channel_id=1, source_target_pairs={{0,2},{1,3},{2,0},{3,1},{4,6},{5,7},{6,4},{7,5},{8,10},{9,11},{10,... | collective-permute-start | bytes 589832 | tf_op jit(solution)/shard_map/ppermute | solution.py:301
  227.8 17.3 %collective-permute-start.24 = (bf16[192,512]{1,0:T(8,128)(2,1)S(1)}, bf16[192,512]{1,0:T(8,128)(2,1)S(1)}, u32[]{:S(2)}, u32[]{:S(2)}) collective-permute-start(bf16[192,512]{1,0:T(8,128)(2,1)S(1)} %add_convert_fusion.1), channel_id=1, source_target_pairs={{0,2},{1,3},{2,0},{3,1},{4,6},{5,7},{6,4},{7,5},{8,10},{9,11},{10,... | collective-permute-start | bytes 589832 | tf_op jit(solution)/shard_map/ppermute | solution.py:301
  230.7 17.0 %collective-permute-start.20 = (bf16[192,256]{1,0:T(8,128)(2,1)S(1)}, bf16[192,256]{1,0:T(8,128)(2,1)S(1)}, u32[]{:S(2)}, u32[]{:S(2)}) collective-permute-start(bf16[192,256]{1,0:T(8,128)(2,1)S(1)} %add_convert_fusion.3), channel_id=1, source_target_pairs={{0,2},{1,3},{2,0},{3,1},{4,6},{5,7},{6,4},{7,5},{8,10},{9,11},{10,... | collective-permute-start | bytes 294920 | tf_op jit(solution)/shard_map/ppermute | solution.py:301
  260.5 24.3 %collective-permute-start.28 = (bf16[384,256]{1,0:T(8,128)(2,1)S(1)}, bf16[384,256]{1,0:T(8,128)(2,1)S(1)}, u32[]{:S(2)}, u32[]{:S(2)}) collective-permute-start(bf16[384,256]{1,0:T(8,128)(2,1)S(1)} %pad_maximum_fusion.3), channel_id=1, source_target_pairs={{0,1},{1,0},{2,3},{3,2},{4,5},{5,4},{6,7},{7,6},{8,9},{9,8},{10,11... | collective-permute-start | bytes 589832 | tf_op jit(solution)/shard_map/ppermute | solution.py:321
  260.6 21.3 %collective-permute-start.32 = (bf16[384,512]{1,0:T(8,128)(2,1)S(1)}, bf16[384,512]{1,0:T(8,128)(2,1)S(1)}, u32[]{:S(2)}, u32[]{:S(2)}) collective-permute-start(bf16[384,512]{1,0:T(8,128)(2,1)S(1)} %pad_maximum_fusion), channel_id=1, source_target_pairs={{0,1},{1,0},{2,3},{3,2},{4,5},{5,4},{6,7},{7,6},{8,9},{9,8},{10,11... | collective-permute-start | bytes 1179656 | tf_op jit(solution)/shard_map/ppermute | solution.py:321
  268.2 15.2 %collective-permute-start.30 = (bf16[384,256]{1,0:T(8,128)(2,1)S(1)}, bf16[384,256]{1,0:T(8,128)(2,1)S(1)}, u32[]{:S(2)}, u32[]{:S(2)}) collective-permute-start(bf16[384,256]{1,0:T(8,128)(2,1)S(1)} %pad_maximum_fusion.4), channel_id=1, source_target_pairs={{0,1},{1,0},{2,3},{3,2},{4,5},{5,4},{6,7},{7,6},{8,9},{9,8},{10,11... | collective-permute-start | bytes 589832 | tf_op jit(solution)/shard_map/ppermute | solution.py:321
  (49 other events, 397.2 us)

commit v2 on v1

v2 whole, which is shorter than its diff:
```python
import functools

import jax
import jax.numpy as jnp
from jax import lax
from jax.experimental import pallas as pl
from jax.experimental.pallas import tpu as pltpu
from jax.sharding import PartitionSpec as P

beta_first = 0.9
beta_second = 0.95
bias_first = 1.0 - 0.9**10
bias_second = 1.0 - 0.95**10
adam_epsilon = 1e-08
learn_rate = 0.001
decay_rate = 0.1

VMEM_LIMIT = 24 * 1024 * 1024
COST = 16
CHUNKS = ((0, 512), (512, 512), (1024, 512), (1536, 512))
ANY = pl.BlockSpec(memory_space=pl.ANY)


def params():
    return pltpu.CompilerParams(vmem_limit_bytes=VMEM_LIMIT)


def call(kernel, name, grid, scalars, ins, specs, outs, out_specs, scratch=(), aliases=None, flops=0, moved=0):
    shift = len(scalars)
    return pl.pallas_call(
        kernel,
        name=name,
        grid_spec=pltpu.PrefetchScalarGridSpec(
            num_scalar_prefetch=shift,
            grid=grid,
            in_specs=specs,
            out_specs=out_specs,
            scratch_shapes=list(scratch),
        ),
        out_shape=outs,
        input_output_aliases={shift + a: b for a, b in (aliases or {}).items()},
        compiler_params=params(),
        cost_estimate=pl.CostEstimate(flops=flops // COST, bytes_accessed=moved // COST, transcendentals=0),
    )(*scalars, *ins)


def after(*values):
    return lax.optimization_barrier(values)


def shape(dims, dtype):
    return jax.ShapeDtypeStruct(dims, dtype)


def hidden_kernel(order, groups, preact, out, turned):
    width = preact.shape[-1] // 2
    gate = preact[0, 0, :, :width].astype(jnp.float32)
    up = preact[0, 0, :, width:].astype(jnp.float32)
    value = gate * jax.nn.sigmoid(gate) * up
    turned[...] = value.T.astype(jnp.bfloat16)
    rows = width // 4
    for g in range(4):
        start = pl.multiple_of(groups[g] * rows, 16)
        out[g * rows : (g + 1) * rows, :] = turned[pl.ds(start, rows), :]


def pack_kernel(tokens, chosen, weights, first, second):
    count, width = second.shape
    first[:count, :] = tokens[0, :, :width]
    second[...] = tokens[0, :, width:]
    first[count:, :] = jnp.zeros_like(first[count:, :])
    length = chosen.shape[1]
    first[count : count + 8, :length] = jnp.concatenate([chosen[...].astype(jnp.float32), weights[...]], axis=0).astype(
        jnp.bfloat16
    )


def table_kernel(middle, experts, *refs):
    infos, picks, scales = refs[:-2], refs[-2], refs[-1]
    info = infos[0][...].astype(jnp.float32)
    if len(infos) == 2:
        info = jnp.where(middle[0] == 1, info, infos[1][...].astype(jnp.float32))
    capacity = picks.shape[0] // 2
    tokens = info.shape[1]
    first, second = info[0:1, :], info[1:2, :]
    weight_one = (info[2:3, :] + info[4:5, :]) + info[6:7, :]
    weight_two = (info[3:4, :] + info[5:6, :]) + info[7:8, :]
    before = lax.broadcasted_iota(jnp.int32, (tokens, tokens), 0)
    after = lax.broadcasted_iota(jnp.int32, (tokens, tokens), 1)
    earlier = (before < after).astype(jnp.float32).astype(jnp.bfloat16)
    for k in range(2):
        expert = experts[k].astype(jnp.float32)
        is_first = first == expert
        named = jnp.logical_or(is_first, second == expert)
        flag = jnp.where(named, 1.0, 0.0)
        position = jnp.dot(
            jnp.broadcast_to(flag, (16, tokens)).astype(jnp.bfloat16), earlier, preferred_element_type=jnp.float32
        )[0:1, :]
        place = jnp.where(named, position, -1.0).astype(jnp.int32)
        slot = lax.broadcasted_iota(jnp.int32, (capacity, tokens), 0)
        hit = slot == place
        value = jnp.where(is_first, weight_one, weight_two)
        picks[k * capacity : (k + 1) * capacity, :] = jnp.where(hit, 1.0, 0.0).astype(jnp.bfloat16)
        scales[k * capacity : (k + 1) * capacity, :] = jnp.sum(jnp.where(hit, value, 0.0), axis=1, keepdims=True)


def pick_kernel(halves, both, middle, picks, scales, *refs):
    near, far, (mine, other) = refs[:halves], refs[halves:-2], refs[-2:]
    capacity = mine.shape[0]

    def step(k):
        rows = jnp.where(middle[0] == 1, near[k][...], far[k][...]) if both else near[k][...]
        value = jnp.dot(picks[...], rows, preferred_element_type=jnp.float32) * scales[...]
        mine[...] = value[:capacity].astype(jnp.bfloat16)
        other[...] = value[capacity:].astype(jnp.bfloat16)

    if halves == 1:
        step(0)
    else:
        for k in range(halves):
            pl.when(pl.program_id(0) // (pl.num_programs(0) // halves) == k)(functools.partial(step, k))


def base_kernel(turned, *refs):
    pieces, out = refs[:-1], refs[-1]
    rows = jnp.concatenate([p[...] for p in pieces], axis=0)
    out[...] = jnp.dot(turned[...], rows, preferred_element_type=jnp.float32)


def product_kernel(base, turned, mine, got, send, keep):
    half = send.shape[0]
    rows = jnp.concatenate([mine[...], got[...]], axis=0)
    total = base[...] + jnp.dot(turned[...], rows, preferred_element_type=jnp.float32)
    send[...] = total[:half].astype(jnp.bfloat16)
    keep[...] = total[half:].astype(jnp.bfloat16)


def back_kernel(count, order, *refs):
    pieces = refs[:count]
    weight, preact, out = refs[count], refs[count + 1], refs[-1]
    width = weight.shape[1]
    rows = jnp.concatenate([p[...] for p in pieces], axis=1)
    back = lax.dot_general(rows, weight[0], (((1,), (1,)), ((), ())), preferred_element_type=jnp.float32)
    gate = preact[0, 0, :, :width].astype(jnp.float32)
    up = preact[0, 0, :, width:].astype(jnp.float32)
    sig = jax.nn.sigmoid(gate)
    out[0, 0, :, :width] = (back * up * sig * (1.0 + gate * (1.0 - sig))).astype(jnp.bfloat16)
    out[0, 0, :, width:] = (back * (gate * sig)).astype(jnp.bfloat16)


def adam_kernel(kept, near, far, master, moment1, moment2, *refs):
    out_master, out_one, out_two, out_weight = refs[-4:]
    gradient = (kept[...].astype(jnp.float32) + near[...].astype(jnp.float32)) + far[...].astype(jnp.float32)
    moment_one = beta_first * moment1[0] + (1.0 - beta_first) * gradient
    moment_two = beta_second * moment2[0] + (1.0 - beta_second) * gradient * gradient
    step_size = (
        moment_one / bias_first / (jnp.sqrt(moment_two / bias_second) + adam_epsilon) + decay_rate * master[0]
    )
    master_next = master[0] - learn_rate * step_size
    out_master[0] = master_next
    out_one[0] = moment_one
    out_two[0] = moment_two
    out_weight[...] = master_next.astype(jnp.bfloat16)


def assemble_kernel(places, own, across, sibling, *refs):
    out = refs[-1]
    rows = own.shape[0]

    def put(g, value):
        out[0, pl.ds(pl.multiple_of(places[g] * rows, 16), rows), :] = value

    put(3, own[...])
    put(2, across[...])
    put(1, sibling[:rows, :])
    put(0, sibling[rows:, :])


def line_body(cotangent, routing, route_weight, saved_preact, weight, master, moment1, moment2):
    tokens, width = cotangent.shape[1:]
    slots, hidden_width = saved_preact.shape[2], weight.shape[1]
    capacity = slots // 8
    rows = hidden_width // 4
    expert = lax.axis_index("expert")
    replica = lax.axis_index("dp")
    z, y = expert // 2, expert % 2
    x, core = replica // 2, replica % 2
    middle = jnp.where((z == 1) | (z == 2), 1, 0).astype(jnp.int32).reshape(1)
    lower = z < 2
    blocks = [z, z ^ 1, jnp.where(lower, 2, 1), jnp.where(lower, 3, 0)]
    order = jnp.stack([b * 2 + s for b in blocks for s in (y, 1 - y)]).astype(jnp.int32)
    experts = jnp.stack([expert, expert ^ 1]).astype(jnp.int32)
    groups = jnp.stack([(1 - x) * 2 + 1 - core, x * 2 + 1 - core, (1 - x) * 2 + core, x * 2 + core]).astype(jnp.int32)

    swap_pair = [(e, e ^ 2) for e in range(8)]
    swap_middle = [(2, 4), (4, 2), (3, 5), (5, 3)]
    to_end = [(4, 6), (5, 7), (2, 0), (3, 1)]
    swap_y = [(e, e ^ 1) for e in range(8)]
    swap_x = [(d, d ^ 2) for d in range(4)]
    swap_core = [(d, d ^ 1) for d in range(4)]

    wide = width // 2
    pieces = [lax.reduce_precision(route_weight[0].T, 8, 7)]
    pieces.append(lax.reduce_precision(route_weight[0].T - pieces[0], 8, 7))
    pieces.append(route_weight[0].T - pieces[0] - pieces[1])
    own = call(
        pack_kernel,
        "pack",
        (),
        (),
        (cotangent, routing[0].T, jnp.concatenate(pieces, axis=0)),
        [pl.BlockSpec(memory_space=pltpu.VMEM)] * 3,
        (shape((tokens + 16, wide), jnp.bfloat16), shape((tokens, wide), jnp.bfloat16)),
        (pl.BlockSpec(memory_space=pltpu.VMEM),) * 2,
        moved=8 * tokens * width,
    )

    def permuted(parts, way):
        return [lax.ppermute(p, "expert", way) for p in parts]

    pair = permuted(own, swap_pair)
    middle_one = permuted(own, swap_middle)

    def tables(*given):
        spec = pl.BlockSpec((16, tokens), lambda i, m, e: (tokens // 16, 0))
        return call(
            table_kernel,
            "tables",
            (1,),
            (middle, experts),
            given,
            [spec] * len(given),
            (shape((2 * capacity, tokens), jnp.bfloat16), shape((2 * capacity, 1), jnp.float32)),
            (
                pl.BlockSpec((2 * capacity, tokens), lambda i, m, e: (0, 0)),
                pl.BlockSpec((2 * capacity, 1), lambda i, m, e: (0, 0)),
            ),
            moved=5 * capacity * tokens,
            flops=10 * capacity * tokens,
        )

    def pick(table, near, far, offset, columns, tile):
        halves, steps = len(near), columns // tile
        each, start = steps // halves, offset // tile
        specs = [
            pl.BlockSpec((2 * capacity, tokens), lambda i, m: (0, 0)),
            pl.BlockSpec((2 * capacity, 1), lambda i, m: (0, 0)),
        ]

        def place(h, i):
            return jnp.clip(i - h * each, 0, each - 1) if halves > 1 else i

        for h in range(halves):
            if far:
                specs.append(pl.BlockSpec((tokens, tile), lambda i, m, h=h: (0, (start + place(h, i)) * m[0])))
            else:
                specs.append(pl.BlockSpec((tokens, tile), lambda i, m, h=h: (0, start + place(h, i))))
        for h in range(len(far)):
            specs.append(pl.BlockSpec((tokens, tile), lambda i, m, h=h: (0, place(h, i) * (1 - m[0]))))
        out = shape((capacity, columns), jnp.bfloat16)
        mine, other = call(
            functools.partial(pick_kernel, halves, bool(far)),
            "pick",
            (steps,),
            (middle,),
            (*table, *near, *far),
            specs,
            (out, out),
            (pl.BlockSpec((capacity, tile), lambda i, m: (0, i)),) * 2,
            flops=4 * capacity * tokens * columns,
            moved=4 * (tokens + capacity) * columns,
        )
        return mine, other, lax.ppermute(other, "expert", swap_y)

    def back(place, pieces, previous):
        specs = [pl.BlockSpec(p.shape, lambda i, o: (0, 0)) for p in pieces]
        specs += [
            pl.BlockSpec((1, hidden_width, width), lambda i, o: (0, 0, 0)),
            pl.BlockSpec((1, 1, capacity, 2 * hidden_width), lambda i, o: (0, 0, o[place], 0)),
        ]
        ins = [*pieces, weight, saved_preact]
        aliases = {}
        if previous is not None:
            aliases = {len(ins): 0}
            ins.append(previous)
            specs.append(ANY)
        return call(
            functools.partial(back_kernel, len(pieces)),
            "back",
            (1,),
            (order,),
            ins,
            specs,
            shape(saved_preact.shape, jnp.bfloat16),
            pl.BlockSpec((1, 1, capacity, 2 * hidden_width), lambda i, o: (0, 0, o[place], 0)),
            aliases=aliases,
            flops=2 * capacity * hidden_width * width,
            moved=hidden_width * width + 6 * capacity * hidden_width + 2 * capacity * width,
        )

    mine0, other0, got0 = pick(tables(own[0]), own, (), 0, width, 512)
    turned = call(
        hidden_kernel,
        "hidden",
        (8,),
        (order, groups),
        (saved_preact,),
        [pl.BlockSpec((1, 1, capacity, 2 * hidden_width), lambda i, o, g: (0, 0, o[i], 0))],
        shape((hidden_width, slots), jnp.bfloat16),
        pl.BlockSpec((hidden_width, capacity), lambda i, o, g: (0, i)),
        scratch=[pltpu.VMEM((hidden_width, capacity), jnp.bfloat16)],
        moved=9 * slots * hidden_width,
        flops=40 * slots * hidden_width,
    )
    grad_preact = back(0, [mine0], None)
    middle_two = permuted(pair[:1], swap_middle)
    end_one = permuted(middle_one[:1], to_end)
    grad_preact = back(1, [got0], grad_preact)
    pair[1], middle_one[1], grad_preact, turned = after(pair[1], middle_one[1], grad_preact, turned)
    middle_two += permuted(pair[1:], swap_middle)
    end_one += permuted(middle_one[1:], to_end)
    mine1, other1, got1 = pick(tables(pair[0]), pair, (), 0, width, 512)
    grad_preact = back(2, [mine1], grad_preact)

    chunks = CHUNKS
    ends = []
    for offset, columns in chunks:
        half, inner = offset // wide, offset % wide
        count = tokens if offset else tokens + 16
        ends.append(lax.ppermute(middle_two[half][:count, inner : inner + columns], "expert", to_end))
    grad_preact = back(3, [got1], grad_preact)
    end_one[1], grad_preact = after(end_one[1], grad_preact)
    mine2, other2, got2 = pick(tables(middle_one[0], end_one[0]), middle_one, end_one, 0, width, 512)
    grad_preact = back(4, [mine2], grad_preact)
    ends[0], grad_preact = after(ends[0], grad_preact)
    last_table = tables(middle_two[0], ends[0])
    early = 6 * capacity

    def base_product(got2):
        return call(
            base_kernel,
            "base",
            (4,),
            (),
            (turned, mine0, got0, mine1, got1, mine2, got2),
            [pl.BlockSpec((hidden_width, early), lambda i: (0, 0))]
            + [pl.BlockSpec((capacity, width // 4), lambda i: (0, i))] * 6,
            shape((hidden_width, width), jnp.float32),
            pl.BlockSpec((hidden_width, width // 4), lambda i: (0, i)),
            flops=2 * hidden_width * early * width,
            moved=2 * (hidden_width * early + early * width) + 4 * hidden_width * width,
        )

    def last_block(chunk, end_two):
        offset, columns = chunk
        half, inner = offset // wide, offset % wide
        return pick(last_table, middle_two[half : half + 1], (end_two,), inner, columns, columns)

    def product(chunk, mine3, got3):
        offset, columns = chunk
        column = offset // columns
        half = shape((2 * rows, columns), jnp.bfloat16)
        part = pl.BlockSpec((capacity, columns), lambda i: (0, 0))
        return call(
            product_kernel,
            "product",
            (1,),
            (),
            (base, turned, mine3, got3),
            [
                pl.BlockSpec((hidden_width, columns), lambda i: (0, column)),
                pl.BlockSpec((hidden_width, 2 * capacity), lambda i: (0, 3)),
                part,
                part,
            ],
            (half, half),
            (pl.BlockSpec((2 * rows, columns), lambda i: (0, 0)),) * 2,
            flops=4 * hidden_width * capacity * columns,
            moved=4 * hidden_width * capacity + 6 * hidden_width * columns,
        )

    def adam(chunk, keep, near, far, previous):
        offset, columns = chunk
        column = offset // columns
        state = pl.BlockSpec((1, rows, columns), lambda i: (0, 0, column))
        second = pl.BlockSpec((rows, columns), lambda i: (1, 0))
        whole = pl.BlockSpec((rows, columns), lambda i: (0, 0))
        out_state = shape(master.shape, jnp.float32)
        return call(
            adam_kernel,
            "adam",
            (1,),
            (),
            (keep, near, far, master, moment1, moment2, *previous),
            [second, second, whole, state, state, state] + [ANY] * len(previous),
            (out_state, out_state, out_state, shape((rows, columns), jnp.bfloat16)),
            (state, state, state, whole),
            aliases={6 + k: k for k in range(len(previous))},
            flops=20 * rows * columns,
            moved=32 * rows * columns,
        )

    def assemble(chunk, fresh, crossed, sibling, last):
        offset, columns = chunk
        column = offset // columns
        return call(
            assemble_kernel,
            "assemble",
            (1,),
            (groups,),
            (fresh, crossed, sibling, *last),
            [
                pl.BlockSpec((rows, columns), lambda i, g: (0, 0)),
                pl.BlockSpec((rows, columns), lambda i, g: (0, 0)),
                pl.BlockSpec((2 * rows, columns), lambda i, g: (0, 0)),
            ]
            + [ANY] * len(last),
            shape((1, hidden_width, width), jnp.bfloat16),
            pl.BlockSpec((1, hidden_width, columns), lambda i, g: (0, 0, column)),
            aliases={3: 0} if last else None,
            moved=16 * rows * columns,
        )

    states, next_weight = (), ()
    total = len(chunks)
    mines, gots, others3 = [], [], []
    sends, keeps, nears, acrosses, fars = {}, {}, {}, {}, {}
    freshes, crosseds, siblings = {}, {}, {}

    def tied(value, token):
        return value if token is None else after(value, token)[0]

    def sum_core(k, token):
        sends[k], keeps[k] = product(chunks[k], mines[k], tied(gots[k], token))
        nears[k] = lax.ppermute(sends[k], "dp", swap_core)
        return sends[k]

    def sum_x(k, token):
        near = tied(nears[k], token)
        acrosses[k] = (keeps[k][:rows].astype(jnp.float32) + near[:rows].astype(jnp.float32)).astype(jnp.bfloat16)
        nears[k] = near
        fars[k] = lax.ppermute(acrosses[k], "dp", swap_x)
        return acrosses[k]

    def update(k, token):
        nonlocal states
        *states, freshes[k] = adam(chunks[k], keeps[k], nears[k], tied(fars[k], token), states)
        crosseds[k] = lax.ppermute(freshes[k], "dp", swap_x)
        return freshes[k]

    def gather_core(k, token):
        crosseds[k] = tied(crosseds[k], token)
        both = jnp.concatenate([freshes[k], crosseds[k]], axis=0)
        siblings[k] = lax.ppermute(both, "dp", swap_core)
        return both

    def gathered(k, token):
        nonlocal next_weight
        next_weight = (assemble(chunks[k], freshes[k], crosseds[k], tied(siblings[k], token), next_weight),)
        return next_weight[0]

    stages = (sum_core, sum_x, update, gather_core, gathered)
    for k in range(total):
        mine3, other3, got3 = last_block(chunks[k], ends[k])
        mines.append(mine3)
        gots.append(got3)
        done = []
        if k == 0:
            got2, _ = after(got2, other3)
            grad_preact = back(5, [got2], grad_preact)
            done = [grad_preact, base_product(got2)]
            base = done[1]
        for lag, stage in enumerate(stages):
            if k - 1 - lag >= 0:
                done.append(stage(k - 1 - lag, other3))
        if k + 1 < total:
            ends[k + 1], *done = after(ends[k + 1], *done)
            if k == 0:
                grad_preact, base = done
    grad_preact = back(6, mines, grad_preact)
    for k in range(total, total + len(stages)):
        for lag, stage in reversed(tuple(enumerate(stages))):
            if 0 <= k - 1 - lag < total:
                stage(k - 1 - lag, None)
    gots[-1], _ = after(gots[-1], acrosses[total - 1])
    grad_preact = back(7, gots, grad_preact)
    return (grad_preact, next_weight[0], *states)


def body(cotangent, routing, route_weight, saved_preact, weight, master, moment1, moment2):
    n_expert = lax.axis_size("expert")
    tokens = cotangent[0]
    width = tokens.shape[1]
    slots = saved_preact.shape[2]
    hidden_width = weight.shape[1]
    capacity = slots // n_expert
    route_count = routing.shape[2]
    chosen = routing[0].reshape(-1)
    onehot = (chosen[:, None] == jnp.arange(n_expert, dtype=jnp.int32)[None, :]).astype(jnp.int32)
    earlier = jnp.cumsum(onehot, axis=0) - onehot
    position = jnp.sum(earlier * onehot, axis=1)
    target = chosen * capacity + position
    source_token = jnp.arange(chosen.shape[0], dtype=jnp.int32) // route_count
    token_table = jnp.zeros((slots,), jnp.int32).at[target].set(source_token)
    weight_table = jnp.zeros((slots,), jnp.float32).at[target].set(route_weight[0].reshape(-1))
    scaled = (tokens[token_table].astype(jnp.float32) * weight_table[:, None]).astype(jnp.bfloat16)
    arrived = lax.all_to_all(
        scaled.reshape(n_expert, capacity, width), "expert", split_axis=0, concat_axis=0, tiled=True
    )
    arrived = arrived.reshape(slots, width)
    preact = saved_preact[0, 0].astype(jnp.float32)
    gate_value = preact[:, :hidden_width]
    up_value = preact[:, hidden_width:]
    sigmoid_gate = jax.nn.sigmoid(gate_value)
    activated = gate_value * sigmoid_gate
    hidden = (activated * up_value).astype(jnp.bfloat16)
    back = lax.dot_general(
        arrived, weight[0], (((1,), (1,)), ((), ())), preferred_element_type=jnp.float32
    )
    grad_gate = back * up_value * sigmoid_gate * (1.0 + gate_value * (1.0 - sigmoid_gate))
    grad_up = back * activated
    grad_preact = jnp.concatenate([grad_gate, grad_up], axis=1).astype(jnp.bfloat16)[None, None]
    gradient = lax.psum_scatter(
        lax.dot_general(
            hidden, arrived, (((0,), (0,)), ((), ())), preferred_element_type=jnp.float32
        ).astype(jnp.bfloat16),
        "dp",
        scatter_dimension=0,
        tiled=True,
    ).astype(jnp.float32)
    moment_one = beta_first * moment1[0] + (1.0 - beta_first) * gradient
    moment_two = beta_second * moment2[0] + (1.0 - beta_second) * gradient * gradient
    step_size = (
        moment_one / bias_first / (jnp.sqrt(moment_two / bias_second) + adam_epsilon)
        + decay_rate * master[0]
    )
    master_next = master[0] - learn_rate * step_size
    weight_next = lax.all_gather(master_next.astype(jnp.bfloat16), "dp", axis=0, tiled=True)
    return (grad_preact, weight_next[None], master_next[None], moment_one[None], moment_two[None])


def solution(mesh):
    placed = (
        P("dp", "expert", None),
        P("dp", "expert", None),
        P("dp", "expert", None),
        P("dp", "expert", None, None),
        P("expert", None, None),
        P("expert", "dp", None),
        P("expert", "dp", None),
        P("expert", "dp", None),
    )
    line = mesh.shape["expert"] == 8 and mesh.shape["dp"] == 4
    return jax.shard_map(
        line_body if line else body,
        mesh=mesh,
        in_specs=placed,
        out_specs=(
            P("dp", "expert", None, None),
            P("expert", None, None),
            P("expert", "dp", None),
            P("expert", "dp", None),
            P("expert", "dp", None),
        ),
        check_vma=False,
    )
```

time: 287 us -> 215 us (0.75)
  blocking collectives: 71 us -> 0 us
  starting transfers between devices: 35.3 us -> 42 us
  Pallas kernels: 72.6 us -> 66.5 us
  local copies, waits for them, and re-layouts: 12.3 us -> 6.37 us
  waiting for transfers between devices: 91.7 us -> 97 us
    all_gather x1 -> x0, blocking collectives: 71 us -> none  [line_body(): info = lax.all_gather(info, 'expert')]
    ppermute x37 -> x35, starting transfers between devices: 35.3 us -> 42 us  [the longest x8 13.9 us: permuted(): return [lax.ppermute(p, 'expert', way) for p in parts]]
    pallas_call x29 -> x34, Pallas kernels: 72.6 us -> 66.5 us  [call(): pl.pallas_call(kernel, name=name, grid_spec=pltpu.PrefetchScalarGridSpec(...]
    ppermute x37 -> x35, waiting for transfers between devices: 91.7 us -> 97 us  [the longest x7 36 us: pick(): return (mine, other, lax.ppermute(other, 'expert', swap_y))]
    slice x2 -> x3, local copies, waits for them, and re-layouts: 4.21 us -> 0.14 us  [line_body(): middle_two[half][:count, inner:inner + columns]]
    unnamed x72 -> x22, local copies, waits for them, and re-layouts: 7.96 us -> 6.15 us
  transfers between devices with their start and end apart: 37 -> 35, of which waited for: 9 -> 15; matrix products, arithmetic and copies ran while one was open for 2% -> 0% of each run, Pallas kernels for 25% -> 30%
where the time goes in v2:
time: 215 us; the launch traced here: 214 us
  waiting for transfers between devices  97 us (45%)
  Pallas kernels  66.5 us (31%)
  starting transfers between devices  42 us (20%)
  local copies, waits for them, and re-layouts  6.37 us (3%)
    pallas_call x34, Pallas kernels, call(): pl.pallas_call(kernel, name=name, grid_spec=pltpu.PrefetchScalarGridSpec(...  66.5 us
    ppermute x7, waiting for transfers between devices, pick(): return (mine, other, lax.ppermute(other, 'expert', swap_y))  36 us
    ppermute x8, waiting for transfers between devices, permuted(): return [lax.ppermute(p, 'expert', way) for p in parts]  25.9 us
    ppermute x4, waiting for transfers between devices, line_body(): lax.ppermute(middle_two[half][:count, inner:inner + columns], 'expert', t...  16.9 us
    ppermute x8, starting transfers between devices, permuted(): return [lax.ppermute(p, 'expert', way) for p in parts]  13.9 us
    ppermute x4, waiting for transfers between devices, sum_x(): fars[k] = lax.ppermute(acrosses[k], 'dp', swap_x)  9.86 us
    ppermute x7, starting transfers between devices, pick(): return (mine, other, lax.ppermute(other, 'expert', swap_y))  9.01 us
    ppermute x4, starting transfers between devices, update(): crosseds[k] = lax.ppermute(freshes[k], 'dp', swap_x)  8.93 us
  transfers between devices with their start and end apart: 35, of which 15 were waited for; matrix products, arithmetic and copies ran while one was open for 0% of the time, Pallas kernels for 30%

profile of v2, /device:TPU:0, one launch (start us, length us, event | category | flops | bytes accessed | tf_op | source)
XLA Modules:
  0.0 214.0 jit_solution(1779697316552601827)
XLA Ops:
  6.8 4.9 %collective-permute-start = (bf16[528,1024]{1,0:T(8,128)(2,1)}, bf16[528,1024]{1,0:T(8,128)(2,1)S(1)}, u32[]{:S(2)}, u32[]{:S(2)}) collective-permute-start(bf16[528,1024]{1,0:T(8,128)(2,1)} %get-tuple-element.74.refs_0_), channel_id=1, source_target_pairs={{0,8},{4,12},{8,0},{12,4},{16,24},{20,28},{24,16},{28,20},{1,9},{5... | collective-permute-start | bytes 3244040 | tf_op jit(solution)/shard_map/ppermute | solution.py:219
  13.5 4.6 %pick.7 = (bf16[256,2048]{1,0:T(8,128)(2,1)S(1)}, bf16[256,2048]{1,0:T(8,128)(2,1)}) custom-call(s32[1]{0:T(128)} %bitcast.8.middle, bf16[512,512]{1,0:T(8,128)(2,1)S(1)} %get-tuple-element.78.picks, f32[512,1]{1,0:T(8,128)S(1)} %get-tuple-element.79.scales, bf16[528,1024]{1,0:T(8,128)(2,1)} %get-tuple-element.74.refs_0_, ...), custom_call_target="tpu_custom_call" | custom-call | flops 67108864 | bytes 393216 | tf_op jit(solution)/shard_map/pick/pallas_call | solution.py:30
  25.3 2.8 %copy-done = bf16[1,1,2048,1536]{3,2,1,0:T(8,128)(2,1)S(1)} copy-done((bf16[1,1,2048,1536]{3,2,1,0:T(8,128)(2,1)S(1)}, bf16[1,1,2048,1536]{3,2,1,0:T(8,128)(2,1)}, u32[]{:S(2)}) %copy-start) | copy-done | bytes 6291480
  28.1 3.2 %hidden.1.turned = bf16[768,2048]{1,0:T(8,128)(2,1)S(1)} custom-call(s32[8]{0:T(128)S(1)} %stack.59.order, s32[4]{0:T(128)S(1)} %pad_add_fusion.1.groups.places, bf16[1,1,2048,1536]{3,2,1,0:T(8,128)(2,1)S(1)} %copy-done), custom_call_target="tpu_custom_call" | custom-call | flops 3932160 | bytes 884736 | tf_op jit(solution)/shard_map/hidden/pallas_call | solution.py:30
  31.5 2.6 %back.8.refs_3_ = bf16[1,1,2048,1536]{3,2,1,0:T(8,128)(2,1)} custom-call(s32[8]{0:T(128)S(1)} %stack.59.order, bf16[256,2048]{1,0:T(8,128)(2,1)S(1)} %copy-done.6, bf16[1,768,2048]{2,1,0:T(8,128)(2,1)S(1)} %copy-done.1, bf16[1,1,2048,1536]{3,2,1,0:T(8,128)(2,1)S(1)} %bitcast.32), custom_call_target="tpu_custom_call" | custom-call | flops 50331648 | bytes 237568 | tf_op jit(solution)/shard_map/back/pallas_call | solution.py:30
  34.1 9.6 %collective-permute-done.7.refs_0_.refs_1_ = bf16[256,2048]{1,0:T(8,128)(2,1)} collective-permute-done((bf16[256,2048]{1,0:T(8,128)(2,1)}, bf16[256,2048]{1,0:T(8,128)(2,1)}, u32[]{:S(2)}, u32[]{:S(2)}) %collective-permute-start.7) | collective-permute-done | bytes 1048608 | tf_op jit(solution)/shard_map/ppermute | solution.py:273
  43.7 3.8 %back.9.refs_3_ = bf16[1,1,2048,1536]{3,2,1,0:T(8,128)(2,1)} custom-call(s32[8]{0:T(128)S(1)} %stack.59.order, bf16[256,2048]{1,0:T(8,128)(2,1)} %collective-permute-done.7.refs_0_.refs_1_, bf16[1,768,2048]{2,1,0:T(8,128)(2,1)S(1)} %copy-done.1, bf16[1,1,2048,1536]{3,2,1,0:T(8,128)(2,1)S(1)} %bitcast.32, ...), custom_call_target="tpu_custom_call", output_to_operand_aliasing={{}: (4, {})} | custom-call | flops 50331648 | bytes 237568 | tf_op jit(solution)/shard_map/back/pallas_call | solution.py:30
  47.5 11.6 %collective-permute-done.5.refs_1_ = bf16[512,1024]{1,0:T(8,128)(2,1)} collective-permute-done((bf16[512,1024]{1,0:T(8,128)(2,1)}, bf16[512,1024]{1,0:T(8,128)(2,1)}, u32[]{:S(2)}, u32[]{:S(2)}) %collective-permute-start.5) | collective-permute-done | bytes 1048608 | tf_op jit(solution)/shard_map/ppermute | solution.py:219
  60.1 3.7 %pick.8 = (bf16[256,2048]{1,0:T(8,128)(2,1)S(1)}, bf16[256,2048]{1,0:T(8,128)(2,1)S(1)}) custom-call(s32[1]{0:T(128)} %bitcast.8.middle, bf16[512,512]{1,0:T(8,128)(2,1)S(1)} %get-tuple-element.83.picks, f32[512,1]{1,0:T(8,128)S(1)} %get-tuple-element.84.scales, bf16[528,1024]{1,0:T(8,128)(2,1)S(1)} %collective-permute-done.refs_0_, ...), custom_call_target="tpu_custom_call" | custom-call | flops 67108864 | bytes 393216 | tf_op jit(solution)/shard_map/pick/pallas_call | solution.py:30
  70.8 16.0 %collective-permute-done.9.refs_0_.refs_3_ = bf16[256,2048]{1,0:T(8,128)(2,1)S(1)} collective-permute-done((bf16[256,2048]{1,0:T(8,128)(2,1)S(1)}, bf16[256,2048]{1,0:T(8,128)(2,1)S(1)}, u32[]{:S(2)}, u32[]{:S(2)}) %collective-permute-start.9) | collective-permute-done | bytes 1048608 | tf_op jit(solution)/shard_map/ppermute | solution.py:273
  89.3 14.2 %collective-permute-done.8.refs_3_ = bf16[512,1024]{1,0:T(8,128)(2,1)S(1)} collective-permute-done((bf16[512,1024]{1,0:T(8,128)(2,1)}, bf16[512,1024]{1,0:T(8,128)(2,1)S(1)}, u32[]{:S(2)}, u32[]{:S(2)}) %collective-permute-start.8) | collective-permute-done | bytes 1048608 | tf_op jit(solution)/shard_map/ppermute | solution.py:219
  105.3 3.7 %pick.9 = (bf16[256,2048]{1,0:T(8,128)(2,1)S(1)}, bf16[256,2048]{1,0:T(8,128)(2,1)S(1)}) custom-call(s32[1]{0:T(128)} %bitcast.8.middle, bf16[512,512]{1,0:T(8,128)(2,1)S(1)} %get-tuple-element.75.picks, f32[512,1]{1,0:T(8,128)S(1)} %get-tuple-element.76.scales, bf16[528,1024]{1,0:T(8,128)(2,1)} %collective-permute-done.3.refs_0_, ...), custom_call_target="tpu_custom_call" | custom-call | flops 67108864 | bytes 393216 | tf_op jit(solution)/shard_map/pick/pallas_call | solution.py:30
  113.2 2.6 %back.12.refs_3_ = bf16[1,1,2048,1536]{3,2,1,0:T(8,128)(2,1)} custom-call(s32[8]{0:T(128)S(1)} %stack.59.order, bf16[256,2048]{1,0:T(8,128)(2,1)S(1)} %get-tuple-element.90.refs_0_.refs_4_, bf16[1,768,2048]{2,1,0:T(8,128)(2,1)S(1)} %copy-done.1, bf16[1,1,2048,1536]{3,2,1,0:T(8,128)(2,1)S(1)} %bitcast.32, ...), custom_call_target="tpu_custom_call", output_to_operand_aliasing={{}: (4, {})} | custom-call | flops 50331648 | bytes 237568 | tf_op jit(solution)/shard_map/back/pallas_call | solution.py:30
  115.8 11.9 %collective-permute-done.2.refs_1_ = bf16[528,512]{1,0:T(8,128)(2,1)S(1)} collective-permute-done((bf16[528,512]{1,0:T(8,128)(2,1)S(1)}, bf16[528,512]{1,0:T(8,128)(2,1)S(1)}, u32[]{:S(2)}, u32[]{:S(2)}) %collective-permute-start.2) | collective-permute-done | bytes 540704 | tf_op jit(solution)/shard_map/ppermute | solution.py:330
  131.2 3.9 %collective-permute-done.12.refs_0_.refs_5_ = bf16[256,2048]{1,0:T(8,128)(2,1)S(1)} collective-permute-done((bf16[256,2048]{1,0:T(8,128)(2,1)S(1)}, bf16[256,2048]{1,0:T(8,128)(2,1)S(1)}, u32[]{:S(2)}, u32[]{:S(2)}) %collective-permute-start.12) | collective-permute-done | bytes 1048608 | tf_op jit(solution)/shard_map/ppermute | solution.py:273
  137.7 7.1 %base.1 = f32[768,2048]{1,0:T(8,128)S(1)} custom-call(bf16[768,2048]{1,0:T(8,128)(2,1)S(1)} %hidden.1.turned, bf16[256,2048]{1,0:T(8,128)(2,1)S(1)} %copy-done.6, bf16[256,2048]{1,0:T(8,128)(2,1)} %collective-permute-done.7.refs_0_.refs_1_, bf16[256,2048]{1,0:T(8,128)(2,1)S(1)} %get-tuple-element.87.refs_0_.refs_2_, ...), custom_call_target="tpu_custom_call" | custom-call | flops 301989888 | bytes 933888 | tf_op jit(solution)/shard_map/base/pallas_call | solution.py:30
  149.9 6.5 %collective-permute-done.13.got.refs_1_ = bf16[256,512]{1,0:T(8,128)(2,1)S(1)} collective-permute-done((bf16[256,512]{1,0:T(8,128)(2,1)S(1)}, bf16[256,512]{1,0:T(8,128)(2,1)S(1)}, u32[]{:S(2)}, u32[]{:S(2)}) %collective-permute-start.13) | collective-permute-done | bytes 262176 | tf_op jit(solution)/shard_map/ppermute | solution.py:273
  157.2 5.0 %collective-permute-done.17.refs_1_ = bf16[512,512]{1,0:T(8,128)(2,1)S(1)} collective-permute-done((bf16[512,512]{1,0:T(8,128)(2,1)S(1)}, bf16[512,512]{1,0:T(8,128)(2,1)S(1)}, u32[]{:S(2)}, u32[]{:S(2)}) %collective-permute-start.17) | collective-permute-done | bytes 524320 | tf_op jit(solution)/shard_map/ppermute | solution.py:330
  166.4 4.1 %collective-permute-done.26.far = bf16[192,512]{1,0:T(8,128)(2,1)S(1)} collective-permute-done((bf16[192,512]{1,0:T(8,128)(2,1)S(1)}, bf16[192,512]{1,0:T(8,128)(2,1)S(1)}, u32[]{:S(2)}, u32[]{:S(2)}) %collective-permute-start.26) | collective-permute-done | bytes 196640 | tf_op jit(solution)/shard_map/ppermute | solution.py:442
  176.9 5.1 %collective-permute-done.25.far = bf16[192,512]{1,0:T(8,128)(2,1)S(1)} collective-permute-done((bf16[192,512]{1,0:T(8,128)(2,1)S(1)}, bf16[192,512]{1,0:T(8,128)(2,1)S(1)}, u32[]{:S(2)}, u32[]{:S(2)}) %collective-permute-start.25) | collective-permute-done | bytes 196640 | tf_op jit(solution)/shard_map/ppermute | solution.py:442
  194.7 4.1 %collective-permute-done.29.across = bf16[192,512]{1,0:T(8,128)(2,1)S(1)} collective-permute-done((bf16[192,512]{1,0:T(8,128)(2,1)S(1)}, bf16[192,512]{1,0:T(8,128)(2,1)S(1)}, u32[]{:S(2)}, u32[]{:S(2)}) %collective-permute-start.29) | collective-permute-done | bytes 196640 | tf_op jit(solution)/shard_map/ppermute | solution.py:448
  199.0 3.8 %collective-permute-done.27.across = bf16[192,512]{1,0:T(8,128)(2,1)S(1)} collective-permute-done((bf16[192,512]{1,0:T(8,128)(2,1)S(1)}, bf16[192,512]{1,0:T(8,128)(2,1)S(1)}, u32[]{:S(2)}, u32[]{:S(2)}) %collective-permute-start.27) | collective-permute-done | bytes 196640 | tf_op jit(solution)/shard_map/ppermute | solution.py:448
  202.9 2.6 %back.14.refs_6_ = bf16[1,1,2048,1536]{3,2,1,0:T(8,128)(2,1)} custom-call(s32[8]{0:T(128)S(1)} %stack.59.order, bf16[256,512]{1,0:T(8,128)(2,1)S(1)} %get-tuple-element.103.mine.refs_0_, bf16[256,512]{1,0:T(8,128)(2,1)S(1)} %get-tuple-element.108.mine.refs_1_, bf16[256,512]{1,0:T(8,128)(2,1)S(1)} %get-tuple-element.119.refs_2_.mine, ...), custom_call_target="tpu_custom_call", output_to_operand_aliasing={{}: (7, {})} | custom-call | flops 50331648 | bytes 237568 | tf_op jit(solution)/shard_map/back/pallas_call | solution.py:30
  205.5 2.6 %back.15 = bf16[1,1,2048,1536]{3,2,1,0:T(8,128)(2,1)} custom-call(s32[8]{0:T(128)S(1)} %stack.59.order, bf16[256,512]{1,0:T(8,128)(2,1)S(1)} %collective-permute-done.10.got.refs_0_, bf16[256,512]{1,0:T(8,128)(2,1)S(1)} %collective-permute-done.13.got.refs_1_, ...), custom_call_target="tpu_custom_call", output_to_operand_aliasing={{}: (7, {})} | custom-call | flops 50331648 | bytes 237568 | tf_op jit(solution)/shard_map/back/pallas_call | solution.py:30
  (119 shorter events, 73.0 us)
Async XLA Ops:
  5.1 18.8 %collective-permute-start.3 = (bf16[528,1024]{1,0:T(8,128)(2,1)}, bf16[528,1024]{1,0:T(8,128)(2,1)}, u32[]{:S(2)}, u32[]{:S(2)}) collective-permute-start(bf16[528,1024]{1,0:T(8,128)(2,1)} %get-tuple-element.74.refs_0_), channel_id=1, source_target_pairs={{8,16},{16,8},{12,20},{20,12},{9,17},{17,9},{13,21},{21,13},{10,18... | collective-permute-start | bytes 3244040 | tf_op jit(solution)/shard_map/ppermute | solution.py:219
  6.8 52.4 %collective-permute-start = (bf16[528,1024]{1,0:T(8,128)(2,1)}, bf16[528,1024]{1,0:T(8,128)(2,1)S(1)}, u32[]{:S(2)}, u32[]{:S(2)}) collective-permute-start(bf16[528,1024]{1,0:T(8,128)(2,1)} %get-tuple-element.74.refs_0_), channel_id=1, source_target_pairs={{0,8},{4,12},{8,0},{12,4},{16,24},{20,28},{24,16},{28,20},{1,9},{5... | collective-permute-start | bytes 3244040 | tf_op jit(solution)/shard_map/ppermute | solution.py:219
  19.1 24.6 %collective-permute-start.7 = (bf16[256,2048]{1,0:T(8,128)(2,1)}, bf16[256,2048]{1,0:T(8,128)(2,1)}, u32[]{:S(2)}, u32[]{:S(2)}) collective-permute-start(bf16[256,2048]{1,0:T(8,128)(2,1)} %get-tuple-element.80), channel_id=1, source_target_pairs={{0,4},{4,0},{8,12},{12,8},{16,20},{20,16},{24,28},{28,24},{1,5},{5... | collective-permute-start | bytes 3145736 | tf_op jit(solution)/shard_map/ppermute | solution.py:273
  20.6 26.9 %collective-permute-start.6 = (bf16[512,1024]{1,0:T(8,128)(2,1)}, bf16[512,1024]{1,0:T(8,128)(2,1)}, u32[]{:S(2)}, u32[]{:S(2)}) collective-permute-start(bf16[512,1024]{1,0:T(8,128)(2,1)} %get-tuple-element.77.refs_1_), channel_id=1, source_target_pairs={{8,16},{16,8},{12,20},{20,12},{9,17},{17,9},{13,21},{21,13},{10,18... | collective-permute-start | bytes 3145736 | tf_op jit(solution)/shard_map/ppermute | solution.py:219
  22.2 36.9 %collective-permute-start.5 = (bf16[512,1024]{1,0:T(8,128)(2,1)}, bf16[512,1024]{1,0:T(8,128)(2,1)}, u32[]{:S(2)}, u32[]{:S(2)}) collective-permute-start(bf16[512,1024]{1,0:T(8,128)(2,1)} %get-tuple-element.77.refs_1_), channel_id=1, source_target_pairs={{0,8},{4,12},{8,0},{12,4},{16,24},{20,28},{24,16},{28,20},{1,9},{5... | collective-permute-start | bytes 3145736 | tf_op jit(solution)/shard_map/ppermute | solution.py:219
  23.9 79.7 %collective-permute-start.4 = (bf16[528,1024]{1,0:T(8,128)(2,1)}, bf16[528,1024]{1,0:T(8,128)(2,1)}, u32[]{:S(2)}, u32[]{:S(2)}) collective-permute-start(bf16[528,1024]{1,0:T(8,128)(2,1)} %collective-permute-done.3.refs_0_), channel_id=1, source_target_pairs={{16,24},{20,28},{8,0},{12,4},{17,25},{21,29},{9,1},{13,5},{18,26},... | collective-permute-start | bytes 3244040 | tf_op jit(solution)/shard_map/ppermute | solution.py:219
  63.8 22.9 %collective-permute-start.9 = (bf16[256,2048]{1,0:T(8,128)(2,1)S(1)}, bf16[256,2048]{1,0:T(8,128)(2,1)S(1)}, u32[]{:S(2)}, u32[]{:S(2)}) collective-permute-start(bf16[256,2048]{1,0:T(8,128)(2,1)S(1)} %get-tuple-element.86), channel_id=1, source_target_pairs={{0,4},{4,0},{8,12},{12,8},{16,20},{20,16},{24,28},{28,24},{1,5},{5... | collective-permute-start | bytes 3145736 | tf_op jit(solution)/shard_map/ppermute | solution.py:273
  65.4 38.2 %collective-permute-start.8 = (bf16[512,1024]{1,0:T(8,128)(2,1)}, bf16[512,1024]{1,0:T(8,128)(2,1)S(1)}, u32[]{:S(2)}, u32[]{:S(2)}) collective-permute-start(bf16[512,1024]{1,0:T(8,128)(2,1)} %collective-permute-done.6.refs_1_), channel_id=1, source_target_pairs={{16,24},{20,28},{8,0},{12,4},{17,25},{21,29},{9,1},{13,5},{18,26},... | collective-permute-start | bytes 3145736 | tf_op jit(solution)/shard_map/ppermute | solution.py:219
  66.7 43.8 %collective-permute-start.1 = (bf16[528,1024]{1,0:T(8,128)(2,1)S(1)}, bf16[528,1024]{1,0:T(8,128)(2,1)S(1)}, u32[]{:S(2)}, u32[]{:S(2)}) collective-permute-start(bf16[528,1024]{1,0:T(8,128)(2,1)S(1)} %collective-permute-done.refs_0_), channel_id=1, source_target_pairs={{8,16},{16,8},{12,20},{20,12},{9,17},{17,9},{13,21},{21,13},{10,18... | collective-permute-start | bytes 3244040 | tf_op jit(solution)/shard_map/ppermute | solution.py:219
  67.4 62.2 %collective-permute-start.14 = (bf16[512,1024]{1,0:T(8,128)(2,1)}, bf16[512,1024]{1,0:T(8,128)(2,1)S(1)}, u32[]{:S(2)}, u32[]{:S(2)}) collective-permute-start(bf16[512,1024]{1,0:T(8,128)(2,1)} %collective-permute-done.5.refs_1_), channel_id=1, source_target_pairs={{8,16},{16,8},{12,20},{20,12},{9,17},{17,9},{13,21},{21,13},{10,18... | collective-permute-start | bytes 3145736 | tf_op jit(solution)/shard_map/ppermute | solution.py:219
  109.0 26.2 %collective-permute-start.12 = (bf16[256,2048]{1,0:T(8,128)(2,1)S(1)}, bf16[256,2048]{1,0:T(8,128)(2,1)S(1)}, u32[]{:S(2)}, u32[]{:S(2)}) collective-permute-start(bf16[256,2048]{1,0:T(8,128)(2,1)S(1)} %get-tuple-element.96), channel_id=1, source_target_pairs={{0,4},{4,0},{8,12},{12,8},{16,20},{20,16},{24,28},{28,24},{1,5},{5... | collective-permute-start | bytes 3145736 | tf_op jit(solution)/shard_map/ppermute | solution.py:273
  110.6 17.1 %collective-permute-start.2 = (bf16[528,512]{1,0:T(8,128)(2,1)S(1)}, bf16[528,512]{1,0:T(8,128)(2,1)S(1)}, u32[]{:S(2)}, u32[]{:S(2)}) collective-permute-start(bf16[528,512]{1,0:T(8,128)(2,1)S(1)} %slice.48), channel_id=1, source_target_pairs={{16,24},{20,28},{8,0},{12,4},{17,25},{21,29},{9,1},{13,5},{18,26},... | collective-permute-start | bytes 1622024 | tf_op jit(solution)/shard_map/ppermute | solution.py:330
  111.9 32.9 %collective-permute-start.11 = (bf16[512,512]{1,0:T(8,128)(2,1)S(1)}, bf16[512,512]{1,0:T(8,128)(2,1)S(1)}, u32[]{:S(2)}, u32[]{:S(2)}) collective-permute-start(bf16[512,512]{1,0:T(8,128)(2,1)S(1)} %slice.49), channel_id=1, source_target_pairs={{16,24},{20,28},{8,0},{12,4},{17,25},{21,29},{9,1},{13,5},{18,26},... | collective-permute-start | bytes 1572872 | tf_op jit(solution)/shard_map/ppermute | solution.py:330
  129.1 16.2 %collective-permute-start.10 = (bf16[256,512]{1,0:T(8,128)(2,1)S(1)}, bf16[256,512]{1,0:T(8,128)(2,1)S(1)}, u32[]{:S(2)}, u32[]{:S(2)}) collective-permute-start(bf16[256,512]{1,0:T(8,128)(2,1)S(1)} %get-tuple-element.95), channel_id=1, source_target_pairs={{0,4},{4,0},{8,12},{12,8},{16,20},{20,16},{24,28},{28,24},{1,5},{5... | collective-permute-start | bytes 786440 | tf_op jit(solution)/shard_map/ppermute | solution.py:273
  129.8 19.1 %collective-permute-start.15 = (bf16[512,512]{1,0:T(8,128)(2,1)S(1)}, bf16[512,512]{1,0:T(8,128)(2,1)S(1)}, u32[]{:S(2)}, u32[]{:S(2)}) collective-permute-start(bf16[512,512]{1,0:T(8,128)(2,1)S(1)} %get-tuple-element.144), channel_id=1, source_target_pairs={{16,24},{20,28},{8,0},{12,4},{17,25},{21,29},{9,1},{13,5},{18,26},... | collective-permute-start | bytes 1572872 | tf_op jit(solution)/shard_map/ppermute | solution.py:330
  146.0 16.2 %collective-permute-start.17 = (bf16[512,512]{1,0:T(8,128)(2,1)S(1)}, bf16[512,512]{1,0:T(8,128)(2,1)S(1)}, u32[]{:S(2)}, u32[]{:S(2)}) collective-permute-start(bf16[512,512]{1,0:T(8,128)(2,1)S(1)} %get-tuple-element.143), channel_id=1, source_target_pairs={{16,24},{20,28},{8,0},{12,4},{17,25},{21,29},{9,1},{13,5},{18,26},... | collective-permute-start | bytes 1572872 | tf_op jit(solution)/shard_map/ppermute | solution.py:330
  149.4 16.4 %collective-permute-start.16 = (bf16[256,512]{1,0:T(8,128)(2,1)S(1)}, bf16[256,512]{1,0:T(8,128)(2,1)S(1)}, u32[]{:S(2)}, u32[]{:S(2)}) collective-permute-start(bf16[256,512]{1,0:T(8,128)(2,1)S(1)} %get-tuple-element.107), channel_id=1, source_target_pairs={{0,4},{4,0},{8,12},{12,8},{16,20},{20,16},{24,28},{28,24},{1,5},{5... | collective-permute-start | bytes 786440 | tf_op jit(solution)/shard_map/ppermute | solution.py:273
  157.0 16.3 %collective-permute-start.24 = (bf16[384,512]{1,0:T(8,128)(2,1)S(1)}, bf16[384,512]{1,0:T(8,128)(2,1)S(1)}, u32[]{:S(2)}, u32[]{:S(2)}) collective-permute-start(bf16[384,512]{1,0:T(8,128)(2,1)S(1)} %get-tuple-element.110), channel_id=1, source_target_pairs={{0,1},{1,0},{2,3},{3,2},{4,5},{5,4},{6,7},{7,6},{8,9},{9,8},{10,11... | collective-permute-start | bytes 1179656 | tf_op jit(solution)/shard_map/ppermute | solution.py:435
  171.8 18.2 %collective-permute-start.33 = (bf16[192,512]{1,0:T(8,128)(2,1)S(1)}, bf16[192,512]{1,0:T(8,128)(2,1)S(1)}, u32[]{:S(2)}, u32[]{:S(2)}) collective-permute-start(bf16[192,512]{1,0:T(8,128)(2,1)S(1)} %get-tuple-element.139.own), channel_id=1, source_target_pairs={{0,2},{1,3},{2,0},{3,1},{4,6},{5,7},{6,4},{7,5},{8,10},{9,11},{10,... | collective-permute-start | bytes 589832 | tf_op jit(solution)/shard_map/ppermute | solution.py:448
  174.7 11.5 %collective-permute-start.23 = (bf16[192,512]{1,0:T(8,128)(2,1)S(1)}, bf16[192,512]{1,0:T(8,128)(2,1)S(1)}, u32[]{:S(2)}, u32[]{:S(2)}) collective-permute-start(bf16[192,512]{1,0:T(8,128)(2,1)S(1)} %add_convert_fusion.1), channel_id=1, source_target_pairs={{0,2},{1,3},{2,0},{3,1},{4,6},{5,7},{6,4},{7,5},{8,10},{9,11},{10,... | collective-permute-start | bytes 589832 | tf_op jit(solution)/shard_map/ppermute | solution.py:442
  176.3 14.1 %collective-permute-start.21 = (bf16[192,512]{1,0:T(8,128)(2,1)S(1)}, bf16[192,512]{1,0:T(8,128)(2,1)S(1)}, u32[]{:S(2)}, u32[]{:S(2)}) collective-permute-start(bf16[192,512]{1,0:T(8,128)(2,1)S(1)} %add_convert_fusion.2), channel_id=1, source_target_pairs={{0,2},{1,3},{2,0},{3,1},{4,6},{5,7},{6,4},{7,5},{8,10},{9,11},{10,... | collective-permute-start | bytes 589832 | tf_op jit(solution)/shard_map/ppermute | solution.py:442
  190.0 18.1 %collective-permute-start.34 = (bf16[384,512]{1,0:T(8,128)(2,1)S(1)}, bf16[384,512]{1,0:T(8,128)(2,1)S(1)}, u32[]{:S(2)}, u32[]{:S(2)}) collective-permute-start(bf16[384,512]{1,0:T(8,128)(2,1)S(1)} %pad_maximum_fusion.3), channel_id=1, source_target_pairs={{0,1},{1,0},{2,3},{3,2},{4,5},{5,4},{6,7},{7,6},{8,9},{9,8},{10,11... | collective-permute-start | bytes 1179656 | tf_op jit(solution)/shard_map/ppermute | solution.py:454
  194.7 14.9 %collective-permute-start.32 = (bf16[384,512]{1,0:T(8,128)(2,1)S(1)}, bf16[384,512]{1,0:T(8,128)(2,1)S(1)}, u32[]{:S(2)}, u32[]{:S(2)}) collective-permute-start(bf16[384,512]{1,0:T(8,128)(2,1)S(1)} %pad_maximum_fusion.2), channel_id=1, source_target_pairs={{0,1},{1,0},{2,3},{3,2},{4,5},{5,4},{6,7},{7,6},{8,9},{9,8},{10,11... | collective-permute-start | bytes 1179656 | tf_op jit(solution)/shard_map/ppermute | solution.py:454
  198.9 12.2 %collective-permute-start.30 = (bf16[384,512]{1,0:T(8,128)(2,1)S(1)}, bf16[384,512]{1,0:T(8,128)(2,1)S(1)}, u32[]{:S(2)}, u32[]{:S(2)}) collective-permute-start(bf16[384,512]{1,0:T(8,128)(2,1)S(1)} %pad_maximum_fusion.1), channel_id=1, source_target_pairs={{0,1},{1,0},{2,3},{3,2},{4,5},{5,4},{6,7},{7,6},{8,9},{9,8},{10,11... | collective-permute-start | bytes 1179656 | tf_op jit(solution)/shard_map/ppermute | solution.py:454
  (22 other events, 149.1 us)

commit v3 on v2

--- a/solution.py
+++ b/solution.py
@@ -16,16 +16,22 @@
 decay_rate = 0.1
 
 VMEM_LIMIT = 24 * 1024 * 1024
-COST = 16
-CHUNKS = ((0, 512), (512, 512), (1024, 512), (1536, 512))
+COST = 4096
+EARLY = False
+CLAIM = 3_000_000_000
+TILE = 256
+HALF = 1280
+PACK_LIMIT = 56 * 1024 * 1024
+SENT = ((0, 512), (512, 768), (1280, 768))
+CHUNKS = ((0, 512), (512, 768), (1280, 512), (1792, 256))
 ANY = pl.BlockSpec(memory_space=pl.ANY)
 
 
-def params():
-    return pltpu.CompilerParams(vmem_limit_bytes=VMEM_LIMIT)
-
-
-def call(kernel, name, grid, scalars, ins, specs, outs, out_specs, scratch=(), aliases=None, flops=0, moved=0):
+def params(limit):
+    return pltpu.CompilerParams(vmem_limit_bytes=limit)
+
+
+def call(kernel, name, grid, scalars, ins, specs, outs, out_specs, scratch=(), aliases=None, flops=0, moved=0, limit=VMEM_LIMIT):
     shift = len(scalars)
     return pl.pallas_call(
         kernel,
@@ -39,7 +45,7 @@
         ),
         out_shape=outs,
         input_output_aliases={shift + a: b for a, b in (aliases or {}).items()},
-        compiler_params=params(),
+        compiler_params=params(limit),
         cost_estimate=pl.CostEstimate(flops=flops // COST, bytes_accessed=moved // COST, transcendentals=0),
     )(*scalars, *ins)
 
@@ -64,15 +70,20 @@
         out[g * rows : (g + 1) * rows, :] = turned[pl.ds(start, rows), :]
 
 
-def pack_kernel(tokens, chosen, weights, first, second):
-    count, width = second.shape
-    first[:count, :] = tokens[0, :, :width]
-    second[...] = tokens[0, :, width:]
-    first[count:, :] = jnp.zeros_like(first[count:, :])
-    length = chosen.shape[1]
-    first[count : count + 8, :length] = jnp.concatenate([chosen[...].astype(jnp.float32), weights[...]], axis=0).astype(
-        jnp.bfloat16
-    )
+def pack_kernel(tokens, chosen, weights, packed):
+    last = pl.program_id(0) == pl.num_programs(0) - 1
+
+    @pl.when(jnp.logical_not(last))
+    def _():
+        packed[...] = tokens[0]
+
+    @pl.when(last)
+    def _():
+        length = chosen.shape[1]
+        packed[...] = jnp.zeros_like(packed)
+        packed[:8, :length] = jnp.concatenate([chosen[...].astype(jnp.float32), weights[...]], axis=0).astype(
+            jnp.bfloat16
+        )
 
 
 def table_kernel(middle, experts, *refs):
@@ -104,7 +115,8 @@
         scales[k * capacity : (k + 1) * capacity, :] = jnp.sum(jnp.where(hit, value, 0.0), axis=1, keepdims=True)
 
 
-def pick_kernel(halves, both, middle, picks, scales, *refs):
+def pick_kernel(firsts, both, middle, picks, scales, *refs):
+    halves = len(firsts)
     near, far, (mine, other) = refs[:halves], refs[halves:-2], refs[-2:]
     capacity = mine.shape[0]
 
@@ -117,8 +129,9 @@
     if halves == 1:
         step(0)
     else:
-        for k in range(halves):
-            pl.when(pl.program_id(0) // (pl.num_programs(0) // halves) == k)(functools.partial(step, k))
+        late = pl.program_id(0) >= firsts[1]
+        pl.when(jnp.logical_not(late))(functools.partial(step, 0))
+        pl.when(late)(functools.partial(step, 1))
 
 
 def base_kernel(turned, *refs):
@@ -199,21 +212,29 @@
     swap_x = [(d, d ^ 2) for d in range(4)]
     swap_core = [(d, d ^ 1) for d in range(4)]
 
-    wide = width // 2
+    wide = HALF
     pieces = [lax.reduce_precision(route_weight[0].T, 8, 7)]
     pieces.append(lax.reduce_precision(route_weight[0].T - pieces[0], 8, 7))
     pieces.append(route_weight[0].T - pieces[0] - pieces[1])
-    own = call(
+    step = 128
+    count = tokens // step
+    packed = call(
         pack_kernel,
         "pack",
-        (),
+        (count + 1,),
         (),
         (cotangent, routing[0].T, jnp.concatenate(pieces, axis=0)),
-        [pl.BlockSpec(memory_space=pltpu.VMEM)] * 3,
-        (shape((tokens + 16, wide), jnp.bfloat16), shape((tokens, wide), jnp.bfloat16)),
-        (pl.BlockSpec(memory_space=pltpu.VMEM),) * 2,
-        moved=8 * tokens * width,
-    )
+        [
+            pl.BlockSpec((1, step, wide), lambda i: (0, jnp.minimum(i, count - 1), 0)),
+            pl.BlockSpec((2, tokens), lambda i: (0, 0)),
+            pl.BlockSpec((6, tokens), lambda i: (0, 0)),
+        ],
+        shape((tokens + 16, wide), jnp.bfloat16),
+        pl.BlockSpec((step, wide), lambda i: (i, 0)),
+        moved=4 * tokens * width,
+        limit=PACK_LIMIT,
+    )
+    own = [packed, cotangent[0, :, wide:]]
 
     def permuted(parts, way):
         return [lax.ppermute(p, "expert", way) for p in parts]
@@ -239,27 +260,28 @@
             flops=10 * capacity * tokens,
         )
 
-    def pick(table, near, far, offset, columns, tile):
-        halves, steps = len(near), columns // tile
-        each, start = steps // halves, offset // tile
+    def pick(table, near, far, offset, columns, tile=TILE, claim=0, late=0):
+        steps, start = columns // tile, offset // tile
+        counts = [p.shape[1] // tile for p in near] if len(near) > 1 else [steps]
+        firsts = [sum(counts[:h]) for h in range(len(counts))]
         specs = [
             pl.BlockSpec((2 * capacity, tokens), lambda i, m: (0, 0)),
             pl.BlockSpec((2 * capacity, 1), lambda i, m: (0, 0)),
         ]
 
         def place(h, i):
-            return jnp.clip(i - h * each, 0, each - 1) if halves > 1 else i
-
-        for h in range(halves):
+            return jnp.clip(i - firsts[h], 0, counts[h] - 1) if len(counts) > 1 else i
+
+        for h in range(len(near)):
             if far:
                 specs.append(pl.BlockSpec((tokens, tile), lambda i, m, h=h: (0, (start + place(h, i)) * m[0])))
             else:
                 specs.append(pl.BlockSpec((tokens, tile), lambda i, m, h=h: (0, start + place(h, i))))
         for h in range(len(far)):
-            specs.append(pl.BlockSpec((tokens, tile), lambda i, m, h=h: (0, place(h, i) * (1 - m[0]))))
+            specs.append(pl.BlockSpec((tokens, tile), lambda i, m, h=h: (0, (late // tile + place(h, i)) * (1 - m[0]))))
         out = shape((capacity, columns), jnp.bfloat16)
         mine, other = call(
-            functools.partial(pick_kernel, halves, bool(far)),
+            functools.partial(pick_kernel, firsts, bool(far)),
             "pick",
             (steps,),
             (middle,),
@@ -267,7 +289,7 @@
             specs,
             (out, out),
             (pl.BlockSpec((capacity, tile), lambda i, m: (0, i)),) * 2,
-            flops=4 * capacity * tokens * columns,
+            flops=4 * capacity * tokens * columns + claim * COST,
             moved=4 * (tokens + capacity) * columns,
         )
         return mine, other, lax.ppermute(other, "expert", swap_y)
@@ -298,7 +320,7 @@
             moved=hidden_width * width + 6 * capacity * hidden_width + 2 * capacity * width,
         )
 
-    mine0, other0, got0 = pick(tables(own[0]), own, (), 0, width, 512)
+    mine0, other0, got0 = pick(tables(own[0]), own, (), 0, width)
     turned = call(
         hidden_kernel,
         "hidden",
@@ -313,83 +335,105 @@
         flops=40 * slots * hidden_width,
     )
     grad_preact = back(0, [mine0], None)
+    pair[0], middle_one[0], grad_preact, turned = after(pair[0], middle_one[0], grad_preact, turned)
     middle_two = permuted(pair[:1], swap_middle)
     end_one = permuted(middle_one[:1], to_end)
     grad_preact = back(1, [got0], grad_preact)
-    pair[1], middle_one[1], grad_preact, turned = after(pair[1], middle_one[1], grad_preact, turned)
+    pair[1], middle_one[1], grad_preact = after(pair[1], middle_one[1], grad_preact)
     middle_two += permuted(pair[1:], swap_middle)
     end_one += permuted(middle_one[1:], to_end)
-    mine1, other1, got1 = pick(tables(pair[0]), pair, (), 0, width, 512)
+    mine1, other1, got1 = pick(tables(pair[0]), pair, (), 0, width)
     grad_preact = back(2, [mine1], grad_preact)
+    middle_two[0], end_one[0], grad_preact, got1 = after(middle_two[0], end_one[0], grad_preact, got1)
 
     chunks = CHUNKS
-    ends = []
-    for offset, columns in chunks:
-        half, inner = offset // wide, offset % wide
-        count = tokens if offset else tokens + 16
-        ends.append(lax.ppermute(middle_two[half][:count, inner : inner + columns], "expert", to_end))
-    grad_preact = back(3, [got1], grad_preact)
-    end_one[1], grad_preact = after(end_one[1], grad_preact)
-    mine2, other2, got2 = pick(tables(middle_one[0], end_one[0]), middle_one, end_one, 0, width, 512)
-    grad_preact = back(4, [mine2], grad_preact)
-    ends[0], grad_preact = after(ends[0], grad_preact)
-    last_table = tables(middle_two[0], ends[0])
+
     early = 6 * capacity
 
-    def base_product(got2):
+    def base_product(half, mine2, got2):
+        columns = mine2.shape[1]
+        start = half * wide // TILE
+        full = pl.BlockSpec((capacity, TILE), lambda i: (0, start + i))
+        part = pl.BlockSpec((capacity, TILE), lambda i: (0, i))
         return call(
             base_kernel,
             "base",
-            (4,),
+            (columns // TILE,),
             (),
             (turned, mine0, got0, mine1, got1, mine2, got2),
-            [pl.BlockSpec((hidden_width, early), lambda i: (0, 0))]
-            + [pl.BlockSpec((capacity, width // 4), lambda i: (0, i))] * 6,
-            shape((hidden_width, width), jnp.float32),
-            pl.BlockSpec((hidden_width, width // 4), lambda i: (0, i)),
-            flops=2 * hidden_width * early * width,
-            moved=2 * (hidden_width * early + early * width) + 4 * hidden_width * width,
-        )
-
-    def last_block(chunk, end_two):
+            [pl.BlockSpec((hidden_width, early), lambda i: (0, 0))] + [full] * 4 + [part] * 2,
+            shape((hidden_width, columns), jnp.float32),
+            pl.BlockSpec((hidden_width, TILE), lambda i: (0, i)),
+            flops=2 * hidden_width * early * columns,
+            moved=2 * (hidden_width * early + early * columns) + 4 * hidden_width * columns,
+        )
+
+    def to_ends(half):
+        sent = []
+        for offset, columns in SENT:
+            if (offset >= wide) == half:
+                inner = offset - wide * half
+                count = tokens if offset else tokens + 16
+                sent.append(lax.ppermute(middle_two[half][:count, inner : inner + columns], "expert", to_end))
+        return sent
+
+    ends = to_ends(0)
+    table2 = tables(middle_one[0], end_one[0])
+    mine2, other2, got2 = pick(table2, middle_one[:1], end_one[:1], 0, wide, wide // 2)
+    mine2, got2 = [mine2], [got2]
+    grad_preact = back(3, [got1], grad_preact)
+    middle_two[1], end_one[1], grad_preact, other2 = after(middle_two[1], end_one[1], grad_preact, other2)
+    ends += to_ends(1)
+    mine2b, other2, got2b = pick(table2, middle_one[1:], end_one[1:], 0, width - wide, width - wide)
+    mine2.append(mine2b)
+    got2.append(got2b)
+    grad_preact = back(4, mine2, grad_preact)
+    bases = [base_product(0, mine2[0], got2[0])]
+    ends[0], grad_preact, bases[0] = after(ends[0], grad_preact, bases[0])
+    last_table = tables(middle_two[0], ends[0])
+
+    def last_block(k, chunk, end_two):
         offset, columns = chunk
-        half, inner = offset // wide, offset % wide
-        return pick(last_table, middle_two[half : half + 1], (end_two,), inner, columns, columns)
+        half = offset >= wide
+        inner = offset - wide * half
+        late = offset - SENT[k][0]
+        return pick(last_table, (middle_two[half],), (end_two,), inner, columns, claim=CLAIM, late=late)
 
     def product(chunk, mine3, got3):
         offset, columns = chunk
-        column = offset // columns
+        side = int(offset >= wide)
+        start = (offset - wide * side) // TILE
         half = shape((2 * rows, columns), jnp.bfloat16)
-        part = pl.BlockSpec((capacity, columns), lambda i: (0, 0))
+        part = pl.BlockSpec((capacity, TILE), lambda i: (0, i))
         return call(
             product_kernel,
             "product",
-            (1,),
+            (columns // TILE,),
             (),
-            (base, turned, mine3, got3),
+            (bases[side], turned, mine3, got3),
             [
-                pl.BlockSpec((hidden_width, columns), lambda i: (0, column)),
+                pl.BlockSpec((hidden_width, TILE), lambda i: (0, start + i)),
                 pl.BlockSpec((hidden_width, 2 * capacity), lambda i: (0, 3)),
                 part,
                 part,
             ],
             (half, half),
-            (pl.BlockSpec((2 * rows, columns), lambda i: (0, 0)),) * 2,
+            (pl.BlockSpec((2 * rows, TILE), lambda i: (0, i)),) * 2,
             flops=4 * hidden_width * capacity * columns,
             moved=4 * hidden_width * capacity + 6 * hidden_width * columns,
         )
 
     def adam(chunk, keep, near, far, previous):
         offset, columns = chunk
-        column = offset // columns
-        state = pl.BlockSpec((1, rows, columns), lambda i: (0, 0, column))
-        second = pl.BlockSpec((rows, columns), lambda i: (1, 0))
-        whole = pl.BlockSpec((rows, columns), lambda i: (0, 0))
+        start = offset // TILE
+        state = pl.BlockSpec((1, rows, TILE), lambda i: (0, 0, start + i))
+        second = pl.BlockSpec((rows, TILE), lambda i: (1, i))
+        whole = pl.BlockSpec((rows, TILE), lambda i: (0, i))
         out_state = shape(master.shape, jnp.float32)
         return call(
             adam_kernel,
             "adam",
-            (1,),
+            (columns // TILE,),
             (),
             (keep, near, far, master, moment1, moment2, *previous),
             [second, second, whole, state, state, state] + [ANY] * len(previous),
@@ -402,27 +446,26 @@
 
     def assemble(chunk, fresh, crossed, sibling, last):
         offset, columns = chunk
-        column = offset // columns
+        start = offset // TILE
         return call(
             assemble_kernel,
             "assemble",
-            (1,),
+            (columns // TILE,),
             (groups,),
             (fresh, crossed, sibling, *last),
             [
-                pl.BlockSpec((rows, columns), lambda i, g: (0, 0)),
-                pl.BlockSpec((rows, columns), lambda i, g: (0, 0)),
-                pl.BlockSpec((2 * rows, columns), lambda i, g: (0, 0)),
+                pl.BlockSpec((rows, TILE), lambda i, g: (0, i)),
+                pl.BlockSpec((rows, TILE), lambda i, g: (0, i)),
+                pl.BlockSpec((2 * rows, TILE), lambda i, g: (0, i)),
             ]
             + [ANY] * len(last),
             shape((1, hidden_width, width), jnp.bfloat16),
-            pl.BlockSpec((1, hidden_width, columns), lambda i, g: (0, 0, column)),
+            pl.BlockSpec((1, hidden_width, TILE), lambda i, g: (0, 0, start + i)),
             aliases={3: 0} if last else None,
             moved=16 * rows * columns,
         )
 
     states, next_weight = (), ()
-    total = len(chunks)
     mines, gots, others3 = [], [], []
     sends, keeps, nears, acrosses, fars = {}, {}, {}, {}, {}
     freshes, crosseds, siblings = {}, {}, {}
@@ -459,31 +502,52 @@
         next_weight = (assemble(chunks[k], freshes[k], crosseds[k], tied(siblings[k], token), next_weight),)
         return next_weight[0]
 
-    stages = (sum_core, sum_x, update, gather_core, gathered)
-    for k in range(total):
-        mine3, other3, got3 = last_block(chunks[k], ends[k])
+    def arrive(k, chunk):
+        mine3, other3, got3 = last_block(k, chunks[chunk], ends[k])
         mines.append(mine3)
         gots.append(got3)
-        done = []
-        if k == 0:
-            got2, _ = after(got2, other3)
-            grad_preact = back(5, [got2], grad_preact)
-            done = [grad_preact, base_product(got2)]
-            base = done[1]
-        for lag, stage in enumerate(stages):
-            if k - 1 - lag >= 0:
-                done.append(stage(k - 1 - lag, other3))
-        if k + 1 < total:
-            ends[k + 1], *done = after(ends[k + 1], *done)
-            if k == 0:
-                grad_preact, base = done
+        return other3
+
+    other = arrive(0, 0)
+    got2[1], _ = after(got2[1], other)
+    bases.append(base_product(1, mine2[1], got2[1]))
+    sum_core(0, bases[1])
+    if EARLY:
+        across = sum_x(0, None)
+        ends[1], across = after(ends[1], across)
+    else:
+        ends[1], send = after(ends[1], sends[0])
+    other = arrive(1, 1)
+    if not EARLY:
+        other = sum_x(0, other)
+    fresh = update(0, other)
+    got2[1], fresh = after(got2[1], fresh)
+    grad_preact = back(5, got2, grad_preact)
+    sum_core(1, grad_preact)
+    ends[2], send = after(ends[2], sends[1])
+    across = sum_x(1, ends[2])
+    ends[2], across = after(ends[2], across)
+    arrive(2, 2)
+    other = arrive(2, 3)
+    both = gather_core(0, other)
+    fresh = update(1, both)
+    send = sum_core(2, fresh)
+    send = sum_core(3, send)
+    across = sum_x(2, send)
+    across = sum_x(3, across)
+    mines[0], _ = after(mines[0], across)
     grad_preact = back(6, mines, grad_preact)
-    for k in range(total, total + len(stages)):
-        for lag, stage in reversed(tuple(enumerate(stages))):
-            if 0 <= k - 1 - lag < total:
-                stage(k - 1 - lag, None)
-    gots[-1], _ = after(gots[-1], acrosses[total - 1])
+    placed = gathered(0, grad_preact)
+    fresh = update(2, placed)
+    fresh = update(3, fresh)
+    both = gather_core(1, fresh)
+    gots[0], _ = after(gots[0], both)
     grad_preact = back(7, gots, grad_preact)
+    placed = gathered(1, grad_preact)
+    both = gather_core(2, placed)
+    gather_core(3, both)
+    gathered(2, None)
+    gathered(3, None)
     return (grad_preact, next_weight[0], *states)
 
 

time: 215 us -> 192 us (0.89)
  waiting for transfers between devices: 97 us -> 60.3 us
  Pallas kernels: 66.5 us -> 78.3 us
    ppermute x4 -> x3, waiting for transfers between devices: 16.9 us -> 4.9 us  [to_ends(): lax.ppermute(middle_two[half][:count, inner:inner + columns], 'expert', t...]
    pallas_call x34 -> x36, Pallas kernels: 66.5 us -> 78.3 us  [call(): pl.pallas_call(kernel, name=name, grid_spec=pltpu.PrefetchScalarGridSpec(...]
    ppermute x7 -> x8, waiting for transfers between devices: 36 us -> 24.5 us  [pick(): return (mine, other, lax.ppermute(other, 'expert', swap_y))]
    ppermute x8, waiting for transfers between devices: 25.9 us -> 15.2 us  [permuted(): return [lax.ppermute(p, 'expert', way) for p in parts]]
    ppermute x7 -> x8, starting transfers between devices: 9.01 us -> 13.3 us  [pick(): return (mine, other, lax.ppermute(other, 'expert', swap_y))]
    ppermute x4, waiting for transfers between devices: 8.34 us -> 4.18 us  [update(): crosseds[k] = lax.ppermute(freshes[k], 'dp', swap_x)]
    ppermute x4, starting transfers between devices: 8.93 us -> 5.14 us  [update(): crosseds[k] = lax.ppermute(freshes[k], 'dp', swap_x)]
    squeeze x0 -> x1, local copies, waits for them, and re-layouts: none -> 2.22 us  [line_body(): own = [packed, cotangent[0, :, wide:]]]
  transfers between devices with their start and end apart: 35 -> 35, of which waited for: 15 -> 17; matrix products, arithmetic and copies ran while one was open for 0% -> 1% of each run, Pallas kernels for 30% -> 38%
where the time goes in v3:
time: 192 us; the launch traced here: 191 us
  Pallas kernels  78.3 us (41%)
  waiting for transfers between devices  60.3 us (31%)
  starting transfers between devices  43.3 us (23%)
  local copies, waits for them, and re-layouts  6.62 us (3%)
    pallas_call x36, Pallas kernels, call(): pl.pallas_call(kernel, name=name, grid_spec=pltpu.PrefetchScalarGridSpec(...  78.3 us
    ppermute x8, waiting for transfers between devices, pick(): return (mine, other, lax.ppermute(other, 'expert', swap_y))  24.5 us
    ppermute x8, waiting for transfers between devices, permuted(): return [lax.ppermute(p, 'expert', way) for p in parts]  15.2 us
    ppermute x8, starting transfers between devices, permuted(): return [lax.ppermute(p, 'expert', way) for p in parts]  13.7 us
    ppermute x8, starting transfers between devices, pick(): return (mine, other, lax.ppermute(other, 'expert', swap_y))  13.3 us
    ppermute x4, waiting for transfers between devices, sum_x(): fars[k] = lax.ppermute(acrosses[k], 'dp', swap_x)  11 us
    ppermute x4, starting transfers between devices, sum_x(): fars[k] = lax.ppermute(acrosses[k], 'dp', swap_x)  6.02 us
    ppermute x4, starting transfers between devices, update(): crosseds[k] = lax.ppermute(freshes[k], 'dp', swap_x)  5.14 us
  transfers between devices with their start and end apart: 35, of which 17 were waited for; matrix products, arithmetic and copies ran while one was open for 1% of the time, Pallas kernels for 38%

profile of v3, /device:TPU:0, one launch (start us, length us, event | category | flops | bytes accessed | tf_op | source)
XLA Modules:
  0.0 191.3 jit_solution(5375888882803948963)
XLA Ops:
  1.9 3.6 %pack.1.refs_0_ = bf16[528,1280]{1,0:T(8,128)(2,1)} custom-call(bf16[1,512,2048]{2,1,0:T(8,128)(2,1)} %tokens.1, s32[2,512]{1,0:T(2,128)} %bitcast.35, f32[6,512]{1,0:T(8,128)} %pad_maximum_fusion.1.weights), custom_call_target="tpu_custom_call" | custom-call | bytes 1024 | tf_op jit(solution)/shard_map/pack/pallas_call | solution.py:36
  5.6 3.0 %collective-permute-start = (bf16[528,1280]{1,0:T(8,128)(2,1)}, bf16[528,1280]{1,0:T(8,128)(2,1)}, u32[]{:S(2)}, u32[]{:S(2)}) collective-permute-start(bf16[528,1280]{1,0:T(8,128)(2,1)} %pack.1.refs_0_), channel_id=1, source_target_pairs={{0,8},{4,12},{8,0},{12,4},{16,24},{20,28},{24,16},{28,20},{1,9},{5... | collective-permute-start | bytes 4055048 | tf_op jit(solution)/shard_map/ppermute | solution.py:240
  14.9 5.9 %pick.8 = (bf16[256,2048]{1,0:T(8,128)(2,1)S(1)}, bf16[256,2048]{1,0:T(8,128)(2,1)}) custom-call(s32[1]{0:T(128)} %bitcast.8.middle, bf16[512,512]{1,0:T(8,128)(2,1)S(1)} %get-tuple-element.95.picks, f32[512,1]{1,0:T(8,128)S(1)} %get-tuple-element.96.scales, bf16[528,1280]{1,0:T(8,128)(2,1)S(1)} %copy-done.5, bf16[512,768]{1,0:T(8,128)(2,1)} %slice_bitcast_fusion.refs_1_), custom_call_target="tpu_custom_call" | custom-call | flops 262144 | bytes 1536 | tf_op jit(solution)/shard_map/pick/pallas_call | solution.py:36
  22.3 3.3 %collective-permute-start.4 = (bf16[512,768]{1,0:T(8,128)(2,1)}, bf16[512,768]{1,0:T(8,128)(2,1)}, u32[]{:S(2)}, u32[]{:S(2)}) collective-permute-start(bf16[512,768]{1,0:T(8,128)(2,1)} %slice_bitcast_fusion.refs_1_), channel_id=1, source_target_pairs={{0,8},{4,12},{8,0},{12,4},{16,24},{20,28},{24,16},{28,20},{1,9},{5... | collective-permute-start | bytes 2359304 | tf_op jit(solution)/shard_map/ppermute | solution.py:240
  27.4 2.8 %copy-done = bf16[1,1,2048,1536]{3,2,1,0:T(8,128)(2,1)S(1)} copy-done((bf16[1,1,2048,1536]{3,2,1,0:T(8,128)(2,1)S(1)}, bf16[1,1,2048,1536]{3,2,1,0:T(8,128)(2,1)}, u32[]{:S(2)}) %copy-start) | copy-done | bytes 6291480
  30.2 3.2 %hidden.1.turned = bf16[768,2048]{1,0:T(8,128)(2,1)S(1)} custom-call(s32[8]{0:T(128)S(1)} %stack.59.order, s32[4]{0:T(128)S(1)} %pad_add_fusion.1.groups.places, bf16[1,1,2048,1536]{3,2,1,0:T(8,128)(2,1)S(1)} %copy-done), custom_call_target="tpu_custom_call" | custom-call | flops 15360 | bytes 3456 | tf_op jit(solution)/shard_map/hidden/pallas_call | solution.py:36
  36.1 3.4 %collective-permute-done.refs_0_ = bf16[528,1280]{1,0:T(8,128)(2,1)} collective-permute-done((bf16[528,1280]{1,0:T(8,128)(2,1)}, bf16[528,1280]{1,0:T(8,128)(2,1)}, u32[]{:S(2)}, u32[]{:S(2)}) %collective-permute-start) | collective-permute-done | bytes 1351712 | tf_op jit(solution)/shard_map/ppermute | solution.py:240
  45.7 3.8 %back.9.refs_3_ = bf16[1,1,2048,1536]{3,2,1,0:T(8,128)(2,1)} custom-call(s32[8]{0:T(128)S(1)} %stack.59.order, bf16[256,2048]{1,0:T(8,128)(2,1)} %collective-permute-done.6.refs_0_.refs_1_, bf16[1,768,2048]{2,1,0:T(8,128)(2,1)S(1)} %copy-done.1, bf16[1,1,2048,1536]{3,2,1,0:T(8,128)(2,1)S(1)} %bitcast.34, ...), custom_call_target="tpu_custom_call", output_to_operand_aliasing={{}: (4, {})} | custom-call | flops 196608 | bytes 928 | tf_op jit(solution)/shard_map/back/pallas_call | solution.py:36
  49.5 6.7 %collective-permute-done.4.refs_1_ = bf16[512,768]{1,0:T(8,128)(2,1)} collective-permute-done((bf16[512,768]{1,0:T(8,128)(2,1)}, bf16[512,768]{1,0:T(8,128)(2,1)}, u32[]{:S(2)}, u32[]{:S(2)}) %collective-permute-start.4) | collective-permute-done | bytes 786464 | tf_op jit(solution)/shard_map/ppermute | solution.py:240
  56.3 5.7 %pick.9 = (bf16[256,2048]{1,0:T(8,128)(2,1)S(1)}, bf16[256,2048]{1,0:T(8,128)(2,1)S(1)}) custom-call(s32[1]{0:T(128)} %bitcast.8.middle, bf16[512,512]{1,0:T(8,128)(2,1)S(1)} %get-tuple-element.100.picks, f32[512,1]{1,0:T(8,128)S(1)} %get-tuple-element.101.scales, bf16[528,1280]{1,0:T(8,128)(2,1)} %collective-permute-done.refs_0_, ...), custom_call_target="tpu_custom_call" | custom-call | flops 262144 | bytes 1536 | tf_op jit(solution)/shard_map/pick/pallas_call | solution.py:36
  66.1 2.6 %back.10.refs_3_ = bf16[1,1,2048,1536]{3,2,1,0:T(8,128)(2,1)} custom-call(s32[8]{0:T(128)S(1)} %stack.59.order, bf16[256,2048]{1,0:T(8,128)(2,1)S(1)} %get-tuple-element.105.refs_0_.refs_2_, bf16[1,768,2048]{2,1,0:T(8,128)(2,1)S(1)} %copy-done.1, bf16[1,1,2048,1536]{3,2,1,0:T(8,128)(2,1)S(1)} %bitcast.34, ...), custom_call_target="tpu_custom_call", output_to_operand_aliasing={{}: (4, {})} | custom-call | flops 196608 | bytes 928 | tf_op jit(solution)/shard_map/back/pallas_call | solution.py:36
  68.7 16.9 %collective-permute-done.7.refs_0_.refs_3_ = bf16[256,2048]{1,0:T(8,128)(2,1)S(1)} collective-permute-done((bf16[256,2048]{1,0:T(8,128)(2,1)S(1)}, bf16[256,2048]{1,0:T(8,128)(2,1)S(1)}, u32[]{:S(2)}, u32[]{:S(2)}) %collective-permute-start.7) | collective-permute-done | bytes 1048608 | tf_op jit(solution)/shard_map/ppermute | solution.py:295
  96.8 5.2 %collective-permute-done.10.refs_1_ = bf16[512,768]{1,0:T(8,128)(2,1)S(1)} collective-permute-done((bf16[512,768]{1,0:T(8,128)(2,1)}, bf16[512,768]{1,0:T(8,128)(2,1)S(1)}, u32[]{:S(2)}, u32[]{:S(2)}) %collective-permute-start.10) | collective-permute-done | bytes 786464 | tf_op jit(solution)/shard_map/ppermute | solution.py:240
  105.8 2.6 %back.12.refs_4_ = bf16[1,1,2048,1536]{3,2,1,0:T(8,128)(2,1)} custom-call(s32[8]{0:T(128)S(1)} %stack.59.order, bf16[256,1280]{1,0:T(8,128)(2,1)S(1)} %get-tuple-element.112.refs_0_.refs_4_, bf16[256,768]{1,0:T(8,128)(2,1)S(1)} %get-tuple-element.118.refs_1_.refs_4_, bf16[1,768,2048]{2,1,0:T(8,128)(2,1)S(1)} %copy-done.1, ...), custom_call_target="tpu_custom_call", output_to_operand_aliasing={{}: (5, {})} | custom-call | flops 196608 | bytes 928 | tf_op jit(solution)/shard_map/back/pallas_call | solution.py:36
  108.4 5.3 %base.2 = f32[768,1280]{1,0:T(8,128)S(1)} custom-call(bf16[768,2048]{1,0:T(8,128)(2,1)S(1)} %hidden.1.turned, bf16[256,2048]{1,0:T(8,128)(2,1)S(1)} %get-tuple-element.97.refs_0_, bf16[256,2048]{1,0:T(8,128)(2,1)} %collective-permute-done.6.refs_0_.refs_1_, bf16[256,2048]{1,0:T(8,128)(2,1)S(1)} %get-tuple-element.105.refs_0_.refs_2_, ...), custom_call_target="tpu_custom_call" | custom-call | flops 737280 | bytes 2496 | tf_op jit(solution)/shard_map/base/pallas_call | solution.py:36
  117.4 3.5 %base.3 = f32[768,768]{1,0:T(8,128)S(1)} custom-call(bf16[768,2048]{1,0:T(8,128)(2,1)S(1)} %hidden.1.turned, bf16[256,2048]{1,0:T(8,128)(2,1)S(1)} %get-tuple-element.97.refs_0_, bf16[256,2048]{1,0:T(8,128)(2,1)} %collective-permute-done.6.refs_0_.refs_1_, bf16[256,2048]{1,0:T(8,128)(2,1)S(1)} %get-tuple-element.105.refs_0_.refs_2_, ...), custom_call_target="tpu_custom_call" | custom-call | flops 442368 | bytes 1728 | tf_op jit(solution)/shard_map/base/pallas_call | solution.py:36
  124.7 4.9 %collective-permute-done.13.refs_1_ = bf16[512,768]{1,0:T(8,128)(2,1)S(1)} collective-permute-done((bf16[512,768]{1,0:T(8,128)(2,1)S(1)}, bf16[512,768]{1,0:T(8,128)(2,1)S(1)}, u32[]{:S(2)}, u32[]{:S(2)}) %collective-permute-start.13) | collective-permute-done | bytes 786464 | tf_op jit(solution)/shard_map/ppermute | solution.py:377
  130.7 2.8 %collective-permute-start.15 = (bf16[256,768]{1,0:T(8,128)(2,1)S(1)}, bf16[256,768]{1,0:T(8,128)(2,1)S(1)}, u32[]{:S(2)}, u32[]{:S(2)}) collective-permute-start(bf16[256,768]{1,0:T(8,128)(2,1)S(1)} %get-tuple-element.133), channel_id=1, source_target_pairs={{0,4},{4,0},{8,12},{12,8},{16,20},{20,16},{24,28},{28,24},{1,5},{5... | collective-permute-start | bytes 1179656 | tf_op jit(solution)/shard_map/ppermute | solution.py:295
  135.2 4.2 %collective-permute-done.17.far = bf16[192,512]{1,0:T(8,128)(2,1)S(1)} collective-permute-done((bf16[192,512]{1,0:T(8,128)(2,1)S(1)}, bf16[192,512]{1,0:T(8,128)(2,1)S(1)}, u32[]{:S(2)}, u32[]{:S(2)}) %collective-permute-start.17) | collective-permute-done | bytes 196640 | tf_op jit(solution)/shard_map/ppermute | solution.py:485
  140.8 2.6 %back.13.refs_6_ = bf16[1,1,2048,1536]{3,2,1,0:T(8,128)(2,1)} custom-call(s32[8]{0:T(128)S(1)} %stack.59.order, bf16[256,1280]{1,0:T(8,128)(2,1)S(1)} %collective-permute-done.11.refs_5_.refs_0_, bf16[256,768]{1,0:T(8,128)(2,1)S(1)} %collective-permute-done.14.refs_5_.refs_1_, bf16[1,768,2048]{2,1,0:T(8,128)(2,1)S(1)} %copy-done.1, ...), custom_call_target="tpu_custom_call", output_to_operand_aliasing={{}: (5, {})} | custom-call | flops 196608 | bytes 928 | tf_op jit(solution)/shard_map/back/pallas_call | solution.py:36
  152.8 5.9 %collective-permute-done.20.far = bf16[192,768]{1,0:T(8,128)(2,1)S(1)} collective-permute-done((bf16[192,768]{1,0:T(8,128)(2,1)S(1)}, bf16[192,768]{1,0:T(8,128)(2,1)S(1)}, u32[]{:S(2)}, u32[]{:S(2)}) %collective-permute-start.20) | collective-permute-done | bytes 294944 | tf_op jit(solution)/shard_map/ppermute | solution.py:485
  163.9 3.9 %collective-permute-done.23.got.refs_3_ = bf16[256,256]{1,0:T(8,128)(2,1)S(1)} collective-permute-done((bf16[256,256]{1,0:T(8,128)(2,1)S(1)}, bf16[256,256]{1,0:T(8,128)(2,1)S(1)}, u32[]{:S(2)}, u32[]{:S(2)}) %collective-permute-start.23) | collective-permute-done | bytes 131104 | tf_op jit(solution)/shard_map/ppermute | solution.py:295
  171.3 2.6 %back.14.refs_6_ = bf16[1,1,2048,1536]{3,2,1,0:T(8,128)(2,1)} custom-call(s32[8]{0:T(128)S(1)} %stack.59.order, bf16[256,512]{1,0:T(8,128)(2,1)S(1)} %get-tuple-element.165.mine.refs_0_, bf16[256,768]{1,0:T(8,128)(2,1)S(1)} %get-tuple-element.132.mine.refs_1_, bf16[256,512]{1,0:T(8,128)(2,1)S(1)} %get-tuple-element.155.mine.refs_2_, ...), custom_call_target="tpu_custom_call", output_to_operand_aliasing={{}: (7, {})} | custom-call | flops 196608 | bytes 928 | tf_op jit(solution)/shard_map/back/pallas_call | solution.py:36
  180.9 2.6 %back.15 = bf16[1,1,2048,1536]{3,2,1,0:T(8,128)(2,1)} custom-call(s32[8]{0:T(128)S(1)} %stack.59.order, bf16[256,512]{1,0:T(8,128)(2,1)S(1)} %collective-permute-done.12.got.refs_0_, bf16[256,768]{1,0:T(8,128)(2,1)S(1)} %collective-permute-done.15.got.refs_1_, ...), custom_call_target="tpu_custom_call", output_to_operand_aliasing={{}: (7, {})} | custom-call | flops 196608 | bytes 928 | tf_op jit(solution)/shard_map/back/pallas_call | solution.py:36
  (118 shorter events, 83.1 us)
Async XLA Ops:
  5.6 33.8 %collective-permute-start = (bf16[528,1280]{1,0:T(8,128)(2,1)}, bf16[528,1280]{1,0:T(8,128)(2,1)}, u32[]{:S(2)}, u32[]{:S(2)}) collective-permute-start(bf16[528,1280]{1,0:T(8,128)(2,1)} %pack.1.refs_0_), channel_id=1, source_target_pairs={{0,8},{4,12},{8,0},{12,4},{16,24},{20,28},{24,16},{28,20},{1,9},{5... | collective-permute-start | bytes 4055048 | tf_op jit(solution)/shard_map/ppermute | solution.py:240
  8.6 30.8 %collective-permute-start.1 = (bf16[528,1280]{1,0:T(8,128)(2,1)}, bf16[528,1280]{1,0:T(8,128)(2,1)}, u32[]{:S(2)}, u32[]{:S(2)}) collective-permute-start(bf16[528,1280]{1,0:T(8,128)(2,1)} %pack.1.refs_0_), channel_id=1, source_target_pairs={{8,16},{16,8},{12,20},{20,12},{9,17},{17,9},{13,21},{21,13},{10,18... | collective-permute-start | bytes 4055048 | tf_op jit(solution)/shard_map/ppermute | solution.py:240
  20.8 24.9 %collective-permute-start.6 = (bf16[256,2048]{1,0:T(8,128)(2,1)}, bf16[256,2048]{1,0:T(8,128)(2,1)}, u32[]{:S(2)}, u32[]{:S(2)}) collective-permute-start(bf16[256,2048]{1,0:T(8,128)(2,1)} %get-tuple-element.102), channel_id=1, source_target_pairs={{0,4},{4,0},{8,12},{12,8},{16,20},{20,16},{24,28},{28,24},{1,5},{5... | collective-permute-start | bytes 3145736 | tf_op jit(solution)/shard_map/ppermute | solution.py:295
  22.3 33.9 %collective-permute-start.4 = (bf16[512,768]{1,0:T(8,128)(2,1)}, bf16[512,768]{1,0:T(8,128)(2,1)}, u32[]{:S(2)}, u32[]{:S(2)}) collective-permute-start(bf16[512,768]{1,0:T(8,128)(2,1)} %slice_bitcast_fusion.refs_1_), channel_id=1, source_target_pairs={{0,8},{4,12},{8,0},{12,4},{16,24},{20,28},{24,16},{28,20},{1,9},{5... | collective-permute-start | bytes 2359304 | tf_op jit(solution)/shard_map/ppermute | solution.py:240
  25.7 30.6 %collective-permute-start.5 = (bf16[512,768]{1,0:T(8,128)(2,1)}, bf16[512,768]{1,0:T(8,128)(2,1)}, u32[]{:S(2)}, u32[]{:S(2)}) collective-permute-start(bf16[512,768]{1,0:T(8,128)(2,1)} %slice_bitcast_fusion.refs_1_), channel_id=1, source_target_pairs={{8,16},{16,8},{12,20},{20,12},{9,17},{17,9},{13,21},{21,13},{10,18... | collective-permute-start | bytes 2359304 | tf_op jit(solution)/shard_map/ppermute | solution.py:240
  39.4 46.2 %collective-permute-start.2 = (bf16[528,1280]{1,0:T(8,128)(2,1)}, bf16[528,1280]{1,0:T(8,128)(2,1)S(1)}, u32[]{:S(2)}, u32[]{:S(2)}) collective-permute-start(bf16[528,1280]{1,0:T(8,128)(2,1)} %collective-permute-done.refs_0_), channel_id=1, source_target_pairs={{8,16},{16,8},{12,20},{20,12},{9,17},{17,9},{13,21},{21,13},{10,18... | collective-permute-start | bytes 4055048 | tf_op jit(solution)/shard_map/ppermute | solution.py:240
  40.2 45.4 %collective-permute-start.3 = (bf16[528,1280]{1,0:T(8,128)(2,1)}, bf16[528,1280]{1,0:T(8,128)(2,1)S(1)}, u32[]{:S(2)}, u32[]{:S(2)}) collective-permute-start(bf16[528,1280]{1,0:T(8,128)(2,1)} %collective-permute-done.1.refs_0_), channel_id=1, source_target_pairs={{16,24},{20,28},{8,0},{12,4},{17,25},{21,29},{9,1},{13,5},{18,26},... | collective-permute-start | bytes 4055048 | tf_op jit(solution)/shard_map/ppermute | solution.py:240
  62.0 23.6 %collective-permute-start.7 = (bf16[256,2048]{1,0:T(8,128)(2,1)S(1)}, bf16[256,2048]{1,0:T(8,128)(2,1)S(1)}, u32[]{:S(2)}, u32[]{:S(2)}) collective-permute-start(bf16[256,2048]{1,0:T(8,128)(2,1)S(1)} %get-tuple-element.107), channel_id=1, source_target_pairs={{0,4},{4,0},{8,12},{12,8},{16,20},{20,16},{24,28},{28,24},{1,5},{5... | collective-permute-start | bytes 3145736 | tf_op jit(solution)/shard_map/ppermute | solution.py:295
  64.1 32.7 %collective-permute-start.9 = (bf16[512,768]{1,0:T(8,128)(2,1)}, bf16[512,768]{1,0:T(8,128)(2,1)S(1)}, u32[]{:S(2)}, u32[]{:S(2)}) collective-permute-start(bf16[512,768]{1,0:T(8,128)(2,1)} %collective-permute-done.4.refs_1_), channel_id=1, source_target_pairs={{8,16},{16,8},{12,20},{20,12},{9,17},{17,9},{13,21},{21,13},{10,18... | collective-permute-start | bytes 2359304 | tf_op jit(solution)/shard_map/ppermute | solution.py:240
  64.8 37.2 %collective-permute-start.10 = (bf16[512,768]{1,0:T(8,128)(2,1)}, bf16[512,768]{1,0:T(8,128)(2,1)S(1)}, u32[]{:S(2)}, u32[]{:S(2)}) collective-permute-start(bf16[512,768]{1,0:T(8,128)(2,1)} %collective-permute-done.5.refs_0_), channel_id=1, source_target_pairs={{16,24},{20,28},{8,0},{12,4},{17,25},{21,29},{9,1},{13,5},{18,26},... | collective-permute-start | bytes 2359304 | tf_op jit(solution)/shard_map/ppermute | solution.py:240
  89.7 18.6 %collective-permute-start.11 = (bf16[256,1280]{1,0:T(8,128)(2,1)S(1)}, bf16[256,1280]{1,0:T(8,128)(2,1)S(1)}, u32[]{:S(2)}, u32[]{:S(2)}) collective-permute-start(bf16[256,1280]{1,0:T(8,128)(2,1)S(1)} %get-tuple-element.116), channel_id=1, source_target_pairs={{0,4},{4,0},{8,12},{12,8},{16,20},{20,16},{24,28},{28,24},{1,5},{5... | collective-permute-start | bytes 1966088 | tf_op jit(solution)/shard_map/ppermute | solution.py:295
  91.4 22.3 %collective-permute-start.8 = (bf16[528,512]{1,0:T(8,128)(2,1)S(1)}, bf16[528,512]{1,0:T(8,128)(2,1)S(1)}, u32[]{:S(2)}, u32[]{:S(2)}) collective-permute-start(bf16[528,512]{1,0:T(8,128)(2,1)S(1)} %slice.34), channel_id=1, source_target_pairs={{16,24},{20,28},{8,0},{12,4},{17,25},{21,29},{9,1},{13,5},{18,26},... | collective-permute-start | bytes 1622024 | tf_op jit(solution)/shard_map/ppermute | solution.py:377
  92.7 36.8 %collective-permute-start.13 = (bf16[512,768]{1,0:T(8,128)(2,1)S(1)}, bf16[512,768]{1,0:T(8,128)(2,1)S(1)}, u32[]{:S(2)}, u32[]{:S(2)}) collective-permute-start(bf16[512,768]{1,0:T(8,128)(2,1)S(1)} %slice.35), channel_id=1, source_target_pairs={{16,24},{20,28},{8,0},{12,4},{17,25},{21,29},{9,1},{13,5},{18,26},... | collective-permute-start | bytes 2359304 | tf_op jit(solution)/shard_map/ppermute | solution.py:377
  103.7 13.7 %collective-permute-start.14 = (bf16[256,768]{1,0:T(8,128)(2,1)S(1)}, bf16[256,768]{1,0:T(8,128)(2,1)S(1)}, u32[]{:S(2)}, u32[]{:S(2)}) collective-permute-start(bf16[256,768]{1,0:T(8,128)(2,1)S(1)} %get-tuple-element.127), channel_id=1, source_target_pairs={{0,4},{4,0},{8,12},{12,8},{16,20},{20,16},{24,28},{28,24},{1,5},{5... | collective-permute-start | bytes 1179656 | tf_op jit(solution)/shard_map/ppermute | solution.py:295
  123.1 10.5 %collective-permute-start.16 = (bf16[384,512]{1,0:T(8,128)(2,1)S(1)}, bf16[384,512]{1,0:T(8,128)(2,1)S(1)}, u32[]{:S(2)}, u32[]{:S(2)}) collective-permute-start(bf16[384,512]{1,0:T(8,128)(2,1)S(1)} %get-tuple-element.130), channel_id=1, source_target_pairs={{0,1},{1,0},{2,3},{3,2},{4,5},{5,4},{6,7},{7,6},{8,9},{9,8},{10,11... | collective-permute-start | bytes 1179656 | tf_op jit(solution)/shard_map/ppermute | solution.py:478
  123.2 23.4 %collective-permute-start.19 = (bf16[512,768]{1,0:T(8,128)(2,1)S(1)}, bf16[512,768]{1,0:T(8,128)(2,1)S(1)}, u32[]{:S(2)}, u32[]{:S(2)}) collective-permute-start(bf16[512,768]{1,0:T(8,128)(2,1)S(1)} %collective-permute-done.9.refs_0_), channel_id=1, source_target_pairs={{16,24},{20,28},{8,0},{12,4},{17,25},{21,29},{9,1},{13,5},{18,26},... | collective-permute-start | bytes 2359304 | tf_op jit(solution)/shard_map/ppermute | solution.py:377
  130.7 12.6 %collective-permute-start.15 = (bf16[256,768]{1,0:T(8,128)(2,1)S(1)}, bf16[256,768]{1,0:T(8,128)(2,1)S(1)}, u32[]{:S(2)}, u32[]{:S(2)}) collective-permute-start(bf16[256,768]{1,0:T(8,128)(2,1)S(1)} %get-tuple-element.133), channel_id=1, source_target_pairs={{0,4},{4,0},{8,12},{12,8},{16,20},{20,16},{24,28},{28,24},{1,5},{5... | collective-permute-start | bytes 1179656 | tf_op jit(solution)/shard_map/ppermute | solution.py:295
  145.0 7.8 %collective-permute-start.21 = (bf16[192,512]{1,0:T(8,128)(2,1)S(1)}, bf16[192,512]{1,0:T(8,128)(2,1)S(1)}, u32[]{:S(2)}, u32[]{:S(2)}) collective-permute-start(bf16[192,512]{1,0:T(8,128)(2,1)S(1)} %get-tuple-element.137.own), channel_id=1, source_target_pairs={{0,2},{1,3},{2,0},{3,1},{4,6},{5,7},{6,4},{7,5},{8,10},{9,11},{10,... | collective-permute-start | bytes 589832 | tf_op jit(solution)/shard_map/ppermute | solution.py:491
  147.0 11.6 %collective-permute-start.20 = (bf16[192,768]{1,0:T(8,128)(2,1)S(1)}, bf16[192,768]{1,0:T(8,128)(2,1)S(1)}, u32[]{:S(2)}, u32[]{:S(2)}) collective-permute-start(bf16[192,768]{1,0:T(8,128)(2,1)S(1)} %add_convert_fusion), channel_id=1, source_target_pairs={{0,2},{1,3},{2,0},{3,1},{4,6},{5,7},{6,4},{7,5},{8,10},{9,11},{10,... | collective-permute-start | bytes 884744 | tf_op jit(solution)/shard_map/ppermute | solution.py:485
  149.4 11.4 %collective-permute-start.24 = (bf16[256,512]{1,0:T(8,128)(2,1)S(1)}, bf16[256,512]{1,0:T(8,128)(2,1)S(1)}, u32[]{:S(2)}, u32[]{:S(2)}) collective-permute-start(bf16[256,512]{1,0:T(8,128)(2,1)S(1)} %get-tuple-element.156), channel_id=1, source_target_pairs={{0,4},{4,0},{8,12},{12,8},{16,20},{20,16},{24,28},{28,24},{1,5},{5... | collective-permute-start | bytes 786440 | tf_op jit(solution)/shard_map/ppermute | solution.py:295
  162.0 11.9 %collective-permute-start.29 = (bf16[384,512]{1,0:T(8,128)(2,1)S(1)}, bf16[384,512]{1,0:T(8,128)(2,1)S(1)}, u32[]{:S(2)}, u32[]{:S(2)}) collective-permute-start(bf16[384,512]{1,0:T(8,128)(2,1)S(1)} %constant_dynamic-update-slice_fusion), channel_id=1, source_target_pairs={{0,1},{1,0},{2,3},{3,2},{4,5},{5,4},{6,7},{7,6},{8,9},{9,8},{10,11... | collective-permute-start | bytes 1179656 | tf_op jit(solution)/shard_map/ppermute | solution.py:497
  162.4 16.4 %collective-permute-start.22 = (bf16[192,768]{1,0:T(8,128)(2,1)S(1)}, bf16[192,768]{1,0:T(8,128)(2,1)S(1)}, u32[]{:S(2)}, u32[]{:S(2)}) collective-permute-start(bf16[192,768]{1,0:T(8,128)(2,1)S(1)} %get-tuple-element.153.own), channel_id=1, source_target_pairs={{0,2},{1,3},{2,0},{3,1},{4,6},{5,7},{6,4},{7,5},{8,10},{9,11},{10,... | collective-permute-start | bytes 884744 | tf_op jit(solution)/shard_map/ppermute | solution.py:491
  169.9 7.9 %collective-permute-start.27 = (bf16[192,256]{1,0:T(8,128)(2,1)S(1)}, bf16[192,256]{1,0:T(8,128)(2,1)S(1)}, u32[]{:S(2)}, u32[]{:S(2)}) collective-permute-start(bf16[192,256]{1,0:T(8,128)(2,1)S(1)} %add_convert_fusion.3), channel_id=1, source_target_pairs={{0,2},{1,3},{2,0},{3,1},{4,6},{5,7},{6,4},{7,5},{8,10},{9,11},{10,... | collective-permute-start | bytes 294920 | tf_op jit(solution)/shard_map/ppermute | solution.py:485
  180.4 7.9 %collective-permute-start.30 = (bf16[192,256]{1,0:T(8,128)(2,1)S(1)}, bf16[192,256]{1,0:T(8,128)(2,1)S(1)}, u32[]{:S(2)}, u32[]{:S(2)}) collective-permute-start(bf16[192,256]{1,0:T(8,128)(2,1)S(1)} %get-tuple-element.176.own), channel_id=1, source_target_pairs={{0,2},{1,3},{2,0},{3,1},{4,6},{5,7},{6,4},{7,5},{8,10},{9,11},{10,... | collective-permute-start | bytes 294920 | tf_op jit(solution)/shard_map/ppermute | solution.py:491
  (19 other events, 112.9 us)

commit v4 on v3

--- a/solution.py
+++ b/solution.py
@@ -70,20 +70,32 @@
         out[g * rows : (g + 1) * rows, :] = turned[pl.ds(start, rows), :]
 
 
-def pack_kernel(tokens, chosen, weights, packed):
-    last = pl.program_id(0) == pl.num_programs(0) - 1
-
-    @pl.when(jnp.logical_not(last))
-    def _():
-        packed[...] = tokens[0]
-
-    @pl.when(last)
-    def _():
-        length = chosen.shape[1]
-        packed[...] = jnp.zeros_like(packed)
-        packed[:8, :length] = jnp.concatenate([chosen[...].astype(jnp.float32), weights[...]], axis=0).astype(
-            jnp.bfloat16
-        )
+def pack_kernel(tokens, chosen, weights, packed, held, into, out):
+    count, wide = tokens.shape[1], packed.shape[1]
+    parts = 8
+    part = count // parts
+    loads, stores = [], []
+    for k in range(parts):
+        here = pl.ds(k * part, part)
+        loads.append(pltpu.make_async_copy(tokens.at[0, here, pl.ds(0, wide)], held.at[here, :], into.at[k]))
+        stores.append(pltpu.make_async_copy(held.at[here, :], packed.at[here, :], out.at[k]))
+    tail = pl.ds(count, 16)
+    stores.append(pltpu.make_async_copy(held.at[tail, :], packed.at[tail, :], out.at[parts]))
+    for load in loads:
+        load.start()
+    exact = weights[...]
+    high = exact.astype(jnp.bfloat16).astype(jnp.float32)
+    middle = (exact - high).astype(jnp.bfloat16).astype(jnp.float32)
+    low = exact - high - middle
+    info = jnp.concatenate([chosen[...].astype(jnp.float32), high, middle, low, jnp.zeros((8, count))], axis=0)
+    held[count:, :] = jnp.zeros((16, wide), jnp.bfloat16)
+    held[count:, :count] = info.astype(jnp.bfloat16)
+    stores[parts].start()
+    for k in range(parts):
+        loads[k].wait()
+        stores[k].start()
+    for store in stores:
+        store.wait()
 
 
 def table_kernel(middle, experts, *refs):
@@ -213,24 +225,21 @@
     swap_core = [(d, d ^ 1) for d in range(4)]
 
     wide = HALF
-    pieces = [lax.reduce_precision(route_weight[0].T, 8, 7)]
-    pieces.append(lax.reduce_precision(route_weight[0].T - pieces[0], 8, 7))
-    pieces.append(route_weight[0].T - pieces[0] - pieces[1])
-    step = 128
-    count = tokens // step
+    vmem = pl.BlockSpec(memory_space=pltpu.VMEM)
     packed = call(
         pack_kernel,
         "pack",
-        (count + 1,),
         (),
-        (cotangent, routing[0].T, jnp.concatenate(pieces, axis=0)),
-        [
-            pl.BlockSpec((1, step, wide), lambda i: (0, jnp.minimum(i, count - 1), 0)),
-            pl.BlockSpec((2, tokens), lambda i: (0, 0)),
-            pl.BlockSpec((6, tokens), lambda i: (0, 0)),
+        (),
+        (cotangent, routing[0].T, route_weight[0].T),
+        [ANY, vmem, vmem],
+        shape((tokens + 16, wide), jnp.bfloat16),
+        ANY,
+        scratch=[
+            pltpu.VMEM((tokens + 16, wide), jnp.bfloat16),
+            pltpu.SemaphoreType.DMA((8,)),
+            pltpu.SemaphoreType.DMA((9,)),
         ],
-        shape((tokens + 16, wide), jnp.bfloat16),
-        pl.BlockSpec((step, wide), lambda i: (i, 0)),
         moved=4 * tokens * width,
         limit=PACK_LIMIT,
     )

time: 192 us -> 190 us (0.990)
  no operation moved by 1% of the time
where the time goes in v4:
time: 190 us; the launch traced here: 189 us
  Pallas kernels  77.6 us (41%)
  waiting for transfers between devices  60.4 us (32%)
  starting transfers between devices  43.3 us (23%)
  local copies, waits for them, and re-layouts  6.62 us (3%)
    pallas_call x36, Pallas kernels, call(): pl.pallas_call(kernel, name=name, grid_spec=pltpu.PrefetchScalarGridSpec(...  77.6 us
    ppermute x8, waiting for transfers between devices, pick(): return (mine, other, lax.ppermute(other, 'expert', swap_y))  24.6 us
    ppermute x8, waiting for transfers between devices, permuted(): return [lax.ppermute(p, 'expert', way) for p in parts]  15.2 us
    ppermute x8, starting transfers between devices, permuted(): return [lax.ppermute(p, 'expert', way) for p in parts]  13.7 us
    ppermute x8, starting transfers between devices, pick(): return (mine, other, lax.ppermute(other, 'expert', swap_y))  13.3 us
    ppermute x4, waiting for transfers between devices, sum_x(): fars[k] = lax.ppermute(acrosses[k], 'dp', swap_x)  11 us
    ppermute x4, starting transfers between devices, sum_x(): fars[k] = lax.ppermute(acrosses[k], 'dp', swap_x)  6 us
    ppermute x4, starting transfers between devices, update(): crosseds[k] = lax.ppermute(freshes[k], 'dp', swap_x)  5.12 us
  transfers between devices with their start and end apart: 35, of which 17 were waited for; matrix products, arithmetic and copies ran while one was open for 1% of the time, Pallas kernels for 38%

profile of v4, /device:TPU:0, one launch (start us, length us, event | category | flops | bytes accessed | tf_op | source)
XLA Modules:
  0.0 189.3 jit_solution(7265052137106175392)
XLA Ops:
  0.6 2.9 %pack.1.refs_0_ = bf16[528,1280]{1,0:T(8,128)(2,1)} custom-call(bf16[1,512,2048]{2,1,0:T(8,128)(2,1)} %tokens.1, s32[2,512]{1,0:T(2,128)} %bitcast.25, f32[2,512]{1,0:T(2,128)} %bitcast.26), custom_call_target="tpu_custom_call" | custom-call | bytes 1024 | tf_op jit(solution)/shard_map/pack/pallas_call | solution.py:36
  3.6 3.1 %collective-permute-start = (bf16[528,1280]{1,0:T(8,128)(2,1)}, bf16[528,1280]{1,0:T(8,128)(2,1)}, u32[]{:S(2)}, u32[]{:S(2)}) collective-permute-start(bf16[528,1280]{1,0:T(8,128)(2,1)} %pack.1.refs_0_), channel_id=1, source_target_pairs={{0,8},{4,12},{8,0},{12,4},{16,24},{20,28},{24,16},{28,20},{1,9},{5... | collective-permute-start | bytes 4055048 | tf_op jit(solution)/shard_map/ppermute | solution.py:249
  13.0 5.9 %pick.8 = (bf16[256,2048]{1,0:T(8,128)(2,1)S(1)}, bf16[256,2048]{1,0:T(8,128)(2,1)}) custom-call(s32[1]{0:T(128)} %bitcast.8.middle, bf16[512,512]{1,0:T(8,128)(2,1)S(1)} %get-tuple-element.95.picks, f32[512,1]{1,0:T(8,128)S(1)} %get-tuple-element.96.scales, bf16[528,1280]{1,0:T(8,128)(2,1)S(1)} %copy-done.5, bf16[512,768]{1,0:T(8,128)(2,1)} %slice_bitcast_fusion.refs_1_), custom_call_target="tpu_custom_call" | custom-call | flops 262144 | bytes 1536 | tf_op jit(solution)/shard_map/pick/pallas_call | solution.py:36
  20.4 3.3 %collective-permute-start.4 = (bf16[512,768]{1,0:T(8,128)(2,1)}, bf16[512,768]{1,0:T(8,128)(2,1)}, u32[]{:S(2)}, u32[]{:S(2)}) collective-permute-start(bf16[512,768]{1,0:T(8,128)(2,1)} %slice_bitcast_fusion.refs_1_), channel_id=1, source_target_pairs={{0,8},{4,12},{8,0},{12,4},{16,24},{20,28},{24,16},{28,20},{1,9},{5... | collective-permute-start | bytes 2359304 | tf_op jit(solution)/shard_map/ppermute | solution.py:249
  25.4 2.8 %copy-done = bf16[1,1,2048,1536]{3,2,1,0:T(8,128)(2,1)S(1)} copy-done((bf16[1,1,2048,1536]{3,2,1,0:T(8,128)(2,1)S(1)}, bf16[1,1,2048,1536]{3,2,1,0:T(8,128)(2,1)}, u32[]{:S(2)}) %copy-start) | copy-done | bytes 6291480
  28.2 3.2 %hidden.1.turned = bf16[768,2048]{1,0:T(8,128)(2,1)S(1)} custom-call(s32[8]{0:T(128)S(1)} %stack.59.order, s32[4]{0:T(128)S(1)} %pad_add_fusion.1.groups.places, bf16[1,1,2048,1536]{3,2,1,0:T(8,128)(2,1)S(1)} %copy-done), custom_call_target="tpu_custom_call" | custom-call | flops 15360 | bytes 3456 | tf_op jit(solution)/shard_map/hidden/pallas_call | solution.py:36
  34.1 3.4 %collective-permute-done.refs_0_ = bf16[528,1280]{1,0:T(8,128)(2,1)} collective-permute-done((bf16[528,1280]{1,0:T(8,128)(2,1)}, bf16[528,1280]{1,0:T(8,128)(2,1)}, u32[]{:S(2)}, u32[]{:S(2)}) %collective-permute-start) | collective-permute-done | bytes 1351712 | tf_op jit(solution)/shard_map/ppermute | solution.py:249
  41.2 2.6 %collective-permute-done.6.refs_0_.refs_1_ = bf16[256,2048]{1,0:T(8,128)(2,1)} collective-permute-done((bf16[256,2048]{1,0:T(8,128)(2,1)}, bf16[256,2048]{1,0:T(8,128)(2,1)}, u32[]{:S(2)}, u32[]{:S(2)}) %collective-permute-start.6) | collective-permute-done | bytes 1048608 | tf_op jit(solution)/shard_map/ppermute | solution.py:304
  43.8 3.8 %back.9.refs_3_ = bf16[1,1,2048,1536]{3,2,1,0:T(8,128)(2,1)} custom-call(s32[8]{0:T(128)S(1)} %stack.59.order, bf16[256,2048]{1,0:T(8,128)(2,1)} %collective-permute-done.6.refs_0_.refs_1_, bf16[1,768,2048]{2,1,0:T(8,128)(2,1)S(1)} %copy-done.1, bf16[1,1,2048,1536]{3,2,1,0:T(8,128)(2,1)S(1)} %bitcast.24, ...), custom_call_target="tpu_custom_call", output_to_operand_aliasing={{}: (4, {})} | custom-call | flops 196608 | bytes 928 | tf_op jit(solution)/shard_map/back/pallas_call | solution.py:36
  47.6 6.7 %collective-permute-done.4.refs_1_ = bf16[512,768]{1,0:T(8,128)(2,1)} collective-permute-done((bf16[512,768]{1,0:T(8,128)(2,1)}, bf16[512,768]{1,0:T(8,128)(2,1)}, u32[]{:S(2)}, u32[]{:S(2)}) %collective-permute-start.4) | collective-permute-done | bytes 786464 | tf_op jit(solution)/shard_map/ppermute | solution.py:249
  54.3 5.7 %pick.9 = (bf16[256,2048]{1,0:T(8,128)(2,1)S(1)}, bf16[256,2048]{1,0:T(8,128)(2,1)S(1)}) custom-call(s32[1]{0:T(128)} %bitcast.8.middle, bf16[512,512]{1,0:T(8,128)(2,1)S(1)} %get-tuple-element.100.picks, f32[512,1]{1,0:T(8,128)S(1)} %get-tuple-element.101.scales, bf16[528,1280]{1,0:T(8,128)(2,1)} %collective-permute-done.refs_0_, ...), custom_call_target="tpu_custom_call" | custom-call | flops 262144 | bytes 1536 | tf_op jit(solution)/shard_map/pick/pallas_call | solution.py:36
  64.1 2.6 %back.10.refs_3_ = bf16[1,1,2048,1536]{3,2,1,0:T(8,128)(2,1)} custom-call(s32[8]{0:T(128)S(1)} %stack.59.order, bf16[256,2048]{1,0:T(8,128)(2,1)S(1)} %get-tuple-element.105.refs_0_.refs_2_, bf16[1,768,2048]{2,1,0:T(8,128)(2,1)S(1)} %copy-done.1, bf16[1,1,2048,1536]{3,2,1,0:T(8,128)(2,1)S(1)} %bitcast.24, ...), custom_call_target="tpu_custom_call", output_to_operand_aliasing={{}: (4, {})} | custom-call | flops 196608 | bytes 928 | tf_op jit(solution)/shard_map/back/pallas_call | solution.py:36
  66.7 16.9 %collective-permute-done.7.refs_0_.refs_3_ = bf16[256,2048]{1,0:T(8,128)(2,1)S(1)} collective-permute-done((bf16[256,2048]{1,0:T(8,128)(2,1)S(1)}, bf16[256,2048]{1,0:T(8,128)(2,1)S(1)}, u32[]{:S(2)}, u32[]{:S(2)}) %collective-permute-start.7) | collective-permute-done | bytes 1048608 | tf_op jit(solution)/shard_map/ppermute | solution.py:304
  94.9 5.2 %collective-permute-done.10.refs_1_ = bf16[512,768]{1,0:T(8,128)(2,1)S(1)} collective-permute-done((bf16[512,768]{1,0:T(8,128)(2,1)}, bf16[512,768]{1,0:T(8,128)(2,1)S(1)}, u32[]{:S(2)}, u32[]{:S(2)}) %collective-permute-start.10) | collective-permute-done | bytes 786464 | tf_op jit(solution)/shard_map/ppermute | solution.py:249
  106.4 5.3 %base.2 = f32[768,1280]{1,0:T(8,128)S(1)} custom-call(bf16[768,2048]{1,0:T(8,128)(2,1)S(1)} %hidden.1.turned, bf16[256,2048]{1,0:T(8,128)(2,1)S(1)} %get-tuple-element.97.refs_0_, bf16[256,2048]{1,0:T(8,128)(2,1)} %collective-permute-done.6.refs_0_.refs_1_, bf16[256,2048]{1,0:T(8,128)(2,1)S(1)} %get-tuple-element.105.refs_0_.refs_2_, ...), custom_call_target="tpu_custom_call" | custom-call | flops 737280 | bytes 2496 | tf_op jit(solution)/shard_map/base/pallas_call | solution.py:36
  115.5 3.5 %base.3 = f32[768,768]{1,0:T(8,128)S(1)} custom-call(bf16[768,2048]{1,0:T(8,128)(2,1)S(1)} %hidden.1.turned, bf16[256,2048]{1,0:T(8,128)(2,1)S(1)} %get-tuple-element.97.refs_0_, bf16[256,2048]{1,0:T(8,128)(2,1)} %collective-permute-done.6.refs_0_.refs_1_, bf16[256,2048]{1,0:T(8,128)(2,1)S(1)} %get-tuple-element.105.refs_0_.refs_2_, ...), custom_call_target="tpu_custom_call" | custom-call | flops 442368 | bytes 1728 | tf_op jit(solution)/shard_map/base/pallas_call | solution.py:36
  122.7 4.9 %collective-permute-done.13.refs_1_ = bf16[512,768]{1,0:T(8,128)(2,1)S(1)} collective-permute-done((bf16[512,768]{1,0:T(8,128)(2,1)S(1)}, bf16[512,768]{1,0:T(8,128)(2,1)S(1)}, u32[]{:S(2)}, u32[]{:S(2)}) %collective-permute-start.13) | collective-permute-done | bytes 786464 | tf_op jit(solution)/shard_map/ppermute | solution.py:386
  128.8 2.8 %collective-permute-start.15 = (bf16[256,768]{1,0:T(8,128)(2,1)S(1)}, bf16[256,768]{1,0:T(8,128)(2,1)S(1)}, u32[]{:S(2)}, u32[]{:S(2)}) collective-permute-start(bf16[256,768]{1,0:T(8,128)(2,1)S(1)} %get-tuple-element.133), channel_id=1, source_target_pairs={{0,4},{4,0},{8,12},{12,8},{16,20},{20,16},{24,28},{28,24},{1,5},{5... | collective-permute-start | bytes 1179656 | tf_op jit(solution)/shard_map/ppermute | solution.py:304
  133.2 4.2 %collective-permute-done.17.far = bf16[192,512]{1,0:T(8,128)(2,1)S(1)} collective-permute-done((bf16[192,512]{1,0:T(8,128)(2,1)S(1)}, bf16[192,512]{1,0:T(8,128)(2,1)S(1)}, u32[]{:S(2)}, u32[]{:S(2)}) %collective-permute-start.17) | collective-permute-done | bytes 196640 | tf_op jit(solution)/shard_map/ppermute | solution.py:494
  138.8 2.6 %back.13.refs_6_ = bf16[1,1,2048,1536]{3,2,1,0:T(8,128)(2,1)} custom-call(s32[8]{0:T(128)S(1)} %stack.59.order, bf16[256,1280]{1,0:T(8,128)(2,1)S(1)} %collective-permute-done.11.refs_5_.refs_0_, bf16[256,768]{1,0:T(8,128)(2,1)S(1)} %collective-permute-done.14.refs_5_.refs_1_, bf16[1,768,2048]{2,1,0:T(8,128)(2,1)S(1)} %copy-done.1, ...), custom_call_target="tpu_custom_call", output_to_operand_aliasing={{}: (5, {})} | custom-call | flops 196608 | bytes 928 | tf_op jit(solution)/shard_map/back/pallas_call | solution.py:36
  150.8 5.9 %collective-permute-done.20.far = bf16[192,768]{1,0:T(8,128)(2,1)S(1)} collective-permute-done((bf16[192,768]{1,0:T(8,128)(2,1)S(1)}, bf16[192,768]{1,0:T(8,128)(2,1)S(1)}, u32[]{:S(2)}, u32[]{:S(2)}) %collective-permute-start.20) | collective-permute-done | bytes 294944 | tf_op jit(solution)/shard_map/ppermute | solution.py:494
  161.9 3.9 %collective-permute-done.23.got.refs_3_ = bf16[256,256]{1,0:T(8,128)(2,1)S(1)} collective-permute-done((bf16[256,256]{1,0:T(8,128)(2,1)S(1)}, bf16[256,256]{1,0:T(8,128)(2,1)S(1)}, u32[]{:S(2)}, u32[]{:S(2)}) %collective-permute-start.23) | collective-permute-done | bytes 131104 | tf_op jit(solution)/shard_map/ppermute | solution.py:304
  169.3 2.6 %back.14.refs_6_ = bf16[1,1,2048,1536]{3,2,1,0:T(8,128)(2,1)} custom-call(s32[8]{0:T(128)S(1)} %stack.59.order, bf16[256,512]{1,0:T(8,128)(2,1)S(1)} %get-tuple-element.165.mine.refs_0_, bf16[256,768]{1,0:T(8,128)(2,1)S(1)} %get-tuple-element.132.mine.refs_1_, bf16[256,512]{1,0:T(8,128)(2,1)S(1)} %get-tuple-element.155.mine.refs_2_, ...), custom_call_target="tpu_custom_call", output_to_operand_aliasing={{}: (7, {})} | custom-call | flops 196608 | bytes 928 | tf_op jit(solution)/shard_map/back/pallas_call | solution.py:36
  179.0 2.6 %back.15 = bf16[1,1,2048,1536]{3,2,1,0:T(8,128)(2,1)} custom-call(s32[8]{0:T(128)S(1)} %stack.59.order, bf16[256,512]{1,0:T(8,128)(2,1)S(1)} %collective-permute-done.12.got.refs_0_, bf16[256,768]{1,0:T(8,128)(2,1)S(1)} %collective-permute-done.15.got.refs_1_, ...), custom_call_target="tpu_custom_call", output_to_operand_aliasing={{}: (7, {})} | custom-call | flops 196608 | bytes 928 | tf_op jit(solution)/shard_map/back/pallas_call | solution.py:36
  (116 shorter events, 81.8 us)
Async XLA Ops:
  3.6 33.9 %collective-permute-start = (bf16[528,1280]{1,0:T(8,128)(2,1)}, bf16[528,1280]{1,0:T(8,128)(2,1)}, u32[]{:S(2)}, u32[]{:S(2)}) collective-permute-start(bf16[528,1280]{1,0:T(8,128)(2,1)} %pack.1.refs_0_), channel_id=1, source_target_pairs={{0,8},{4,12},{8,0},{12,4},{16,24},{20,28},{24,16},{28,20},{1,9},{5... | collective-permute-start | bytes 4055048 | tf_op jit(solution)/shard_map/ppermute | solution.py:249
  6.7 30.8 %collective-permute-start.1 = (bf16[528,1280]{1,0:T(8,128)(2,1)}, bf16[528,1280]{1,0:T(8,128)(2,1)}, u32[]{:S(2)}, u32[]{:S(2)}) collective-permute-start(bf16[528,1280]{1,0:T(8,128)(2,1)} %pack.1.refs_0_), channel_id=1, source_target_pairs={{8,16},{16,8},{12,20},{20,12},{9,17},{17,9},{13,21},{21,13},{10,18... | collective-permute-start | bytes 4055048 | tf_op jit(solution)/shard_map/ppermute | solution.py:249
  18.9 24.9 %collective-permute-start.6 = (bf16[256,2048]{1,0:T(8,128)(2,1)}, bf16[256,2048]{1,0:T(8,128)(2,1)}, u32[]{:S(2)}, u32[]{:S(2)}) collective-permute-start(bf16[256,2048]{1,0:T(8,128)(2,1)} %get-tuple-element.102), channel_id=1, source_target_pairs={{0,4},{4,0},{8,12},{12,8},{16,20},{20,16},{24,28},{28,24},{1,5},{5... | collective-permute-start | bytes 3145736 | tf_op jit(solution)/shard_map/ppermute | solution.py:304
  20.4 33.9 %collective-permute-start.4 = (bf16[512,768]{1,0:T(8,128)(2,1)}, bf16[512,768]{1,0:T(8,128)(2,1)}, u32[]{:S(2)}, u32[]{:S(2)}) collective-permute-start(bf16[512,768]{1,0:T(8,128)(2,1)} %slice_bitcast_fusion.refs_1_), channel_id=1, source_target_pairs={{0,8},{4,12},{8,0},{12,4},{16,24},{20,28},{24,16},{28,20},{1,9},{5... | collective-permute-start | bytes 2359304 | tf_op jit(solution)/shard_map/ppermute | solution.py:249
  23.7 30.6 %collective-permute-start.5 = (bf16[512,768]{1,0:T(8,128)(2,1)}, bf16[512,768]{1,0:T(8,128)(2,1)}, u32[]{:S(2)}, u32[]{:S(2)}) collective-permute-start(bf16[512,768]{1,0:T(8,128)(2,1)} %slice_bitcast_fusion.refs_1_), channel_id=1, source_target_pairs={{8,16},{16,8},{12,20},{20,12},{9,17},{17,9},{13,21},{21,13},{10,18... | collective-permute-start | bytes 2359304 | tf_op jit(solution)/shard_map/ppermute | solution.py:249
  37.5 46.2 %collective-permute-start.2 = (bf16[528,1280]{1,0:T(8,128)(2,1)}, bf16[528,1280]{1,0:T(8,128)(2,1)S(1)}, u32[]{:S(2)}, u32[]{:S(2)}) collective-permute-start(bf16[528,1280]{1,0:T(8,128)(2,1)} %collective-permute-done.refs_0_), channel_id=1, source_target_pairs={{8,16},{16,8},{12,20},{20,12},{9,17},{17,9},{13,21},{21,13},{10,18... | collective-permute-start | bytes 4055048 | tf_op jit(solution)/shard_map/ppermute | solution.py:249
  38.2 45.4 %collective-permute-start.3 = (bf16[528,1280]{1,0:T(8,128)(2,1)}, bf16[528,1280]{1,0:T(8,128)(2,1)S(1)}, u32[]{:S(2)}, u32[]{:S(2)}) collective-permute-start(bf16[528,1280]{1,0:T(8,128)(2,1)} %collective-permute-done.1.refs_0_), channel_id=1, source_target_pairs={{16,24},{20,28},{8,0},{12,4},{17,25},{21,29},{9,1},{13,5},{18,26},... | collective-permute-start | bytes 4055048 | tf_op jit(solution)/shard_map/ppermute | solution.py:249
  60.1 23.6 %collective-permute-start.7 = (bf16[256,2048]{1,0:T(8,128)(2,1)S(1)}, bf16[256,2048]{1,0:T(8,128)(2,1)S(1)}, u32[]{:S(2)}, u32[]{:S(2)}) collective-permute-start(bf16[256,2048]{1,0:T(8,128)(2,1)S(1)} %get-tuple-element.107), channel_id=1, source_target_pairs={{0,4},{4,0},{8,12},{12,8},{16,20},{20,16},{24,28},{28,24},{1,5},{5... | collective-permute-start | bytes 3145736 | tf_op jit(solution)/shard_map/ppermute | solution.py:304
  62.1 32.7 %collective-permute-start.9 = (bf16[512,768]{1,0:T(8,128)(2,1)}, bf16[512,768]{1,0:T(8,128)(2,1)S(1)}, u32[]{:S(2)}, u32[]{:S(2)}) collective-permute-start(bf16[512,768]{1,0:T(8,128)(2,1)} %collective-permute-done.4.refs_1_), channel_id=1, source_target_pairs={{8,16},{16,8},{12,20},{20,12},{9,17},{17,9},{13,21},{21,13},{10,18... | collective-permute-start | bytes 2359304 | tf_op jit(solution)/shard_map/ppermute | solution.py:249
  62.8 37.2 %collective-permute-start.10 = (bf16[512,768]{1,0:T(8,128)(2,1)}, bf16[512,768]{1,0:T(8,128)(2,1)S(1)}, u32[]{:S(2)}, u32[]{:S(2)}) collective-permute-start(bf16[512,768]{1,0:T(8,128)(2,1)} %collective-permute-done.5.refs_0_), channel_id=1, source_target_pairs={{16,24},{20,28},{8,0},{12,4},{17,25},{21,29},{9,1},{13,5},{18,26},... | collective-permute-start | bytes 2359304 | tf_op jit(solution)/shard_map/ppermute | solution.py:249
  87.8 18.6 %collective-permute-start.11 = (bf16[256,1280]{1,0:T(8,128)(2,1)S(1)}, bf16[256,1280]{1,0:T(8,128)(2,1)S(1)}, u32[]{:S(2)}, u32[]{:S(2)}) collective-permute-start(bf16[256,1280]{1,0:T(8,128)(2,1)S(1)} %get-tuple-element.116), channel_id=1, source_target_pairs={{0,4},{4,0},{8,12},{12,8},{16,20},{20,16},{24,28},{28,24},{1,5},{5... | collective-permute-start | bytes 1966088 | tf_op jit(solution)/shard_map/ppermute | solution.py:304
  89.4 22.3 %collective-permute-start.8 = (bf16[528,512]{1,0:T(8,128)(2,1)S(1)}, bf16[528,512]{1,0:T(8,128)(2,1)S(1)}, u32[]{:S(2)}, u32[]{:S(2)}) collective-permute-start(bf16[528,512]{1,0:T(8,128)(2,1)S(1)} %slice.34), channel_id=1, source_target_pairs={{16,24},{20,28},{8,0},{12,4},{17,25},{21,29},{9,1},{13,5},{18,26},... | collective-permute-start | bytes 1622024 | tf_op jit(solution)/shard_map/ppermute | solution.py:386
  90.8 36.8 %collective-permute-start.13 = (bf16[512,768]{1,0:T(8,128)(2,1)S(1)}, bf16[512,768]{1,0:T(8,128)(2,1)S(1)}, u32[]{:S(2)}, u32[]{:S(2)}) collective-permute-start(bf16[512,768]{1,0:T(8,128)(2,1)S(1)} %slice.35), channel_id=1, source_target_pairs={{16,24},{20,28},{8,0},{12,4},{17,25},{21,29},{9,1},{13,5},{18,26},... | collective-permute-start | bytes 2359304 | tf_op jit(solution)/shard_map/ppermute | solution.py:386
  101.8 13.7 %collective-permute-start.14 = (bf16[256,768]{1,0:T(8,128)(2,1)S(1)}, bf16[256,768]{1,0:T(8,128)(2,1)S(1)}, u32[]{:S(2)}, u32[]{:S(2)}) collective-permute-start(bf16[256,768]{1,0:T(8,128)(2,1)S(1)} %get-tuple-element.127), channel_id=1, source_target_pairs={{0,4},{4,0},{8,12},{12,8},{16,20},{20,16},{24,28},{28,24},{1,5},{5... | collective-permute-start | bytes 1179656 | tf_op jit(solution)/shard_map/ppermute | solution.py:304
  121.2 10.5 %collective-permute-start.16 = (bf16[384,512]{1,0:T(8,128)(2,1)S(1)}, bf16[384,512]{1,0:T(8,128)(2,1)S(1)}, u32[]{:S(2)}, u32[]{:S(2)}) collective-permute-start(bf16[384,512]{1,0:T(8,128)(2,1)S(1)} %get-tuple-element.130), channel_id=1, source_target_pairs={{0,1},{1,0},{2,3},{3,2},{4,5},{5,4},{6,7},{7,6},{8,9},{9,8},{10,11... | collective-permute-start | bytes 1179656 | tf_op jit(solution)/shard_map/ppermute | solution.py:487
  121.2 23.4 %collective-permute-start.19 = (bf16[512,768]{1,0:T(8,128)(2,1)S(1)}, bf16[512,768]{1,0:T(8,128)(2,1)S(1)}, u32[]{:S(2)}, u32[]{:S(2)}) collective-permute-start(bf16[512,768]{1,0:T(8,128)(2,1)S(1)} %collective-permute-done.9.refs_0_), channel_id=1, source_target_pairs={{16,24},{20,28},{8,0},{12,4},{17,25},{21,29},{9,1},{13,5},{18,26},... | collective-permute-start | bytes 2359304 | tf_op jit(solution)/shard_map/ppermute | solution.py:386
  128.8 12.6 %collective-permute-start.15 = (bf16[256,768]{1,0:T(8,128)(2,1)S(1)}, bf16[256,768]{1,0:T(8,128)(2,1)S(1)}, u32[]{:S(2)}, u32[]{:S(2)}) collective-permute-start(bf16[256,768]{1,0:T(8,128)(2,1)S(1)} %get-tuple-element.133), channel_id=1, source_target_pairs={{0,4},{4,0},{8,12},{12,8},{16,20},{20,16},{24,28},{28,24},{1,5},{5... | collective-permute-start | bytes 1179656 | tf_op jit(solution)/shard_map/ppermute | solution.py:304
  143.0 7.8 %collective-permute-start.21 = (bf16[192,512]{1,0:T(8,128)(2,1)S(1)}, bf16[192,512]{1,0:T(8,128)(2,1)S(1)}, u32[]{:S(2)}, u32[]{:S(2)}) collective-permute-start(bf16[192,512]{1,0:T(8,128)(2,1)S(1)} %get-tuple-element.137.own), channel_id=1, source_target_pairs={{0,2},{1,3},{2,0},{3,1},{4,6},{5,7},{6,4},{7,5},{8,10},{9,11},{10,... | collective-permute-start | bytes 589832 | tf_op jit(solution)/shard_map/ppermute | solution.py:500
  145.1 11.6 %collective-permute-start.20 = (bf16[192,768]{1,0:T(8,128)(2,1)S(1)}, bf16[192,768]{1,0:T(8,128)(2,1)S(1)}, u32[]{:S(2)}, u32[]{:S(2)}) collective-permute-start(bf16[192,768]{1,0:T(8,128)(2,1)S(1)} %add_convert_fusion), channel_id=1, source_target_pairs={{0,2},{1,3},{2,0},{3,1},{4,6},{5,7},{6,4},{7,5},{8,10},{9,11},{10,... | collective-permute-start | bytes 884744 | tf_op jit(solution)/shard_map/ppermute | solution.py:494
  147.4 11.4 %collective-permute-start.24 = (bf16[256,512]{1,0:T(8,128)(2,1)S(1)}, bf16[256,512]{1,0:T(8,128)(2,1)S(1)}, u32[]{:S(2)}, u32[]{:S(2)}) collective-permute-start(bf16[256,512]{1,0:T(8,128)(2,1)S(1)} %get-tuple-element.156), channel_id=1, source_target_pairs={{0,4},{4,0},{8,12},{12,8},{16,20},{20,16},{24,28},{28,24},{1,5},{5... | collective-permute-start | bytes 786440 | tf_op jit(solution)/shard_map/ppermute | solution.py:304
  160.0 11.9 %collective-permute-start.29 = (bf16[384,512]{1,0:T(8,128)(2,1)S(1)}, bf16[384,512]{1,0:T(8,128)(2,1)S(1)}, u32[]{:S(2)}, u32[]{:S(2)}) collective-permute-start(bf16[384,512]{1,0:T(8,128)(2,1)S(1)} %constant_dynamic-update-slice_fusion), channel_id=1, source_target_pairs={{0,1},{1,0},{2,3},{3,2},{4,5},{5,4},{6,7},{7,6},{8,9},{9,8},{10,11... | collective-permute-start | bytes 1179656 | tf_op jit(solution)/shard_map/ppermute | solution.py:506
  160.4 16.4 %collective-permute-start.22 = (bf16[192,768]{1,0:T(8,128)(2,1)S(1)}, bf16[192,768]{1,0:T(8,128)(2,1)S(1)}, u32[]{:S(2)}, u32[]{:S(2)}) collective-permute-start(bf16[192,768]{1,0:T(8,128)(2,1)S(1)} %get-tuple-element.153.own), channel_id=1, source_target_pairs={{0,2},{1,3},{2,0},{3,1},{4,6},{5,7},{6,4},{7,5},{8,10},{9,11},{10,... | collective-permute-start | bytes 884744 | tf_op jit(solution)/shard_map/ppermute | solution.py:500
  167.9 7.9 %collective-permute-start.27 = (bf16[192,256]{1,0:T(8,128)(2,1)S(1)}, bf16[192,256]{1,0:T(8,128)(2,1)S(1)}, u32[]{:S(2)}, u32[]{:S(2)}) collective-permute-start(bf16[192,256]{1,0:T(8,128)(2,1)S(1)} %add_convert_fusion.3), channel_id=1, source_target_pairs={{0,2},{1,3},{2,0},{3,1},{4,6},{5,7},{6,4},{7,5},{8,10},{9,11},{10,... | collective-permute-start | bytes 294920 | tf_op jit(solution)/shard_map/ppermute | solution.py:494
  178.4 7.9 %collective-permute-start.30 = (bf16[192,256]{1,0:T(8,128)(2,1)S(1)}, bf16[192,256]{1,0:T(8,128)(2,1)S(1)}, u32[]{:S(2)}, u32[]{:S(2)}) collective-permute-start(bf16[192,256]{1,0:T(8,128)(2,1)S(1)} %get-tuple-element.176.own), channel_id=1, source_target_pairs={{0,2},{1,3},{2,0},{3,1},{4,6},{5,7},{6,4},{7,5},{8,10},{9,11},{10,... | collective-permute-start | bytes 294920 | tf_op jit(solution)/shard_map/ppermute | solution.py:500
  (19 other events, 112.9 us)

commit v5 on v4

--- a/solution.py
+++ b/solution.py
@@ -17,8 +17,9 @@
 
 VMEM_LIMIT = 24 * 1024 * 1024
 COST = 4096
-EARLY = False
-CLAIM = 3_000_000_000
+EARLY = True
+SUM = 2
+CLAIM = (3_000_000_000, 3_000_000_000, 3_000_000_000)
 TILE = 256
 HALF = 1280
 PACK_LIMIT = 56 * 1024 * 1024
@@ -152,12 +153,19 @@
     out[...] = jnp.dot(turned[...], rows, preferred_element_type=jnp.float32)
 
 
-def product_kernel(base, turned, mine, got, send, keep):
-    half = send.shape[0]
+def product_kernel(base, turned, mine, got, *outs):
+    *firsts, second, keep_first, keep_second = outs
     rows = jnp.concatenate([mine[...], got[...]], axis=0)
     total = base[...] + jnp.dot(turned[...], rows, preferred_element_type=jnp.float32)
-    send[...] = total[:half].astype(jnp.bfloat16)
-    keep[...] = total[half:].astype(jnp.bfloat16)
+    total = total.astype(jnp.bfloat16)
+    quarter = second.shape[0]
+    for k, out in enumerate((second, keep_first, keep_second), 1):
+        out[...] = total[k * quarter : (k + 1) * quarter]
+    for k, first in enumerate(firsts):
+
+        @pl.when(pl.program_id(0) == k)
+        def _():
+            first[...] = total[:quarter]
 
 
 def back_kernel(count, order, *refs):
@@ -406,13 +414,13 @@
         half = offset >= wide
         inner = offset - wide * half
         late = offset - SENT[k][0]
-        return pick(last_table, (middle_two[half],), (end_two,), inner, columns, claim=CLAIM, late=late)
+        return pick(last_table, (middle_two[half],), (end_two,), inner, columns, claim=CLAIM[k], late=late)
 
     def product(chunk, mine3, got3):
         offset, columns = chunk
         side = int(offset >= wide)
         start = (offset - wide * side) // TILE
-        half = shape((2 * rows, columns), jnp.bfloat16)
+        quarter = shape((rows, columns), jnp.bfloat16)
         part = pl.BlockSpec((capacity, TILE), lambda i: (0, i))
         return call(
             product_kernel,
@@ -426,8 +434,9 @@
                 part,
                 part,
             ],
-            (half, half),
-            (pl.BlockSpec((2 * rows, TILE), lambda i: (0, i)),) * 2,
+            (shape((rows, TILE), jnp.bfloat16),) * (columns // TILE) + (quarter,) * 3,
+            (pl.BlockSpec((rows, TILE), lambda i: (0, 0)),) * (columns // TILE)
+            + (pl.BlockSpec((rows, TILE), lambda i: (0, i)),) * 3,
             flops=4 * hidden_width * capacity * columns,
             moved=4 * hidden_width * capacity + 6 * hidden_width * columns,
         )
@@ -436,7 +445,6 @@
         offset, columns = chunk
         start = offset // TILE
         state = pl.BlockSpec((1, rows, TILE), lambda i: (0, 0, start + i))
-        second = pl.BlockSpec((rows, TILE), lambda i: (1, i))
         whole = pl.BlockSpec((rows, TILE), lambda i: (0, i))
         out_state = shape(master.shape, jnp.float32)
         return call(
@@ -445,7 +453,7 @@
             (columns // TILE,),
             (),
             (keep, near, far, master, moment1, moment2, *previous),
-            [second, second, whole, state, state, state] + [ANY] * len(previous),
+            [whole, whole, whole, state, state, state] + [ANY] * len(previous),
             (out_state, out_state, out_state, shape((rows, columns), jnp.bfloat16)),
             (state, state, state, whole),
             aliases={6 + k: k for k in range(len(previous))},
@@ -483,22 +491,32 @@
         return value if token is None else after(value, token)[0]
 
     def sum_core(k, token):
-        sends[k], keeps[k] = product(chunks[k], mines[k], tied(gots[k], token))
-        nears[k] = lax.ppermute(sends[k], "dp", swap_core)
-        return sends[k]
-
-    def sum_x(k, token):
-        near = tied(nears[k], token)
-        acrosses[k] = (keeps[k][:rows].astype(jnp.float32) + near[:rows].astype(jnp.float32)).astype(jnp.bfloat16)
-        nears[k] = near
-        fars[k] = lax.ppermute(acrosses[k], "dp", swap_x)
+        *firsts, second, keep_first, keep_second = product(chunks[k], mines[k], tied(gots[k], token))
+        keeps[k] = [keep_first, keep_second]
+        nears[k] = [[lax.ppermute(p, "dp", swap_core) for p in firsts], lax.ppermute(second, "dp", swap_core)]
+        sends[k] = second
+        return second
+
+    def sum_x(k, token, others=()):
+        for c in (k, *others):
+            near = jnp.concatenate(nears[c][0], axis=1)
+            acrosses[c] = (keeps[c][0].astype(jnp.float32) + near.astype(jnp.float32)).astype(jnp.bfloat16)
+        if others:
+            group = after(*(acrosses[c] for c in (k, *others)))
+            for c, value in zip((k, *others), group):
+                acrosses[c] = value
+        for c in (k, *others):
+            fars[c] = lax.ppermute(acrosses[c], "dp", swap_x)
         return acrosses[k]
 
     def update(k, token):
         nonlocal states
-        *states, freshes[k] = adam(chunks[k], keeps[k], nears[k], tied(fars[k], token), states)
+        *states, freshes[k] = adam(chunks[k], keeps[k][1], nears[k][1], tied(fars[k], token), states)
+        return freshes[k]
+
+    def gather_x(k, token):
+        freshes[k] = tied(freshes[k], token)
         crosseds[k] = lax.ppermute(freshes[k], "dp", swap_x)
-        return freshes[k]
 
     def gather_core(k, token):
         crosseds[k] = tied(crosseds[k], token)
@@ -533,28 +551,43 @@
     got2[1], fresh = after(got2[1], fresh)
     grad_preact = back(5, got2, grad_preact)
     sum_core(1, grad_preact)
-    ends[2], send = after(ends[2], sends[1])
-    across = sum_x(1, ends[2])
-    ends[2], across = after(ends[2], across)
+    if SUM == 0:
+        ends[2], nears[1][0][0] = after(ends[2], nears[1][0][0])
+        sum_x(1, None)
+        gather_x(0, None)
+    else:
+        gather_x(0, None)
+        crosseds[0], nears[1][0][0] = after(crosseds[0], nears[1][0][0])
+        sum_x(1, None)
+    if SUM == 2:
+        ends[2], acrosses[1] = after(ends[2], acrosses[1])
     arrive(2, 2)
     other = arrive(2, 3)
-    both = gather_core(0, other)
-    fresh = update(1, both)
-    send = sum_core(2, fresh)
-    send = sum_core(3, send)
-    across = sum_x(2, send)
-    across = sum_x(3, across)
-    mines[0], _ = after(mines[0], across)
     grad_preact = back(6, mines, grad_preact)
-    placed = gathered(0, grad_preact)
-    fresh = update(2, placed)
-    fresh = update(3, fresh)
-    both = gather_core(1, fresh)
-    gots[0], _ = after(gots[0], both)
+    fars[1], grad_preact = after(fars[1], grad_preact)
+    update(1, None)
+    gots[2], gots[3], freshes[1] = after(gots[2], gots[3], freshes[1])
+    gather_x(1, None)
+    gather_core(0, None)
+    sum_core(2, None)
+    sum_core(3, None)
     grad_preact = back(7, gots, grad_preact)
-    placed = gathered(1, grad_preact)
-    both = gather_core(2, placed)
-    gather_core(3, both)
+    crosseds[1], nears[2][0][0], nears[3][0][0], grad_preact = after(
+        crosseds[1], nears[2][0][0], nears[3][0][0], grad_preact
+    )
+    sum_x(2, None, (3,))
+    gather_core(1, None)
+    gathered(0, None)
+    gathered(1, None)
+    fars[2], nears[2][1], nears[3][1], next_weight = after(fars[2], nears[2][1], nears[3][1], next_weight[0])
+    next_weight = (next_weight,)
+    update(2, None)
+    fars[3], freshes[2] = after(fars[3], freshes[2])
+    gather_x(2, None)
+    update(3, None)
+    gather_x(3, None)
+    gather_core(2, None)
+    gather_core(3, None)
     gathered(2, None)
     gathered(3, None)
     return (grad_preact, next_weight[0], *states)

time: 190 us -> 188 us (0.989)
    ppermute x12 -> x20, starting transfers between devices: 11.4 us -> 12.2 us  [the longest x4 5.01 us: gather_x(): crosseds[k] = lax.ppermute(freshes[k], 'dp', swap_x)]
    ppermute x12 -> x20, waiting for transfers between devices: 15.6 us -> 15.5 us  [the longest x4 8.53 us: sum_x(): fars[c] = lax.ppermute(acrosses[c], 'dp', swap_x)]
    unnamed x19 -> x16, local copies, waits for them, and re-layouts: 4.19 us -> 4.15 us
  transfers between devices with their start and end apart: 35 -> 43, of which waited for: 17 -> 20; matrix products, arithmetic and copies ran while one was open for 1% -> 2% of each run, Pallas kernels for 38% -> 39%
where the time goes in v5:
time: 188 us; the launch traced here: 187 us
  Pallas kernels  77.7 us (41%)
  waiting for transfers between devices  59.6 us (32%)
  starting transfers between devices  41.8 us (22%)
  local copies, waits for them, and re-layouts  6.54 us (3%)
    pallas_call x36, Pallas kernels, call(): pl.pallas_call(kernel, name=name, grid_spec=pltpu.PrefetchScalarGridSpec(...  77.7 us
    ppermute x8, waiting for transfers between devices, pick(): return (mine, other, lax.ppermute(other, 'expert', swap_y))  23.2 us
    ppermute x8, waiting for transfers between devices, permuted(): return [lax.ppermute(p, 'expert', way) for p in parts]  16.8 us
    ppermute x8, starting transfers between devices, permuted(): return [lax.ppermute(p, 'expert', way) for p in parts]  13.8 us
    ppermute x8, starting transfers between devices, pick(): return (mine, other, lax.ppermute(other, 'expert', swap_y))  11.5 us
    ppermute x4, waiting for transfers between devices, sum_x(): fars[c] = lax.ppermute(acrosses[c], 'dp', swap_x)  8.53 us
    ppermute x4, waiting for transfers between devices, gather_x(): crosseds[k] = lax.ppermute(freshes[k], 'dp', swap_x)  6.21 us
    ppermute x4, starting transfers between devices, gather_x(): crosseds[k] = lax.ppermute(freshes[k], 'dp', swap_x)  5.01 us
  transfers between devices with their start and end apart: 43, of which 20 were waited for; matrix products, arithmetic and copies ran while one was open for 2% of the time, Pallas kernels for 39%

profile of v5, /device:TPU:0, one launch (start us, length us, event | category | flops | bytes accessed | tf_op | source)
XLA Modules:
  0.0 187.2 jit_solution(7841136032879499699)
XLA Ops:
  0.6 2.9 %pack.1.refs_0_ = bf16[528,1280]{1,0:T(8,128)(2,1)} custom-call(bf16[1,512,2048]{2,1,0:T(8,128)(2,1)} %tokens.1, s32[2,512]{1,0:T(2,128)} %bitcast.25, f32[2,512]{1,0:T(2,128)} %bitcast.26), custom_call_target="tpu_custom_call" | custom-call | bytes 1024 | tf_op jit(solution)/shard_map/pack/pallas_call | solution.py:37
  3.6 3.1 %collective-permute-start = (bf16[528,1280]{1,0:T(8,128)(2,1)}, bf16[528,1280]{1,0:T(8,128)(2,1)}, u32[]{:S(2)}, u32[]{:S(2)}) collective-permute-start(bf16[528,1280]{1,0:T(8,128)(2,1)} %pack.1.refs_0_), channel_id=1, source_target_pairs={{0,8},{4,12},{8,0},{12,4},{16,24},{20,28},{24,16},{28,20},{1,9},{5... | collective-permute-start | bytes 4055048 | tf_op jit(solution)/shard_map/ppermute | solution.py:257
  13.0 5.9 %pick.8 = (bf16[256,2048]{1,0:T(8,128)(2,1)S(1)}, bf16[256,2048]{1,0:T(8,128)(2,1)}) custom-call(s32[1]{0:T(128)} %bitcast.middle, bf16[512,512]{1,0:T(8,128)(2,1)S(1)} %get-tuple-element.108.picks, f32[512,1]{1,0:T(8,128)S(1)} %get-tuple-element.109.scales, bf16[528,1280]{1,0:T(8,128)(2,1)S(1)} %copy-done.5, bf16[512,768]{1,0:T(8,128)(2,1)} %slice_bitcast_fusion.refs_1_), custom_call_target="tpu_custom_call" | custom-call | flops 262144 | bytes 1536 | tf_op jit(solution)/shard_map/pick/pallas_call | solution.py:37
  20.4 3.3 %collective-permute-start.4 = (bf16[512,768]{1,0:T(8,128)(2,1)}, bf16[512,768]{1,0:T(8,128)(2,1)}, u32[]{:S(2)}, u32[]{:S(2)}) collective-permute-start(bf16[512,768]{1,0:T(8,128)(2,1)} %slice_bitcast_fusion.refs_1_), channel_id=1, source_target_pairs={{0,8},{4,12},{8,0},{12,4},{16,24},{20,28},{24,16},{28,20},{1,9},{5... | collective-permute-start | bytes 2359304 | tf_op jit(solution)/shard_map/ppermute | solution.py:257
  25.4 2.8 %copy-done = bf16[1,1,2048,1536]{3,2,1,0:T(8,128)(2,1)S(1)} copy-done((bf16[1,1,2048,1536]{3,2,1,0:T(8,128)(2,1)S(1)}, bf16[1,1,2048,1536]{3,2,1,0:T(8,128)(2,1)}, u32[]{:S(2)}) %copy-start) | copy-done | bytes 6291480
  28.2 3.2 %hidden.1.turned = bf16[768,2048]{1,0:T(8,128)(2,1)S(1)} custom-call(s32[8]{0:T(128)S(1)} %stack.62.order, s32[4]{0:T(128)S(1)} %pad_add_fusion.1.groups.places, bf16[1,1,2048,1536]{3,2,1,0:T(8,128)(2,1)S(1)} %copy-done), custom_call_target="tpu_custom_call" | custom-call | flops 15360 | bytes 3456 | tf_op jit(solution)/shard_map/hidden/pallas_call | solution.py:37
  34.1 3.3 %collective-permute-done.refs_0_ = bf16[528,1280]{1,0:T(8,128)(2,1)} collective-permute-done((bf16[528,1280]{1,0:T(8,128)(2,1)}, bf16[528,1280]{1,0:T(8,128)(2,1)}, u32[]{:S(2)}, u32[]{:S(2)}) %collective-permute-start) | collective-permute-done | bytes 1351712 | tf_op jit(solution)/shard_map/ppermute | solution.py:257
  41.2 2.6 %collective-permute-done.6.refs_0_.refs_1_ = bf16[256,2048]{1,0:T(8,128)(2,1)} collective-permute-done((bf16[256,2048]{1,0:T(8,128)(2,1)}, bf16[256,2048]{1,0:T(8,128)(2,1)}, u32[]{:S(2)}, u32[]{:S(2)}) %collective-permute-start.6) | collective-permute-done | bytes 1048608 | tf_op jit(solution)/shard_map/ppermute | solution.py:312
  43.8 3.8 %back.9.refs_3_ = bf16[1,1,2048,1536]{3,2,1,0:T(8,128)(2,1)} custom-call(s32[8]{0:T(128)S(1)} %stack.62.order, bf16[256,2048]{1,0:T(8,128)(2,1)} %collective-permute-done.6.refs_0_.refs_1_, bf16[1,768,2048]{2,1,0:T(8,128)(2,1)S(1)} %copy-done.1, bf16[1,1,2048,1536]{3,2,1,0:T(8,128)(2,1)S(1)} %bitcast.24, ...), custom_call_target="tpu_custom_call", output_to_operand_aliasing={{}: (4, {})} | custom-call | flops 196608 | bytes 928 | tf_op jit(solution)/shard_map/back/pallas_call | solution.py:37
  47.6 6.7 %collective-permute-done.4.refs_1_ = bf16[512,768]{1,0:T(8,128)(2,1)} collective-permute-done((bf16[512,768]{1,0:T(8,128)(2,1)}, bf16[512,768]{1,0:T(8,128)(2,1)}, u32[]{:S(2)}, u32[]{:S(2)}) %collective-permute-start.4) | collective-permute-done | bytes 786464 | tf_op jit(solution)/shard_map/ppermute | solution.py:257
  54.3 5.7 %pick.9 = (bf16[256,2048]{1,0:T(8,128)(2,1)S(1)}, bf16[256,2048]{1,0:T(8,128)(2,1)S(1)}) custom-call(s32[1]{0:T(128)} %bitcast.middle, bf16[512,512]{1,0:T(8,128)(2,1)S(1)} %get-tuple-element.113.picks, f32[512,1]{1,0:T(8,128)S(1)} %get-tuple-element.114.scales, bf16[528,1280]{1,0:T(8,128)(2,1)} %collective-permute-done.refs_0_, ...), custom_call_target="tpu_custom_call" | custom-call | flops 262144 | bytes 1536 | tf_op jit(solution)/shard_map/pick/pallas_call | solution.py:37
  64.1 2.6 %back.10.refs_3_ = bf16[1,1,2048,1536]{3,2,1,0:T(8,128)(2,1)} custom-call(s32[8]{0:T(128)S(1)} %stack.62.order, bf16[256,2048]{1,0:T(8,128)(2,1)S(1)} %get-tuple-element.118.refs_0_.refs_2_, bf16[1,768,2048]{2,1,0:T(8,128)(2,1)S(1)} %copy-done.1, bf16[1,1,2048,1536]{3,2,1,0:T(8,128)(2,1)S(1)} %bitcast.24, ...), custom_call_target="tpu_custom_call", output_to_operand_aliasing={{}: (4, {})} | custom-call | flops 196608 | bytes 928 | tf_op jit(solution)/shard_map/back/pallas_call | solution.py:37
  66.7 16.9 %collective-permute-done.7.refs_0_.refs_3_ = bf16[256,2048]{1,0:T(8,128)(2,1)S(1)} collective-permute-done((bf16[256,2048]{1,0:T(8,128)(2,1)S(1)}, bf16[256,2048]{1,0:T(8,128)(2,1)S(1)}, u32[]{:S(2)}, u32[]{:S(2)}) %collective-permute-start.7) | collective-permute-done | bytes 1048608 | tf_op jit(solution)/shard_map/ppermute | solution.py:312
  90.7 2.6 %back.11.refs_4_ = bf16[1,1,2048,1536]{3,2,1,0:T(8,128)(2,1)} custom-call(s32[8]{0:T(128)S(1)} %stack.62.order, bf16[256,2048]{1,0:T(8,128)(2,1)S(1)} %collective-permute-done.7.refs_0_.refs_3_, bf16[1,768,2048]{2,1,0:T(8,128)(2,1)S(1)} %copy-done.1, bf16[1,1,2048,1536]{3,2,1,0:T(8,128)(2,1)S(1)} %bitcast.24, ...), custom_call_target="tpu_custom_call", output_to_operand_aliasing={{}: (4, {})} | custom-call | flops 196608 | bytes 928 | tf_op jit(solution)/shard_map/back/pallas_call | solution.py:37
  93.3 6.7 %collective-permute-done.10.refs_1_ = bf16[512,768]{1,0:T(8,128)(2,1)S(1)} collective-permute-done((bf16[512,768]{1,0:T(8,128)(2,1)}, bf16[512,768]{1,0:T(8,128)(2,1)S(1)}, u32[]{:S(2)}, u32[]{:S(2)}) %collective-permute-start.10) | collective-permute-done | bytes 786464 | tf_op jit(solution)/shard_map/ppermute | solution.py:257
  105.4 2.6 %back.12.refs_4_ = bf16[1,1,2048,1536]{3,2,1,0:T(8,128)(2,1)} custom-call(s32[8]{0:T(128)S(1)} %stack.62.order, bf16[256,1280]{1,0:T(8,128)(2,1)S(1)} %get-tuple-element.125.refs_0_.refs_4_, bf16[256,768]{1,0:T(8,128)(2,1)S(1)} %get-tuple-element.131.refs_1_.refs_4_, bf16[1,768,2048]{2,1,0:T(8,128)(2,1)S(1)} %copy-done.1, ...), custom_call_target="tpu_custom_call", output_to_operand_aliasing={{}: (5, {})} | custom-call | flops 196608 | bytes 928 | tf_op jit(solution)/shard_map/back/pallas_call | solution.py:37
  108.0 5.3 %base.2 = f32[768,1280]{1,0:T(8,128)S(1)} custom-call(bf16[768,2048]{1,0:T(8,128)(2,1)S(1)} %hidden.1.turned, bf16[256,2048]{1,0:T(8,128)(2,1)S(1)} %get-tuple-element.110.refs_0_, bf16[256,2048]{1,0:T(8,128)(2,1)} %collective-permute-done.6.refs_0_.refs_1_, bf16[256,2048]{1,0:T(8,128)(2,1)S(1)} %get-tuple-element.118.refs_0_.refs_2_, ...), custom_call_target="tpu_custom_call" | custom-call | flops 737280 | bytes 2496 | tf_op jit(solution)/shard_map/base/pallas_call | solution.py:37
  115.5 3.5 %base.3 = f32[768,768]{1,0:T(8,128)S(1)} custom-call(bf16[768,2048]{1,0:T(8,128)(2,1)S(1)} %hidden.1.turned, bf16[256,2048]{1,0:T(8,128)(2,1)S(1)} %get-tuple-element.110.refs_0_, bf16[256,2048]{1,0:T(8,128)(2,1)} %collective-permute-done.6.refs_0_.refs_1_, bf16[256,2048]{1,0:T(8,128)(2,1)S(1)} %get-tuple-element.118.refs_0_.refs_2_, ...), custom_call_target="tpu_custom_call" | custom-call | flops 442368 | bytes 1728 | tf_op jit(solution)/shard_map/base/pallas_call | solution.py:37
  124.6 3.1 %collective-permute-done.13.refs_1_ = bf16[512,768]{1,0:T(8,128)(2,1)S(1)} collective-permute-done((bf16[512,768]{1,0:T(8,128)(2,1)S(1)}, bf16[512,768]{1,0:T(8,128)(2,1)S(1)}, u32[]{:S(2)}, u32[]{:S(2)}) %collective-permute-start.13) | collective-permute-done | bytes 786464 | tf_op jit(solution)/shard_map/ppermute | solution.py:394
  132.0 4.2 %collective-permute-done.20.far = bf16[192,512]{1,0:T(8,128)(2,1)S(1)} collective-permute-done((bf16[192,512]{1,0:T(8,128)(2,1)S(1)}, bf16[192,512]{1,0:T(8,128)(2,1)S(1)}, u32[]{:S(2)}, u32[]{:S(2)}) %collective-permute-start.20) | collective-permute-done | bytes 196640 | tf_op jit(solution)/shard_map/ppermute | solution.py:509
  139.1 2.6 %back.13.refs_6_ = bf16[1,1,2048,1536]{3,2,1,0:T(8,128)(2,1)} custom-call(s32[8]{0:T(128)S(1)} %stack.62.order, bf16[256,1280]{1,0:T(8,128)(2,1)S(1)} %collective-permute-done.11.refs_5_.refs_0_, bf16[256,768]{1,0:T(8,128)(2,1)S(1)} %collective-permute-done.15.refs_5_.refs_1_, bf16[1,768,2048]{2,1,0:T(8,128)(2,1)S(1)} %copy-done.1, ...), custom_call_target="tpu_custom_call", output_to_operand_aliasing={{}: (5, {})} | custom-call | flops 196608 | bytes 928 | tf_op jit(solution)/shard_map/back/pallas_call | solution.py:37
  149.5 2.6 %back.14.refs_6_ = bf16[1,1,2048,1536]{3,2,1,0:T(8,128)(2,1)} custom-call(s32[8]{0:T(128)S(1)} %stack.62.order, bf16[256,512]{1,0:T(8,128)(2,1)S(1)} %get-tuple-element.139.mine.refs_0_, bf16[256,768]{1,0:T(8,128)(2,1)S(1)} %get-tuple-element.148.mine.refs_1_, bf16[256,512]{1,0:T(8,128)(2,1)S(1)} %get-tuple-element.167.refs_2_.mine, ...), custom_call_target="tpu_custom_call", output_to_operand_aliasing={{}: (7, {})} | custom-call | flops 196608 | bytes 928 | tf_op jit(solution)/shard_map/back/pallas_call | solution.py:37
  161.8 2.6 %back.15 = bf16[1,1,2048,1536]{3,2,1,0:T(8,128)(2,1)} custom-call(s32[8]{0:T(128)S(1)} %stack.62.order, bf16[256,512]{1,0:T(8,128)(2,1)S(1)} %collective-permute-done.14.got.refs_0_, bf16[256,768]{1,0:T(8,128)(2,1)S(1)} %collective-permute-done.18.got.refs_1_, ...), custom_call_target="tpu_custom_call", output_to_operand_aliasing={{}: (7, {})} | custom-call | flops 196608 | bytes 928 | tf_op jit(solution)/shard_map/back/pallas_call | solution.py:37
  177.9 4.6 %collective-permute-done.41.across = bf16[192,512]{1,0:T(8,128)(2,1)S(1)} collective-permute-done((bf16[192,512]{1,0:T(8,128)(2,1)S(1)}, bf16[192,512]{1,0:T(8,128)(2,1)S(1)}, u32[]{:S(2)}, u32[]{:S(2)}) %collective-permute-start.41) | collective-permute-done | bytes 196640 | tf_op jit(solution)/shard_map/ppermute | solution.py:519
  (129 shorter events, 82.8 us)
Async XLA Ops:
  3.6 33.9 %collective-permute-start = (bf16[528,1280]{1,0:T(8,128)(2,1)}, bf16[528,1280]{1,0:T(8,128)(2,1)}, u32[]{:S(2)}, u32[]{:S(2)}) collective-permute-start(bf16[528,1280]{1,0:T(8,128)(2,1)} %pack.1.refs_0_), channel_id=1, source_target_pairs={{0,8},{4,12},{8,0},{12,4},{16,24},{20,28},{24,16},{28,20},{1,9},{5... | collective-permute-start | bytes 4055048 | tf_op jit(solution)/shard_map/ppermute | solution.py:257
  6.7 30.8 %collective-permute-start.1 = (bf16[528,1280]{1,0:T(8,128)(2,1)}, bf16[528,1280]{1,0:T(8,128)(2,1)}, u32[]{:S(2)}, u32[]{:S(2)}) collective-permute-start(bf16[528,1280]{1,0:T(8,128)(2,1)} %pack.1.refs_0_), channel_id=1, source_target_pairs={{8,16},{16,8},{12,20},{20,12},{9,17},{17,9},{13,21},{21,13},{10,18... | collective-permute-start | bytes 4055048 | tf_op jit(solution)/shard_map/ppermute | solution.py:257
  18.9 24.9 %collective-permute-start.6 = (bf16[256,2048]{1,0:T(8,128)(2,1)}, bf16[256,2048]{1,0:T(8,128)(2,1)}, u32[]{:S(2)}, u32[]{:S(2)}) collective-permute-start(bf16[256,2048]{1,0:T(8,128)(2,1)} %get-tuple-element.115), channel_id=1, source_target_pairs={{0,4},{4,0},{8,12},{12,8},{16,20},{20,16},{24,28},{28,24},{1,5},{5... | collective-permute-start | bytes 3145736 | tf_op jit(solution)/shard_map/ppermute | solution.py:312
  20.4 33.9 %collective-permute-start.4 = (bf16[512,768]{1,0:T(8,128)(2,1)}, bf16[512,768]{1,0:T(8,128)(2,1)}, u32[]{:S(2)}, u32[]{:S(2)}) collective-permute-start(bf16[512,768]{1,0:T(8,128)(2,1)} %slice_bitcast_fusion.refs_1_), channel_id=1, source_target_pairs={{0,8},{4,12},{8,0},{12,4},{16,24},{20,28},{24,16},{28,20},{1,9},{5... | collective-permute-start | bytes 2359304 | tf_op jit(solution)/shard_map/ppermute | solution.py:257
  23.7 30.6 %collective-permute-start.5 = (bf16[512,768]{1,0:T(8,128)(2,1)}, bf16[512,768]{1,0:T(8,128)(2,1)}, u32[]{:S(2)}, u32[]{:S(2)}) collective-permute-start(bf16[512,768]{1,0:T(8,128)(2,1)} %slice_bitcast_fusion.refs_1_), channel_id=1, source_target_pairs={{8,16},{16,8},{12,20},{20,12},{9,17},{17,9},{13,21},{21,13},{10,18... | collective-permute-start | bytes 2359304 | tf_op jit(solution)/shard_map/ppermute | solution.py:257
  37.5 46.2 %collective-permute-start.2 = (bf16[528,1280]{1,0:T(8,128)(2,1)}, bf16[528,1280]{1,0:T(8,128)(2,1)S(1)}, u32[]{:S(2)}, u32[]{:S(2)}) collective-permute-start(bf16[528,1280]{1,0:T(8,128)(2,1)} %collective-permute-done.refs_0_), channel_id=1, source_target_pairs={{8,16},{16,8},{12,20},{20,12},{9,17},{17,9},{13,21},{21,13},{10,18... | collective-permute-start | bytes 4055048 | tf_op jit(solution)/shard_map/ppermute | solution.py:257
  38.2 45.4 %collective-permute-start.3 = (bf16[528,1280]{1,0:T(8,128)(2,1)}, bf16[528,1280]{1,0:T(8,128)(2,1)S(1)}, u32[]{:S(2)}, u32[]{:S(2)}) collective-permute-start(bf16[528,1280]{1,0:T(8,128)(2,1)} %collective-permute-done.1.refs_0_), channel_id=1, source_target_pairs={{16,24},{20,28},{8,0},{12,4},{17,25},{21,29},{9,1},{13,5},{18,26},... | collective-permute-start | bytes 4055048 | tf_op jit(solution)/shard_map/ppermute | solution.py:257
  60.1 23.6 %collective-permute-start.7 = (bf16[256,2048]{1,0:T(8,128)(2,1)S(1)}, bf16[256,2048]{1,0:T(8,128)(2,1)S(1)}, u32[]{:S(2)}, u32[]{:S(2)}) collective-permute-start(bf16[256,2048]{1,0:T(8,128)(2,1)S(1)} %get-tuple-element.120), channel_id=1, source_target_pairs={{0,4},{4,0},{8,12},{12,8},{16,20},{20,16},{24,28},{28,24},{1,5},{5... | collective-permute-start | bytes 3145736 | tf_op jit(solution)/shard_map/ppermute | solution.py:312
  62.1 37.9 %collective-permute-start.10 = (bf16[512,768]{1,0:T(8,128)(2,1)}, bf16[512,768]{1,0:T(8,128)(2,1)S(1)}, u32[]{:S(2)}, u32[]{:S(2)}) collective-permute-start(bf16[512,768]{1,0:T(8,128)(2,1)} %collective-permute-done.5.refs_0_), channel_id=1, source_target_pairs={{16,24},{20,28},{8,0},{12,4},{17,25},{21,29},{9,1},{13,5},{18,26},... | collective-permute-start | bytes 2359304 | tf_op jit(solution)/shard_map/ppermute | solution.py:257
  63.4 36.6 %collective-permute-start.9 = (bf16[512,768]{1,0:T(8,128)(2,1)}, bf16[512,768]{1,0:T(8,128)(2,1)S(1)}, u32[]{:S(2)}, u32[]{:S(2)}) collective-permute-start(bf16[512,768]{1,0:T(8,128)(2,1)} %collective-permute-done.4.refs_1_), channel_id=1, source_target_pairs={{8,16},{16,8},{12,20},{20,12},{9,17},{17,9},{13,21},{21,13},{10,18... | collective-permute-start | bytes 2359304 | tf_op jit(solution)/shard_map/ppermute | solution.py:257
  87.8 20.2 %collective-permute-start.11 = (bf16[256,1280]{1,0:T(8,128)(2,1)S(1)}, bf16[256,1280]{1,0:T(8,128)(2,1)S(1)}, u32[]{:S(2)}, u32[]{:S(2)}) collective-permute-start(bf16[256,1280]{1,0:T(8,128)(2,1)S(1)} %get-tuple-element.129), channel_id=1, source_target_pairs={{0,4},{4,0},{8,12},{12,8},{16,20},{20,16},{24,28},{28,24},{1,5},{5... | collective-permute-start | bytes 1966088 | tf_op jit(solution)/shard_map/ppermute | solution.py:312
  89.4 23.9 %collective-permute-start.8 = (bf16[528,512]{1,0:T(8,128)(2,1)S(1)}, bf16[528,512]{1,0:T(8,128)(2,1)S(1)}, u32[]{:S(2)}, u32[]{:S(2)}) collective-permute-start(bf16[528,512]{1,0:T(8,128)(2,1)S(1)} %slice.10), channel_id=1, source_target_pairs={{16,24},{20,28},{8,0},{12,4},{17,25},{21,29},{9,1},{13,5},{18,26},... | collective-permute-start | bytes 1622024 | tf_op jit(solution)/shard_map/ppermute | solution.py:394
  101.8 13.6 %collective-permute-start.15 = (bf16[256,768]{1,0:T(8,128)(2,1)S(1)}, bf16[256,768]{1,0:T(8,128)(2,1)S(1)}, u32[]{:S(2)}, u32[]{:S(2)}) collective-permute-start(bf16[256,768]{1,0:T(8,128)(2,1)S(1)} %get-tuple-element.141), channel_id=1, source_target_pairs={{0,4},{4,0},{8,12},{12,8},{16,20},{20,16},{24,28},{28,24},{1,5},{5... | collective-permute-start | bytes 1179656 | tf_op jit(solution)/shard_map/ppermute | solution.py:312
  103.9 23.7 %collective-permute-start.13 = (bf16[512,768]{1,0:T(8,128)(2,1)S(1)}, bf16[512,768]{1,0:T(8,128)(2,1)S(1)}, u32[]{:S(2)}, u32[]{:S(2)}) collective-permute-start(bf16[512,768]{1,0:T(8,128)(2,1)S(1)} %slice.11), channel_id=1, source_target_pairs={{16,24},{20,28},{8,0},{12,4},{17,25},{21,29},{9,1},{13,5},{18,26},... | collective-permute-start | bytes 2359304 | tf_op jit(solution)/shard_map/ppermute | solution.py:394
  123.2 23.1 %collective-permute-start.12 = (bf16[512,768]{1,0:T(8,128)(2,1)S(1)}, bf16[512,768]{1,0:T(8,128)(2,1)S(1)}, u32[]{:S(2)}, u32[]{:S(2)}) collective-permute-start(bf16[512,768]{1,0:T(8,128)(2,1)S(1)} %collective-permute-done.9.refs_0_), channel_id=1, source_target_pairs={{16,24},{20,28},{8,0},{12,4},{17,25},{21,29},{9,1},{13,5},{18,26},... | collective-permute-start | bytes 2359304 | tf_op jit(solution)/shard_map/ppermute | solution.py:394
  128.8 12.9 %collective-permute-start.18 = (bf16[256,768]{1,0:T(8,128)(2,1)S(1)}, bf16[256,768]{1,0:T(8,128)(2,1)S(1)}, u32[]{:S(2)}, u32[]{:S(2)}) collective-permute-start(bf16[256,768]{1,0:T(8,128)(2,1)S(1)} %get-tuple-element.149), channel_id=1, source_target_pairs={{0,4},{4,0},{8,12},{12,8},{16,20},{20,16},{24,28},{28,24},{1,5},{5... | collective-permute-start | bytes 1179656 | tf_op jit(solution)/shard_map/ppermute | solution.py:312
  144.0 10.4 %collective-permute-start.27 = (bf16[192,768]{1,0:T(8,128)(2,1)S(1)}, bf16[192,768]{1,0:T(8,128)(2,1)S(1)}, u32[]{:S(2)}, u32[]{:S(2)}) collective-permute-start(bf16[192,768]{1,0:T(8,128)(2,1)S(1)} %get-tuple-element.166), channel_id=1, source_target_pairs={{0,1},{1,0},{2,3},{3,2},{4,5},{5,4},{6,7},{7,6},{8,9},{9,8},{10,11... | collective-permute-start | bytes 884744 | tf_op jit(solution)/shard_map/ppermute | solution.py:496
  145.3 9.1 %collective-permute-start.28 = (bf16[192,768]{1,0:T(8,128)(2,1)S(1)}, bf16[192,768]{1,0:T(8,128)(2,1)S(1)}, u32[]{:S(2)}, u32[]{:S(2)}) collective-permute-start(bf16[192,768]{1,0:T(8,128)(2,1)S(1)} %add_convert_fusion), channel_id=1, source_target_pairs={{0,2},{1,3},{2,0},{3,1},{4,6},{5,7},{6,4},{7,5},{8,10},{9,11},{10,... | collective-permute-start | bytes 884744 | tf_op jit(solution)/shard_map/ppermute | solution.py:509
  147.0 10.6 %collective-permute-start.25 = (bf16[256,512]{1,0:T(8,128)(2,1)S(1)}, bf16[256,512]{1,0:T(8,128)(2,1)S(1)}, u32[]{:S(2)}, u32[]{:S(2)}) collective-permute-start(bf16[256,512]{1,0:T(8,128)(2,1)S(1)} %get-tuple-element.163), channel_id=1, source_target_pairs={{0,4},{4,0},{8,12},{12,8},{16,20},{20,16},{24,28},{28,24},{1,5},{5... | collective-permute-start | bytes 786440 | tf_op jit(solution)/shard_map/ppermute | solution.py:312
  147.9 9.7 %collective-permute-start.26 = (bf16[256,256]{1,0:T(8,128)(2,1)S(1)}, bf16[256,256]{1,0:T(8,128)(2,1)S(1)}, u32[]{:S(2)}, u32[]{:S(2)}) collective-permute-start(bf16[256,256]{1,0:T(8,128)(2,1)S(1)} %get-tuple-element.164), channel_id=1, source_target_pairs={{0,4},{4,0},{8,12},{12,8},{16,20},{20,16},{24,28},{28,24},{1,5},{5... | collective-permute-start | bytes 393224 | tf_op jit(solution)/shard_map/ppermute | solution.py:312
  157.7 7.6 %collective-permute-start.29 = (bf16[192,768]{1,0:T(8,128)(2,1)S(1)}, bf16[192,768]{1,0:T(8,128)(2,1)S(1)}, u32[]{:S(2)}, u32[]{:S(2)}) collective-permute-start(bf16[192,768]{1,0:T(8,128)(2,1)S(1)} %get-tuple-element.174.own), channel_id=1, source_target_pairs={{0,2},{1,3},{2,0},{3,1},{4,6},{5,7},{6,4},{7,5},{8,10},{9,11},{10,... | collective-permute-start | bytes 884744 | tf_op jit(solution)/shard_map/ppermute | solution.py:519
  165.4 7.8 %collective-permute-start.33 = (bf16[192,512]{1,0:T(8,128)(2,1)S(1)}, bf16[192,512]{1,0:T(8,128)(2,1)S(1)}, u32[]{:S(2)}, u32[]{:S(2)}) collective-permute-start(bf16[192,512]{1,0:T(8,128)(2,1)S(1)} %add_convert_fusion.1), channel_id=1, source_target_pairs={{0,2},{1,3},{2,0},{3,1},{4,6},{5,7},{6,4},{7,5},{8,10},{9,11},{10,... | collective-permute-start | bytes 589832 | tf_op jit(solution)/shard_map/ppermute | solution.py:509
  167.2 7.7 %collective-permute-start.38 = (bf16[192,256]{1,0:T(8,128)(2,1)S(1)}, bf16[192,256]{1,0:T(8,128)(2,1)S(1)}, u32[]{:S(2)}, u32[]{:S(2)}) collective-permute-start(bf16[192,256]{1,0:T(8,128)(2,1)S(1)} %add_convert_fusion.3), channel_id=1, source_target_pairs={{0,2},{1,3},{2,0},{3,1},{4,6},{5,7},{6,4},{7,5},{8,10},{9,11},{10,... | collective-permute-start | bytes 294920 | tf_op jit(solution)/shard_map/ppermute | solution.py:509
  174.9 7.6 %collective-permute-start.41 = (bf16[192,512]{1,0:T(8,128)(2,1)S(1)}, bf16[192,512]{1,0:T(8,128)(2,1)S(1)}, u32[]{:S(2)}, u32[]{:S(2)}) collective-permute-start(bf16[192,512]{1,0:T(8,128)(2,1)S(1)} %get-tuple-element.206.own), channel_id=1, source_target_pairs={{0,2},{1,3},{2,0},{3,1},{4,6},{5,7},{6,4},{7,5},{8,10},{9,11},{10,... | collective-permute-start | bytes 589832 | tf_op jit(solution)/shard_map/ppermute | solution.py:519
  (27 other events, 141.4 us)

commit v6 on v5

--- a/solution.py
+++ b/solution.py
@@ -207,6 +207,19 @@
     put(2, across[...])
     put(1, sibling[:rows, :])
     put(0, sibling[rows:, :])
+
+
+def assemble_last(places, *refs):
+    out = refs[-1]
+    late = pl.program_id(0) == pl.num_programs(0) - 1
+
+    def put(own, across, sibling):
+        rows = own.shape[0]
+        for g, value in ((3, own[...]), (2, across[...]), (1, sibling[:rows, :]), (0, sibling[rows:, :])):
+            out[0, pl.ds(pl.multiple_of(places[g] * rows, 16), rows), :] = value
+
+    pl.when(jnp.logical_not(late))(lambda: put(*refs[:3]))
+    pl.when(late)(lambda: put(*refs[3:6]))
 
 
 def line_body(cotangent, routing, route_weight, saved_preact, weight, master, moment1, moment2):
@@ -588,8 +601,23 @@
     gather_x(3, None)
     gather_core(2, None)
     gather_core(3, None)
-    gathered(2, None)
-    gathered(3, None)
+    start, count = chunks[2][0] // TILE, chunks[2][1] // TILE
+    early = lambda i, g: (0, jnp.minimum(i, count - 1))
+    fixed = lambda i, g: (0, 0)
+    sizes = (rows, rows, 2 * rows)
+    last_weight = call(
+        assemble_last,
+        "assemble",
+        (count + 1,),
+        (groups,),
+        (freshes[2], crosseds[2], siblings[2], freshes[3], crosseds[3], siblings[3], next_weight[0]),
+        [pl.BlockSpec((n, TILE), early) for n in sizes] + [pl.BlockSpec((n, TILE), fixed) for n in sizes] + [ANY],
+        shape((1, hidden_width, width), jnp.bfloat16),
+        pl.BlockSpec((1, hidden_width, TILE), lambda i, g: (0, 0, start + i)),
+        aliases={6: 0},
+        moved=16 * rows * TILE * (count + 1),
+    )
+    next_weight = (last_weight,)
     return (grad_preact, next_weight[0], *states)
 
 

time: 188 us -> 188 us (level)
    pallas_call x36 -> x35, Pallas kernels: 77.7 us -> 77.1 us  [call(): pl.pallas_call(kernel, name=name, grid_spec=pltpu.PrefetchScalarGridSpec(...]
  transfers between devices with their start and end apart: 43 -> 43, of which waited for: 20 -> 20; matrix products, arithmetic and copies ran while one was open for 2% -> 2% of each run, Pallas kernels for 39% -> 38%
where the time goes in v6:
time: 188 us; the launch traced here: 187 us
  Pallas kernels  77.1 us (41%)
  waiting for transfers between devices  60.4 us (32%)
  starting transfers between devices  41.8 us (22%)
  local copies, waits for them, and re-layouts  6.54 us (3%)
    pallas_call x35, Pallas kernels, call(): pl.pallas_call(kernel, name=name, grid_spec=pltpu.PrefetchScalarGridSpec(...  77.1 us
    ppermute x8, waiting for transfers between devices, pick(): return (mine, other, lax.ppermute(other, 'expert', swap_y))  23.2 us
    ppermute x8, waiting for transfers between devices, permuted(): return [lax.ppermute(p, 'expert', way) for p in parts]  16.8 us
    ppermute x8, starting transfers between devices, permuted(): return [lax.ppermute(p, 'expert', way) for p in parts]  13.8 us
    ppermute x8, starting transfers between devices, pick(): return (mine, other, lax.ppermute(other, 'expert', swap_y))  11.5 us
    ppermute x4, waiting for transfers between devices, sum_x(): fars[c] = lax.ppermute(acrosses[c], 'dp', swap_x)  8.53 us
    ppermute x4, waiting for transfers between devices, gather_x(): crosseds[k] = lax.ppermute(freshes[k], 'dp', swap_x)  6.21 us
    ppermute x4, starting transfers between devices, gather_x(): crosseds[k] = lax.ppermute(freshes[k], 'dp', swap_x)  5.01 us
  transfers between devices with their start and end apart: 43, of which 20 were waited for; matrix products, arithmetic and copies ran while one was open for 2% of the time, Pallas kernels for 38%

profile of v6, /device:TPU:0, one launch (start us, length us, event | category | flops | bytes accessed | tf_op | source)
XLA Modules:
  0.0 187.3 jit_solution(2004310820830938797)
XLA Ops:
  0.6 2.9 %pack.1.refs_0_ = bf16[528,1280]{1,0:T(8,128)(2,1)} custom-call(bf16[1,512,2048]{2,1,0:T(8,128)(2,1)} %tokens.1, s32[2,512]{1,0:T(2,128)} %bitcast.25, f32[2,512]{1,0:T(2,128)} %bitcast.26), custom_call_target="tpu_custom_call" | custom-call | bytes 1024 | tf_op jit(solution)/shard_map/pack/pallas_call | solution.py:37
  3.6 3.1 %collective-permute-start = (bf16[528,1280]{1,0:T(8,128)(2,1)}, bf16[528,1280]{1,0:T(8,128)(2,1)}, u32[]{:S(2)}, u32[]{:S(2)}) collective-permute-start(bf16[528,1280]{1,0:T(8,128)(2,1)} %pack.1.refs_0_), channel_id=1, source_target_pairs={{0,8},{4,12},{8,0},{12,4},{16,24},{20,28},{24,16},{28,20},{1,9},{5... | collective-permute-start | bytes 4055048 | tf_op jit(solution)/shard_map/ppermute | solution.py:270
  13.0 5.9 %pick.8 = (bf16[256,2048]{1,0:T(8,128)(2,1)S(1)}, bf16[256,2048]{1,0:T(8,128)(2,1)}) custom-call(s32[1]{0:T(128)} %bitcast.middle, bf16[512,512]{1,0:T(8,128)(2,1)S(1)} %get-tuple-element.108.picks, f32[512,1]{1,0:T(8,128)S(1)} %get-tuple-element.109.scales, bf16[528,1280]{1,0:T(8,128)(2,1)S(1)} %copy-done.5, bf16[512,768]{1,0:T(8,128)(2,1)} %slice_bitcast_fusion.refs_1_), custom_call_target="tpu_custom_call" | custom-call | flops 262144 | bytes 1536 | tf_op jit(solution)/shard_map/pick/pallas_call | solution.py:37
  20.4 3.3 %collective-permute-start.4 = (bf16[512,768]{1,0:T(8,128)(2,1)}, bf16[512,768]{1,0:T(8,128)(2,1)}, u32[]{:S(2)}, u32[]{:S(2)}) collective-permute-start(bf16[512,768]{1,0:T(8,128)(2,1)} %slice_bitcast_fusion.refs_1_), channel_id=1, source_target_pairs={{0,8},{4,12},{8,0},{12,4},{16,24},{20,28},{24,16},{28,20},{1,9},{5... | collective-permute-start | bytes 2359304 | tf_op jit(solution)/shard_map/ppermute | solution.py:270
  25.4 2.8 %copy-done = bf16[1,1,2048,1536]{3,2,1,0:T(8,128)(2,1)S(1)} copy-done((bf16[1,1,2048,1536]{3,2,1,0:T(8,128)(2,1)S(1)}, bf16[1,1,2048,1536]{3,2,1,0:T(8,128)(2,1)}, u32[]{:S(2)}) %copy-start) | copy-done | bytes 6291480
  28.2 3.2 %hidden.1.turned = bf16[768,2048]{1,0:T(8,128)(2,1)S(1)} custom-call(s32[8]{0:T(128)S(1)} %stack.62.order, s32[4]{0:T(128)S(1)} %pad_add_fusion.1.groups.places, bf16[1,1,2048,1536]{3,2,1,0:T(8,128)(2,1)S(1)} %copy-done), custom_call_target="tpu_custom_call" | custom-call | flops 15360 | bytes 3456 | tf_op jit(solution)/shard_map/hidden/pallas_call | solution.py:37
  34.1 3.3 %collective-permute-done.refs_0_ = bf16[528,1280]{1,0:T(8,128)(2,1)} collective-permute-done((bf16[528,1280]{1,0:T(8,128)(2,1)}, bf16[528,1280]{1,0:T(8,128)(2,1)}, u32[]{:S(2)}, u32[]{:S(2)}) %collective-permute-start) | collective-permute-done | bytes 1351712 | tf_op jit(solution)/shard_map/ppermute | solution.py:270
  41.2 2.6 %collective-permute-done.6.refs_0_.refs_1_ = bf16[256,2048]{1,0:T(8,128)(2,1)} collective-permute-done((bf16[256,2048]{1,0:T(8,128)(2,1)}, bf16[256,2048]{1,0:T(8,128)(2,1)}, u32[]{:S(2)}, u32[]{:S(2)}) %collective-permute-start.6) | collective-permute-done | bytes 1048608 | tf_op jit(solution)/shard_map/ppermute | solution.py:325
  43.8 3.8 %back.9.refs_3_ = bf16[1,1,2048,1536]{3,2,1,0:T(8,128)(2,1)} custom-call(s32[8]{0:T(128)S(1)} %stack.62.order, bf16[256,2048]{1,0:T(8,128)(2,1)} %collective-permute-done.6.refs_0_.refs_1_, bf16[1,768,2048]{2,1,0:T(8,128)(2,1)S(1)} %copy-done.1, bf16[1,1,2048,1536]{3,2,1,0:T(8,128)(2,1)S(1)} %bitcast.24, ...), custom_call_target="tpu_custom_call", output_to_operand_aliasing={{}: (4, {})} | custom-call | flops 196608 | bytes 928 | tf_op jit(solution)/shard_map/back/pallas_call | solution.py:37
  47.6 6.7 %collective-permute-done.4.refs_1_ = bf16[512,768]{1,0:T(8,128)(2,1)} collective-permute-done((bf16[512,768]{1,0:T(8,128)(2,1)}, bf16[512,768]{1,0:T(8,128)(2,1)}, u32[]{:S(2)}, u32[]{:S(2)}) %collective-permute-start.4) | collective-permute-done | bytes 786464 | tf_op jit(solution)/shard_map/ppermute | solution.py:270
  54.3 5.7 %pick.9 = (bf16[256,2048]{1,0:T(8,128)(2,1)S(1)}, bf16[256,2048]{1,0:T(8,128)(2,1)S(1)}) custom-call(s32[1]{0:T(128)} %bitcast.middle, bf16[512,512]{1,0:T(8,128)(2,1)S(1)} %get-tuple-element.113.picks, f32[512,1]{1,0:T(8,128)S(1)} %get-tuple-element.114.scales, bf16[528,1280]{1,0:T(8,128)(2,1)} %collective-permute-done.refs_0_, ...), custom_call_target="tpu_custom_call" | custom-call | flops 262144 | bytes 1536 | tf_op jit(solution)/shard_map/pick/pallas_call | solution.py:37
  64.1 2.6 %back.10.refs_3_ = bf16[1,1,2048,1536]{3,2,1,0:T(8,128)(2,1)} custom-call(s32[8]{0:T(128)S(1)} %stack.62.order, bf16[256,2048]{1,0:T(8,128)(2,1)S(1)} %get-tuple-element.118.refs_0_.refs_2_, bf16[1,768,2048]{2,1,0:T(8,128)(2,1)S(1)} %copy-done.1, bf16[1,1,2048,1536]{3,2,1,0:T(8,128)(2,1)S(1)} %bitcast.24, ...), custom_call_target="tpu_custom_call", output_to_operand_aliasing={{}: (4, {})} | custom-call | flops 196608 | bytes 928 | tf_op jit(solution)/shard_map/back/pallas_call | solution.py:37
  66.7 16.9 %collective-permute-done.7.refs_0_.refs_3_ = bf16[256,2048]{1,0:T(8,128)(2,1)S(1)} collective-permute-done((bf16[256,2048]{1,0:T(8,128)(2,1)S(1)}, bf16[256,2048]{1,0:T(8,128)(2,1)S(1)}, u32[]{:S(2)}, u32[]{:S(2)}) %collective-permute-start.7) | collective-permute-done | bytes 1048608 | tf_op jit(solution)/shard_map/ppermute | solution.py:325
  90.7 2.6 %back.11.refs_4_ = bf16[1,1,2048,1536]{3,2,1,0:T(8,128)(2,1)} custom-call(s32[8]{0:T(128)S(1)} %stack.62.order, bf16[256,2048]{1,0:T(8,128)(2,1)S(1)} %collective-permute-done.7.refs_0_.refs_3_, bf16[1,768,2048]{2,1,0:T(8,128)(2,1)S(1)} %copy-done.1, bf16[1,1,2048,1536]{3,2,1,0:T(8,128)(2,1)S(1)} %bitcast.24, ...), custom_call_target="tpu_custom_call", output_to_operand_aliasing={{}: (4, {})} | custom-call | flops 196608 | bytes 928 | tf_op jit(solution)/shard_map/back/pallas_call | solution.py:37
  93.3 6.7 %collective-permute-done.10.refs_1_ = bf16[512,768]{1,0:T(8,128)(2,1)S(1)} collective-permute-done((bf16[512,768]{1,0:T(8,128)(2,1)}, bf16[512,768]{1,0:T(8,128)(2,1)S(1)}, u32[]{:S(2)}, u32[]{:S(2)}) %collective-permute-start.10) | collective-permute-done | bytes 786464 | tf_op jit(solution)/shard_map/ppermute | solution.py:270
  105.4 2.6 %back.12.refs_4_ = bf16[1,1,2048,1536]{3,2,1,0:T(8,128)(2,1)} custom-call(s32[8]{0:T(128)S(1)} %stack.62.order, bf16[256,1280]{1,0:T(8,128)(2,1)S(1)} %get-tuple-element.125.refs_0_.refs_4_, bf16[256,768]{1,0:T(8,128)(2,1)S(1)} %get-tuple-element.131.refs_1_.refs_4_, bf16[1,768,2048]{2,1,0:T(8,128)(2,1)S(1)} %copy-done.1, ...), custom_call_target="tpu_custom_call", output_to_operand_aliasing={{}: (5, {})} | custom-call | flops 196608 | bytes 928 | tf_op jit(solution)/shard_map/back/pallas_call | solution.py:37
  108.0 5.3 %base.2 = f32[768,1280]{1,0:T(8,128)S(1)} custom-call(bf16[768,2048]{1,0:T(8,128)(2,1)S(1)} %hidden.1.turned, bf16[256,2048]{1,0:T(8,128)(2,1)S(1)} %get-tuple-element.110.refs_0_, bf16[256,2048]{1,0:T(8,128)(2,1)} %collective-permute-done.6.refs_0_.refs_1_, bf16[256,2048]{1,0:T(8,128)(2,1)S(1)} %get-tuple-element.118.refs_0_.refs_2_, ...), custom_call_target="tpu_custom_call" | custom-call | flops 737280 | bytes 2496 | tf_op jit(solution)/shard_map/base/pallas_call | solution.py:37
  115.5 3.5 %base.3 = f32[768,768]{1,0:T(8,128)S(1)} custom-call(bf16[768,2048]{1,0:T(8,128)(2,1)S(1)} %hidden.1.turned, bf16[256,2048]{1,0:T(8,128)(2,1)S(1)} %get-tuple-element.110.refs_0_, bf16[256,2048]{1,0:T(8,128)(2,1)} %collective-permute-done.6.refs_0_.refs_1_, bf16[256,2048]{1,0:T(8,128)(2,1)S(1)} %get-tuple-element.118.refs_0_.refs_2_, ...), custom_call_target="tpu_custom_call" | custom-call | flops 442368 | bytes 1728 | tf_op jit(solution)/shard_map/base/pallas_call | solution.py:37
  124.6 3.1 %collective-permute-done.13.refs_1_ = bf16[512,768]{1,0:T(8,128)(2,1)S(1)} collective-permute-done((bf16[512,768]{1,0:T(8,128)(2,1)S(1)}, bf16[512,768]{1,0:T(8,128)(2,1)S(1)}, u32[]{:S(2)}, u32[]{:S(2)}) %collective-permute-start.13) | collective-permute-done | bytes 786464 | tf_op jit(solution)/shard_map/ppermute | solution.py:407
  132.0 4.2 %collective-permute-done.20.far = bf16[192,512]{1,0:T(8,128)(2,1)S(1)} collective-permute-done((bf16[192,512]{1,0:T(8,128)(2,1)S(1)}, bf16[192,512]{1,0:T(8,128)(2,1)S(1)}, u32[]{:S(2)}, u32[]{:S(2)}) %collective-permute-start.20) | collective-permute-done | bytes 196640 | tf_op jit(solution)/shard_map/ppermute | solution.py:522
  139.1 2.6 %back.13.refs_6_ = bf16[1,1,2048,1536]{3,2,1,0:T(8,128)(2,1)} custom-call(s32[8]{0:T(128)S(1)} %stack.62.order, bf16[256,1280]{1,0:T(8,128)(2,1)S(1)} %collective-permute-done.11.refs_5_.refs_0_, bf16[256,768]{1,0:T(8,128)(2,1)S(1)} %collective-permute-done.15.refs_5_.refs_1_, bf16[1,768,2048]{2,1,0:T(8,128)(2,1)S(1)} %copy-done.1, ...), custom_call_target="tpu_custom_call", output_to_operand_aliasing={{}: (5, {})} | custom-call | flops 196608 | bytes 928 | tf_op jit(solution)/shard_map/back/pallas_call | solution.py:37
  149.5 2.6 %back.14.refs_6_ = bf16[1,1,2048,1536]{3,2,1,0:T(8,128)(2,1)} custom-call(s32[8]{0:T(128)S(1)} %stack.62.order, bf16[256,512]{1,0:T(8,128)(2,1)S(1)} %get-tuple-element.139.mine.refs_0_, bf16[256,768]{1,0:T(8,128)(2,1)S(1)} %get-tuple-element.148.mine.refs_1_, bf16[256,512]{1,0:T(8,128)(2,1)S(1)} %get-tuple-element.167.refs_2_.mine, ...), custom_call_target="tpu_custom_call", output_to_operand_aliasing={{}: (7, {})} | custom-call | flops 196608 | bytes 928 | tf_op jit(solution)/shard_map/back/pallas_call | solution.py:37
  161.8 2.6 %back.15 = bf16[1,1,2048,1536]{3,2,1,0:T(8,128)(2,1)} custom-call(s32[8]{0:T(128)S(1)} %stack.62.order, bf16[256,512]{1,0:T(8,128)(2,1)S(1)} %collective-permute-done.14.got.refs_0_, bf16[256,768]{1,0:T(8,128)(2,1)S(1)} %collective-permute-done.18.got.refs_1_, ...), custom_call_target="tpu_custom_call", output_to_operand_aliasing={{}: (7, {})} | custom-call | flops 196608 | bytes 928 | tf_op jit(solution)/shard_map/back/pallas_call | solution.py:37
  177.9 4.6 %collective-permute-done.39.refs_1_ = bf16[192,512]{1,0:T(8,128)(2,1)S(1)} collective-permute-done((bf16[192,512]{1,0:T(8,128)(2,1)S(1)}, bf16[192,512]{1,0:T(8,128)(2,1)S(1)}, u32[]{:S(2)}, u32[]{:S(2)}) %collective-permute-start.39) | collective-permute-done | bytes 196640 | tf_op jit(solution)/shard_map/ppermute | solution.py:532
  (128 shorter events, 82.9 us)
Async XLA Ops:
  3.6 33.9 %collective-permute-start = (bf16[528,1280]{1,0:T(8,128)(2,1)}, bf16[528,1280]{1,0:T(8,128)(2,1)}, u32[]{:S(2)}, u32[]{:S(2)}) collective-permute-start(bf16[528,1280]{1,0:T(8,128)(2,1)} %pack.1.refs_0_), channel_id=1, source_target_pairs={{0,8},{4,12},{8,0},{12,4},{16,24},{20,28},{24,16},{28,20},{1,9},{5... | collective-permute-start | bytes 4055048 | tf_op jit(solution)/shard_map/ppermute | solution.py:270
  6.7 30.8 %collective-permute-start.1 = (bf16[528,1280]{1,0:T(8,128)(2,1)}, bf16[528,1280]{1,0:T(8,128)(2,1)}, u32[]{:S(2)}, u32[]{:S(2)}) collective-permute-start(bf16[528,1280]{1,0:T(8,128)(2,1)} %pack.1.refs_0_), channel_id=1, source_target_pairs={{8,16},{16,8},{12,20},{20,12},{9,17},{17,9},{13,21},{21,13},{10,18... | collective-permute-start | bytes 4055048 | tf_op jit(solution)/shard_map/ppermute | solution.py:270
  18.9 24.9 %collective-permute-start.6 = (bf16[256,2048]{1,0:T(8,128)(2,1)}, bf16[256,2048]{1,0:T(8,128)(2,1)}, u32[]{:S(2)}, u32[]{:S(2)}) collective-permute-start(bf16[256,2048]{1,0:T(8,128)(2,1)} %get-tuple-element.115), channel_id=1, source_target_pairs={{0,4},{4,0},{8,12},{12,8},{16,20},{20,16},{24,28},{28,24},{1,5},{5... | collective-permute-start | bytes 3145736 | tf_op jit(solution)/shard_map/ppermute | solution.py:325
  20.4 33.9 %collective-permute-start.4 = (bf16[512,768]{1,0:T(8,128)(2,1)}, bf16[512,768]{1,0:T(8,128)(2,1)}, u32[]{:S(2)}, u32[]{:S(2)}) collective-permute-start(bf16[512,768]{1,0:T(8,128)(2,1)} %slice_bitcast_fusion.refs_1_), channel_id=1, source_target_pairs={{0,8},{4,12},{8,0},{12,4},{16,24},{20,28},{24,16},{28,20},{1,9},{5... | collective-permute-start | bytes 2359304 | tf_op jit(solution)/shard_map/ppermute | solution.py:270
  23.7 30.6 %collective-permute-start.5 = (bf16[512,768]{1,0:T(8,128)(2,1)}, bf16[512,768]{1,0:T(8,128)(2,1)}, u32[]{:S(2)}, u32[]{:S(2)}) collective-permute-start(bf16[512,768]{1,0:T(8,128)(2,1)} %slice_bitcast_fusion.refs_1_), channel_id=1, source_target_pairs={{8,16},{16,8},{12,20},{20,12},{9,17},{17,9},{13,21},{21,13},{10,18... | collective-permute-start | bytes 2359304 | tf_op jit(solution)/shard_map/ppermute | solution.py:270
  37.5 46.2 %collective-permute-start.2 = (bf16[528,1280]{1,0:T(8,128)(2,1)}, bf16[528,1280]{1,0:T(8,128)(2,1)S(1)}, u32[]{:S(2)}, u32[]{:S(2)}) collective-permute-start(bf16[528,1280]{1,0:T(8,128)(2,1)} %collective-permute-done.refs_0_), channel_id=1, source_target_pairs={{8,16},{16,8},{12,20},{20,12},{9,17},{17,9},{13,21},{21,13},{10,18... | collective-permute-start | bytes 4055048 | tf_op jit(solution)/shard_map/ppermute | solution.py:270
  38.2 45.4 %collective-permute-start.3 = (bf16[528,1280]{1,0:T(8,128)(2,1)}, bf16[528,1280]{1,0:T(8,128)(2,1)S(1)}, u32[]{:S(2)}, u32[]{:S(2)}) collective-permute-start(bf16[528,1280]{1,0:T(8,128)(2,1)} %collective-permute-done.1.refs_0_), channel_id=1, source_target_pairs={{16,24},{20,28},{8,0},{12,4},{17,25},{21,29},{9,1},{13,5},{18,26},... | collective-permute-start | bytes 4055048 | tf_op jit(solution)/shard_map/ppermute | solution.py:270
  60.1 23.6 %collective-permute-start.7 = (bf16[256,2048]{1,0:T(8,128)(2,1)S(1)}, bf16[256,2048]{1,0:T(8,128)(2,1)S(1)}, u32[]{:S(2)}, u32[]{:S(2)}) collective-permute-start(bf16[256,2048]{1,0:T(8,128)(2,1)S(1)} %get-tuple-element.120), channel_id=1, source_target_pairs={{0,4},{4,0},{8,12},{12,8},{16,20},{20,16},{24,28},{28,24},{1,5},{5... | collective-permute-start | bytes 3145736 | tf_op jit(solution)/shard_map/ppermute | solution.py:325
  62.1 37.9 %collective-permute-start.10 = (bf16[512,768]{1,0:T(8,128)(2,1)}, bf16[512,768]{1,0:T(8,128)(2,1)S(1)}, u32[]{:S(2)}, u32[]{:S(2)}) collective-permute-start(bf16[512,768]{1,0:T(8,128)(2,1)} %collective-permute-done.5.refs_0_), channel_id=1, source_target_pairs={{16,24},{20,28},{8,0},{12,4},{17,25},{21,29},{9,1},{13,5},{18,26},... | collective-permute-start | bytes 2359304 | tf_op jit(solution)/shard_map/ppermute | solution.py:270
  63.4 36.6 %collective-permute-start.9 = (bf16[512,768]{1,0:T(8,128)(2,1)}, bf16[512,768]{1,0:T(8,128)(2,1)S(1)}, u32[]{:S(2)}, u32[]{:S(2)}) collective-permute-start(bf16[512,768]{1,0:T(8,128)(2,1)} %collective-permute-done.4.refs_1_), channel_id=1, source_target_pairs={{8,16},{16,8},{12,20},{20,12},{9,17},{17,9},{13,21},{21,13},{10,18... | collective-permute-start | bytes 2359304 | tf_op jit(solution)/shard_map/ppermute | solution.py:270
  87.8 20.2 %collective-permute-start.11 = (bf16[256,1280]{1,0:T(8,128)(2,1)S(1)}, bf16[256,1280]{1,0:T(8,128)(2,1)S(1)}, u32[]{:S(2)}, u32[]{:S(2)}) collective-permute-start(bf16[256,1280]{1,0:T(8,128)(2,1)S(1)} %get-tuple-element.129), channel_id=1, source_target_pairs={{0,4},{4,0},{8,12},{12,8},{16,20},{20,16},{24,28},{28,24},{1,5},{5... | collective-permute-start | bytes 1966088 | tf_op jit(solution)/shard_map/ppermute | solution.py:325
  89.4 23.9 %collective-permute-start.8 = (bf16[528,512]{1,0:T(8,128)(2,1)S(1)}, bf16[528,512]{1,0:T(8,128)(2,1)S(1)}, u32[]{:S(2)}, u32[]{:S(2)}) collective-permute-start(bf16[528,512]{1,0:T(8,128)(2,1)S(1)} %slice.10), channel_id=1, source_target_pairs={{16,24},{20,28},{8,0},{12,4},{17,25},{21,29},{9,1},{13,5},{18,26},... | collective-permute-start | bytes 1622024 | tf_op jit(solution)/shard_map/ppermute | solution.py:407
  101.8 13.6 %collective-permute-start.15 = (bf16[256,768]{1,0:T(8,128)(2,1)S(1)}, bf16[256,768]{1,0:T(8,128)(2,1)S(1)}, u32[]{:S(2)}, u32[]{:S(2)}) collective-permute-start(bf16[256,768]{1,0:T(8,128)(2,1)S(1)} %get-tuple-element.141), channel_id=1, source_target_pairs={{0,4},{4,0},{8,12},{12,8},{16,20},{20,16},{24,28},{28,24},{1,5},{5... | collective-permute-start | bytes 1179656 | tf_op jit(solution)/shard_map/ppermute | solution.py:325
  103.9 23.7 %collective-permute-start.13 = (bf16[512,768]{1,0:T(8,128)(2,1)S(1)}, bf16[512,768]{1,0:T(8,128)(2,1)S(1)}, u32[]{:S(2)}, u32[]{:S(2)}) collective-permute-start(bf16[512,768]{1,0:T(8,128)(2,1)S(1)} %slice.11), channel_id=1, source_target_pairs={{16,24},{20,28},{8,0},{12,4},{17,25},{21,29},{9,1},{13,5},{18,26},... | collective-permute-start | bytes 2359304 | tf_op jit(solution)/shard_map/ppermute | solution.py:407
  123.2 23.1 %collective-permute-start.12 = (bf16[512,768]{1,0:T(8,128)(2,1)S(1)}, bf16[512,768]{1,0:T(8,128)(2,1)S(1)}, u32[]{:S(2)}, u32[]{:S(2)}) collective-permute-start(bf16[512,768]{1,0:T(8,128)(2,1)S(1)} %collective-permute-done.9.refs_0_), channel_id=1, source_target_pairs={{16,24},{20,28},{8,0},{12,4},{17,25},{21,29},{9,1},{13,5},{18,26},... | collective-permute-start | bytes 2359304 | tf_op jit(solution)/shard_map/ppermute | solution.py:407
  128.8 12.9 %collective-permute-start.18 = (bf16[256,768]{1,0:T(8,128)(2,1)S(1)}, bf16[256,768]{1,0:T(8,128)(2,1)S(1)}, u32[]{:S(2)}, u32[]{:S(2)}) collective-permute-start(bf16[256,768]{1,0:T(8,128)(2,1)S(1)} %get-tuple-element.149), channel_id=1, source_target_pairs={{0,4},{4,0},{8,12},{12,8},{16,20},{20,16},{24,28},{28,24},{1,5},{5... | collective-permute-start | bytes 1179656 | tf_op jit(solution)/shard_map/ppermute | solution.py:325
  144.0 10.4 %collective-permute-start.27 = (bf16[192,768]{1,0:T(8,128)(2,1)S(1)}, bf16[192,768]{1,0:T(8,128)(2,1)S(1)}, u32[]{:S(2)}, u32[]{:S(2)}) collective-permute-start(bf16[192,768]{1,0:T(8,128)(2,1)S(1)} %get-tuple-element.166), channel_id=1, source_target_pairs={{0,1},{1,0},{2,3},{3,2},{4,5},{5,4},{6,7},{7,6},{8,9},{9,8},{10,11... | collective-permute-start | bytes 884744 | tf_op jit(solution)/shard_map/ppermute | solution.py:509
  145.3 9.1 %collective-permute-start.28 = (bf16[192,768]{1,0:T(8,128)(2,1)S(1)}, bf16[192,768]{1,0:T(8,128)(2,1)S(1)}, u32[]{:S(2)}, u32[]{:S(2)}) collective-permute-start(bf16[192,768]{1,0:T(8,128)(2,1)S(1)} %add_convert_fusion), channel_id=1, source_target_pairs={{0,2},{1,3},{2,0},{3,1},{4,6},{5,7},{6,4},{7,5},{8,10},{9,11},{10,... | collective-permute-start | bytes 884744 | tf_op jit(solution)/shard_map/ppermute | solution.py:522
  147.0 10.6 %collective-permute-start.25 = (bf16[256,512]{1,0:T(8,128)(2,1)S(1)}, bf16[256,512]{1,0:T(8,128)(2,1)S(1)}, u32[]{:S(2)}, u32[]{:S(2)}) collective-permute-start(bf16[256,512]{1,0:T(8,128)(2,1)S(1)} %get-tuple-element.163), channel_id=1, source_target_pairs={{0,4},{4,0},{8,12},{12,8},{16,20},{20,16},{24,28},{28,24},{1,5},{5... | collective-permute-start | bytes 786440 | tf_op jit(solution)/shard_map/ppermute | solution.py:325
  147.9 9.7 %collective-permute-start.26 = (bf16[256,256]{1,0:T(8,128)(2,1)S(1)}, bf16[256,256]{1,0:T(8,128)(2,1)S(1)}, u32[]{:S(2)}, u32[]{:S(2)}) collective-permute-start(bf16[256,256]{1,0:T(8,128)(2,1)S(1)} %get-tuple-element.164), channel_id=1, source_target_pairs={{0,4},{4,0},{8,12},{12,8},{16,20},{20,16},{24,28},{28,24},{1,5},{5... | collective-permute-start | bytes 393224 | tf_op jit(solution)/shard_map/ppermute | solution.py:325
  157.7 7.6 %collective-permute-start.29 = (bf16[192,768]{1,0:T(8,128)(2,1)S(1)}, bf16[192,768]{1,0:T(8,128)(2,1)S(1)}, u32[]{:S(2)}, u32[]{:S(2)}) collective-permute-start(bf16[192,768]{1,0:T(8,128)(2,1)S(1)} %get-tuple-element.174.own), channel_id=1, source_target_pairs={{0,2},{1,3},{2,0},{3,1},{4,6},{5,7},{6,4},{7,5},{8,10},{9,11},{10,... | collective-permute-start | bytes 884744 | tf_op jit(solution)/shard_map/ppermute | solution.py:532
  165.4 7.8 %collective-permute-start.34 = (bf16[192,512]{1,0:T(8,128)(2,1)S(1)}, bf16[192,512]{1,0:T(8,128)(2,1)S(1)}, u32[]{:S(2)}, u32[]{:S(2)}) collective-permute-start(bf16[192,512]{1,0:T(8,128)(2,1)S(1)} %add_convert_fusion.1), channel_id=1, source_target_pairs={{0,2},{1,3},{2,0},{3,1},{4,6},{5,7},{6,4},{7,5},{8,10},{9,11},{10,... | collective-permute-start | bytes 589832 | tf_op jit(solution)/shard_map/ppermute | solution.py:522
  167.2 7.7 %collective-permute-start.33 = (bf16[192,256]{1,0:T(8,128)(2,1)S(1)}, bf16[192,256]{1,0:T(8,128)(2,1)S(1)}, u32[]{:S(2)}, u32[]{:S(2)}) collective-permute-start(bf16[192,256]{1,0:T(8,128)(2,1)S(1)} %add_convert_fusion.3), channel_id=1, source_target_pairs={{0,2},{1,3},{2,0},{3,1},{4,6},{5,7},{6,4},{7,5},{8,10},{9,11},{10,... | collective-permute-start | bytes 294920 | tf_op jit(solution)/shard_map/ppermute | solution.py:522
  174.9 7.6 %collective-permute-start.39 = (bf16[192,512]{1,0:T(8,128)(2,1)S(1)}, bf16[192,512]{1,0:T(8,128)(2,1)S(1)}, u32[]{:S(2)}, u32[]{:S(2)}) collective-permute-start(bf16[192,512]{1,0:T(8,128)(2,1)S(1)} %get-tuple-element.199.refs_0_), channel_id=1, source_target_pairs={{0,2},{1,3},{2,0},{3,1},{4,6},{5,7},{6,4},{7,5},{8,10},{9,11},{10,... | collective-permute-start | bytes 589832 | tf_op jit(solution)/shard_map/ppermute | solution.py:532
  (27 other events, 141.3 us)
